TPU v7x, 512 devices: a whole 4x8x8 slice. The times are simulated.
512 devices in a mesh: row: 32 (over x_lo, y, core), col: 16 (over z, x_hi).
Axes of the slice: x: 4 (x_hi: 2, x_lo: 2; x = x_hi * 2 + x_lo), y: 8, z: 8, core: 2. Of those that a mesh axis runs over, the one named last changes fastest.
Arguments:
- counts: int32 [131072, 4096], P(('row', 'col')), may hold values from 0 to 1024, as said below
- row_marg: int32 [131072], P(('row', 'col')), may hold values from 64 to 999999
- col_marg: int32 [4096], P('col'), may hold values from 64 to 999999
- log_total: float32 [1], replicated, may hold values from 22 to 26
- row_embed: float32 [131072, 256], P(('row', 'col')), may hold values from -0.6 to 0.6
- col_embed: float32 [4096, 256], P('col'), may hold values from -0.6 to 0.6
Outputs:
- row_grad: float32 [131072, 256], P(('row', 'col'))
- col_grad: float32 [4096, 256], P('col')
Inputs may be any that keep to these rules, and one draw needn't show every extreme that they name: About a quarter of the counts are zero; the positive ones spread over powers of two.
All inputs are finite; a program needn't handle non-finite values.
Results may differ from a plain program's by a relative error of at most 0.0003.
Values sent between devices are 32-bit elements; how exact they have to be, the bound alone decides.
No kernel may reach another device: no remote copies, remote signals or barrier semaphores. Data moves between devices by JAX's collectives and lax.ppermute only.
A program may use at most 64 MiB of HBM per device.

v0:
```python
import math

import jax
import jax.numpy as jnp
from jax import lax
from jax.sharding import PartitionSpec as P


def shifted(value, axis, steps):
    count = lax.axis_size(axis)
    pairs = [(source, (source + steps) % count) for source in range(count)]
    return lax.ppermute(value, axis, pairs)


def cell_grads(cnt, score, base):
    x = cnt.astype(jnp.float32)
    pmi = jnp.log(jnp.maximum(x, 1.0)) + base
    weight = 0.1 + 0.25 * jnp.sqrt(x)
    return jnp.where(cnt > 0, weight * (score - pmi), jax.nn.sigmoid(score - base))


def panel_terms(counts, row_embed, base_row, panel, log_col, start):
    width = panel.shape[0]
    cnt = lax.dynamic_slice_in_dim(counts, start, width, 1)
    score = jnp.dot(
        row_embed, panel.T, precision=lax.Precision.HIGHEST, preferred_element_type=jnp.float32
    )
    cell = cell_grads(cnt, score, base_row - log_col[None, :])
    row_term = jnp.dot(
        cell, panel, precision=lax.Precision.HIGHEST, preferred_element_type=jnp.float32
    )
    col_term = jnp.dot(
        cell.T, row_embed, precision=lax.Precision.HIGHEST, preferred_element_type=jnp.float32
    )
    return (row_term, col_term)


def body(counts, row_marg, col_marg, log_total, row_embed, col_embed):
    rows, width = row_embed.shape
    panel_cols = col_embed.shape[0]
    col_count = lax.axis_size("col")
    total_cols = panel_cols * col_count
    total_rows = rows * lax.axis_size("row") * col_count
    mine = lax.axis_index("col")
    base_row = log_total[0] - jnp.log(row_marg.astype(jnp.float32))[:, None]
    log_col = jnp.log(col_marg.astype(jnp.float32))
    row_sum = jnp.zeros((rows, width), jnp.float32)

    def turn(step, carry):
        panel, logs, gsum, racc = carry
        owner = (mine - step + col_count) % col_count
        row_term, col_term = panel_terms(
            counts, row_embed, base_row, panel, logs, owner * panel_cols
        )
        panel, logs, gsum = shifted((panel, logs, gsum + col_term), "col", 1)
        return (panel, logs, gsum, racc + row_term)

    start_sum = jnp.zeros((panel_cols, width), jnp.float32)
    panel, logs, gsum, row_sum = lax.fori_loop(
        0, col_count - 1, turn, (col_embed, log_col, start_sum, row_sum)
    )
    owner = (mine + 1) % col_count
    row_term, col_term = panel_terms(counts, row_embed, base_row, panel, logs, owner * panel_cols)
    row_sum = row_sum + row_term
    col_sum = shifted(gsum + col_term, "col", 1)
    col_total = lax.psum(col_sum, "row")
    row_grad = row_sum / math.sqrt(total_cols)
    col_grad = col_total / math.sqrt(total_rows)
    return (row_grad, col_grad)


def solution(mesh):
    return jax.shard_map(
        body,
        mesh=mesh,
        in_specs=(
            P(("row", "col"), None),
            P(("row", "col")),
            P("col"),
            P(),
            P(("row", "col"), None),
            P("col", None),
        ),
        out_specs=(P(("row", "col"), None), P("col", None)),
        check_vma=False,
    )
```

profile of v0, /device:TPU:6, one launch (start us, length us, event | category | flops | bytes accessed | tf_op | source)
XLA Modules:
  0.0 557.7 jit_solution(5664083586944488888)
XLA Ops:
  11.3 297.4 %while.22 = (s32[]{:T(128)}, f32[256,256]{1,0:T(8,128)S(1)}, f32[256]{0:T(256)S(1)}, f32[256,256]{1,0:T(8,128)S(1)}, f32[256,256]{1,0:T(8,128)S(1)}, /*index=5*/...) while((s32[]{:T(128)}, f32[256,256]{1,0:T(8,128)S(1)}, ...), condition=%wide.region_1.2_spmd.clone, body=%wide.region_0.1_spmd.clone.sunk | while | flops 606011392 | bytes 6040010 | solution.py:59
  11.4 5.1 collective-permute-start
  23.8 5.1 collective-permute-start.1
  31.0 5.8 %collective-permute-start = (f32[256,256]{1,0:T(8,128)S(1)}, f32[256,256]{1,0:T(8,128)S(1)}, u32[]{:S(2)}, u32[]{:S(2)}) collective-permute-start(f32[256,256]{1,0:T(8,128)S(1)} %copy.16), channel_id=1, source_target_pairs={{0,1},{1,2},{2,3},{3,4},{4,5},{5,6},{6,7},{7,8},{8,9},{9,10},{10,1... | collective-permute-start | bytes 786440 | tf_op jit(solution)/shard_map/while/body/eval_jaxpr/ppermute | solution.py:12
  43.4 5.8 %collective-permute-start.1 = (f32[256]{0:T(256)S(1)}, f32[256]{0:T(256)S(1)}, u32[]{:S(2)}, u32[]{:S(2)}) collective-permute-start(f32[256]{0:T(256)S(1)} %copy.17), channel_id=1, source_target_pairs={{0,1},{1,2},{2,3},{3,4},{4,5},{5,6},{6,7},{7,8},{8,9},{9,10},{10,1... | collective-permute-start | bytes 3080 | tf_op jit(solution)/shard_map/while/body/eval_jaxpr/ppermute | solution.py:12
  51.0 6.0 %collective-permute-start = (f32[256,256]{1,0:T(8,128)S(1)}, f32[256,256]{1,0:T(8,128)S(1)}, u32[]{:S(2)}, u32[]{:S(2)}) collective-permute-start(f32[256,256]{1,0:T(8,128)S(1)} %copy.16), channel_id=1, source_target_pairs={{0,1},{1,2},{2,3},{3,4},{4,5},{5,6},{6,7},{7,8},{8,9},{9,10},{10,1... | collective-permute-start | bytes 786440 | tf_op jit(solution)/shard_map/while/body/eval_jaxpr/ppermute | solution.py:12
  64.5 6.2 %collective-permute-start.1 = (f32[256]{0:T(256)S(1)}, f32[256]{0:T(256)S(1)}, u32[]{:S(2)}, u32[]{:S(2)}) collective-permute-start(f32[256]{0:T(256)S(1)} %copy.17), channel_id=1, source_target_pairs={{0,1},{1,2},{2,3},{3,4},{4,5},{5,6},{6,7},{7,8},{8,9},{9,10},{10,1... | collective-permute-start | bytes 3080 | tf_op jit(solution)/shard_map/while/body/eval_jaxpr/ppermute | solution.py:12
  72.4 6.2 %collective-permute-start = (f32[256,256]{1,0:T(8,128)S(1)}, f32[256,256]{1,0:T(8,128)S(1)}, u32[]{:S(2)}, u32[]{:S(2)}) collective-permute-start(f32[256,256]{1,0:T(8,128)S(1)} %copy.16), channel_id=1, source_target_pairs={{0,1},{1,2},{2,3},{3,4},{4,5},{5,6},{6,7},{7,8},{8,9},{9,10},{10,1... | collective-permute-start | bytes 786440 | tf_op jit(solution)/shard_map/while/body/eval_jaxpr/ppermute | solution.py:12
  85.1 6.2 %collective-permute-start.1 = (f32[256]{0:T(256)S(1)}, f32[256]{0:T(256)S(1)}, u32[]{:S(2)}, u32[]{:S(2)}) collective-permute-start(f32[256]{0:T(256)S(1)} %copy.17), channel_id=1, source_target_pairs={{0,1},{1,2},{2,3},{3,4},{4,5},{5,6},{6,7},{7,8},{8,9},{9,10},{10,1... | collective-permute-start | bytes 3080 | tf_op jit(solution)/shard_map/while/body/eval_jaxpr/ppermute | solution.py:12
  93.0 6.2 %collective-permute-start = (f32[256,256]{1,0:T(8,128)S(1)}, f32[256,256]{1,0:T(8,128)S(1)}, u32[]{:S(2)}, u32[]{:S(2)}) collective-permute-start(f32[256,256]{1,0:T(8,128)S(1)} %copy.16), channel_id=1, source_target_pairs={{0,1},{1,2},{2,3},{3,4},{4,5},{5,6},{6,7},{7,8},{8,9},{9,10},{10,1... | collective-permute-start | bytes 786440 | tf_op jit(solution)/shard_map/while/body/eval_jaxpr/ppermute | solution.py:12
  104.5 6.2 %collective-permute-start.1 = (f32[256]{0:T(256)S(1)}, f32[256]{0:T(256)S(1)}, u32[]{:S(2)}, u32[]{:S(2)}) collective-permute-start(f32[256]{0:T(256)S(1)} %copy.17), channel_id=1, source_target_pairs={{0,1},{1,2},{2,3},{3,4},{4,5},{5,6},{6,7},{7,8},{8,9},{9,10},{10,1... | collective-permute-start | bytes 3080 | tf_op jit(solution)/shard_map/while/body/eval_jaxpr/ppermute | solution.py:12
  112.4 6.2 %collective-permute-start = (f32[256,256]{1,0:T(8,128)S(1)}, f32[256,256]{1,0:T(8,128)S(1)}, u32[]{:S(2)}, u32[]{:S(2)}) collective-permute-start(f32[256,256]{1,0:T(8,128)S(1)} %copy.16), channel_id=1, source_target_pairs={{0,1},{1,2},{2,3},{3,4},{4,5},{5,6},{6,7},{7,8},{8,9},{9,10},{10,1... | collective-permute-start | bytes 786440 | tf_op jit(solution)/shard_map/while/body/eval_jaxpr/ppermute | solution.py:12
  123.9 6.2 %collective-permute-start.1 = (f32[256]{0:T(256)S(1)}, f32[256]{0:T(256)S(1)}, u32[]{:S(2)}, u32[]{:S(2)}) collective-permute-start(f32[256]{0:T(256)S(1)} %copy.17), channel_id=1, source_target_pairs={{0,1},{1,2},{2,3},{3,4},{4,5},{5,6},{6,7},{7,8},{8,9},{9,10},{10,1... | collective-permute-start | bytes 3080 | tf_op jit(solution)/shard_map/while/body/eval_jaxpr/ppermute | solution.py:12
  131.8 6.2 %collective-permute-start = (f32[256,256]{1,0:T(8,128)S(1)}, f32[256,256]{1,0:T(8,128)S(1)}, u32[]{:S(2)}, u32[]{:S(2)}) collective-permute-start(f32[256,256]{1,0:T(8,128)S(1)} %copy.16), channel_id=1, source_target_pairs={{0,1},{1,2},{2,3},{3,4},{4,5},{5,6},{6,7},{7,8},{8,9},{9,10},{10,1... | collective-permute-start | bytes 786440 | tf_op jit(solution)/shard_map/while/body/eval_jaxpr/ppermute | solution.py:12
  143.6 5.8 %collective-permute-start.1 = (f32[256]{0:T(256)S(1)}, f32[256]{0:T(256)S(1)}, u32[]{:S(2)}, u32[]{:S(2)}) collective-permute-start(f32[256]{0:T(256)S(1)} %copy.17), channel_id=1, source_target_pairs={{0,1},{1,2},{2,3},{3,4},{4,5},{5,6},{6,7},{7,8},{8,9},{9,10},{10,1... | collective-permute-start | bytes 3080 | tf_op jit(solution)/shard_map/while/body/eval_jaxpr/ppermute | solution.py:12
  152.6 4.8 collective-permute-start
  168.4 4.6 collective-permute-done.1
  180.1 5.7 %collective-permute-start.1 = (f32[256]{0:T(256)S(1)}, f32[256]{0:T(256)S(1)}, u32[]{:S(2)}, u32[]{:S(2)}) collective-permute-start(f32[256]{0:T(256)S(1)} %copy.17), channel_id=1, source_target_pairs={{0,1},{1,2},{2,3},{3,4},{4,5},{5,6},{6,7},{7,8},{8,9},{9,10},{10,1... | collective-permute-start | bytes 3080 | tf_op jit(solution)/shard_map/while/body/eval_jaxpr/ppermute | solution.py:12
  189.1 4.6 collective-permute-start
  199.0 5.4 collective-permute-start.1
  219.7 6.2 %collective-permute-start.1 = (f32[256]{0:T(256)S(1)}, f32[256]{0:T(256)S(1)}, u32[]{:S(2)}, u32[]{:S(2)}) collective-permute-start(f32[256]{0:T(256)S(1)} %copy.17), channel_id=1, source_target_pairs={{0,1},{1,2},{2,3},{3,4},{4,5},{5,6},{6,7},{7,8},{8,9},{9,10},{10,1... | collective-permute-start | bytes 3080 | tf_op jit(solution)/shard_map/while/body/eval_jaxpr/ppermute | solution.py:12
  229.2 4.5 collective-permute-start
  237.0 4.2 collective-permute-start.2
  241.2 5.4 collective-permute-start.1
  248.3 6.3 %collective-permute-start = (f32[256,256]{1,0:T(8,128)S(1)}, f32[256,256]{1,0:T(8,128)S(1)}, u32[]{:S(2)}, u32[]{:S(2)}) collective-permute-start(f32[256,256]{1,0:T(8,128)S(1)} %copy.16), channel_id=1, source_target_pairs={{0,1},{1,2},{2,3},{3,4},{4,5},{5,6},{6,7},{7,8},{8,9},{9,10},{10,1... | collective-permute-start | bytes 786440 | tf_op jit(solution)/shard_map/while/body/eval_jaxpr/ppermute | solution.py:12
  261.9 5.0 collective-permute-start.1
  269.3 5.6 collective-permute-start
  281.0 6.0 %collective-permute-start.1 = (f32[256]{0:T(256)S(1)}, f32[256]{0:T(256)S(1)}, u32[]{:S(2)}, u32[]{:S(2)}) collective-permute-start(f32[256]{0:T(256)S(1)} %copy.17), channel_id=1, source_target_pairs={{0,1},{1,2},{2,3},{3,4},{4,5},{5,6},{6,7},{7,8},{8,9},{9,10},{10,1... | collective-permute-start | bytes 3080 | tf_op jit(solution)/shard_map/while/body/eval_jaxpr/ppermute | solution.py:12
  288.7 6.2 %collective-permute-start = (f32[256,256]{1,0:T(8,128)S(1)}, f32[256,256]{1,0:T(8,128)S(1)}, u32[]{:S(2)}, u32[]{:S(2)}) collective-permute-start(f32[256,256]{1,0:T(8,128)S(1)} %copy.16), channel_id=1, source_target_pairs={{0,1},{1,2},{2,3},{3,4},{4,5},{5,6},{6,7},{7,8},{8,9},{9,10},{10,1... | collective-permute-start | bytes 786440 | tf_op jit(solution)/shard_map/while/body/eval_jaxpr/ppermute | solution.py:12
  300.9 6.2 %collective-permute-start.1 = (f32[256]{0:T(256)S(1)}, f32[256]{0:T(256)S(1)}, u32[]{:S(2)}, u32[]{:S(2)}) collective-permute-start(f32[256]{0:T(256)S(1)} %copy.17), channel_id=1, source_target_pairs={{0,1},{1,2},{2,3},{3,4},{4,5},{5,6},{6,7},{7,8},{8,9},{9,10},{10,1... | collective-permute-start | bytes 3080 | tf_op jit(solution)/shard_map/while/body/eval_jaxpr/ppermute | solution.py:12
  311.6 6.2 %collective-permute-start.3 = (f32[256,256]{1,0:T(8,128)S(1)}, f32[256,256]{1,0:T(8,128)S(1)}, u32[]{:S(2)}, u32[]{:S(2)}) collective-permute-start(f32[256,256]{1,0:T(8,128)S(1)} %convolution_add_fusion.2), channel_id=1, source_target_pairs={{0,1},{1,2},{2,3},{3,4},{4,5},{5,6},{6,7},{7,8},{8,9},{9,10},{10,1... | collective-permute-start | bytes 786440 | tf_op jit(solution)/shard_map/ppermute | solution.py:12
  323.8 225.4 %all-reduce.2.cloned.1.call-done = f32[256,256]{1,0:T(8,128)} async-done(((f32[256,256]{1,0:T(8,128)}), f32[256,256]{1,0:T(8,128)}) %all-reduce.2.cloned.1.call-update) | async-done | bytes 262160 | tf_op jit(solution)/shard_map/psum | solution.py:66
  (152 shorter events, 145.9 us)
Async XLA Ops:
  7.2 542.0 %all-reduce.2.cloned.1.call-start = ((), (), s32[]{:S(2)}) async-start(), calls=%async_computation | async-start | bytes 524288 | tf_op jit(solution)/shard_map/psum | solution.py:66
  11.4 19.6 %collective-permute-start = (f32[256,256]{1,0:T(8,128)S(1)}, f32[256,256]{1,0:T(8,128)S(1)}, u32[]{:S(2)}, u32[]{:S(2)}) collective-permute-start(f32[256,256]{1,0:T(8,128)S(1)} %copy.16), channel_id=1, source_target_pairs={{0,1},{1,2},{2,3},{3,4},{4,5},{5,6},{6,7},{7,8},{8,9},{9,10},{10,1... | collective-permute-start | bytes 786440 | tf_op jit(solution)/shard_map/while/body/eval_jaxpr/ppermute | solution.py:12
  19.7 11.2 %collective-permute-start.2 = (f32[256,256]{1,0:T(8,128)S(1)}, f32[256,256]{1,0:T(8,128)S(1)}, u32[]{:S(2)}, u32[]{:S(2)}) collective-permute-start(f32[256,256]{1,0:T(8,128)S(1)} %convolution_add_fusion.6), channel_id=1, source_target_pairs={{0,1},{1,2},{2,3},{3,4},{4,5},{5,6},{6,7},{7,8},{8,9},{9,10},{10,1... | collective-permute-start | bytes 786440 | tf_op jit(solution)/shard_map/while/body/eval_jaxpr/ppermute | solution.py:12
  31.0 20.0 %collective-permute-start = (f32[256,256]{1,0:T(8,128)S(1)}, f32[256,256]{1,0:T(8,128)S(1)}, u32[]{:S(2)}, u32[]{:S(2)}) collective-permute-start(f32[256,256]{1,0:T(8,128)S(1)} %copy.16), channel_id=1, source_target_pairs={{0,1},{1,2},{2,3},{3,4},{4,5},{5,6},{6,7},{7,8},{8,9},{9,10},{10,1... | collective-permute-start | bytes 786440 | tf_op jit(solution)/shard_map/while/body/eval_jaxpr/ppermute | solution.py:12
  40.0 11.0 %collective-permute-start.2 = (f32[256,256]{1,0:T(8,128)S(1)}, f32[256,256]{1,0:T(8,128)S(1)}, u32[]{:S(2)}, u32[]{:S(2)}) collective-permute-start(f32[256,256]{1,0:T(8,128)S(1)} %convolution_add_fusion.6), channel_id=1, source_target_pairs={{0,1},{1,2},{2,3},{3,4},{4,5},{5,6},{6,7},{7,8},{8,9},{9,10},{10,1... | collective-permute-start | bytes 786440 | tf_op jit(solution)/shard_map/while/body/eval_jaxpr/ppermute | solution.py:12
  51.0 21.3 %collective-permute-start = (f32[256,256]{1,0:T(8,128)S(1)}, f32[256,256]{1,0:T(8,128)S(1)}, u32[]{:S(2)}, u32[]{:S(2)}) collective-permute-start(f32[256,256]{1,0:T(8,128)S(1)} %copy.16), channel_id=1, source_target_pairs={{0,1},{1,2},{2,3},{3,4},{4,5},{5,6},{6,7},{7,8},{8,9},{9,10},{10,1... | collective-permute-start | bytes 786440 | tf_op jit(solution)/shard_map/while/body/eval_jaxpr/ppermute | solution.py:12
  60.3 12.0 %collective-permute-start.2 = (f32[256,256]{1,0:T(8,128)S(1)}, f32[256,256]{1,0:T(8,128)S(1)}, u32[]{:S(2)}, u32[]{:S(2)}) collective-permute-start(f32[256,256]{1,0:T(8,128)S(1)} %convolution_add_fusion.6), channel_id=1, source_target_pairs={{0,1},{1,2},{2,3},{3,4},{4,5},{5,6},{6,7},{7,8},{8,9},{9,10},{10,1... | collective-permute-start | bytes 786440 | tf_op jit(solution)/shard_map/while/body/eval_jaxpr/ppermute | solution.py:12
  72.4 20.6 %collective-permute-start = (f32[256,256]{1,0:T(8,128)S(1)}, f32[256,256]{1,0:T(8,128)S(1)}, u32[]{:S(2)}, u32[]{:S(2)}) collective-permute-start(f32[256,256]{1,0:T(8,128)S(1)} %copy.16), channel_id=1, source_target_pairs={{0,1},{1,2},{2,3},{3,4},{4,5},{5,6},{6,7},{7,8},{8,9},{9,10},{10,1... | collective-permute-start | bytes 786440 | tf_op jit(solution)/shard_map/while/body/eval_jaxpr/ppermute | solution.py:12
  81.8 11.2 %collective-permute-start.2 = (f32[256,256]{1,0:T(8,128)S(1)}, f32[256,256]{1,0:T(8,128)S(1)}, u32[]{:S(2)}, u32[]{:S(2)}) collective-permute-start(f32[256,256]{1,0:T(8,128)S(1)} %convolution_add_fusion.6), channel_id=1, source_target_pairs={{0,1},{1,2},{2,3},{3,4},{4,5},{5,6},{6,7},{7,8},{8,9},{9,10},{10,1... | collective-permute-start | bytes 786440 | tf_op jit(solution)/shard_map/while/body/eval_jaxpr/ppermute | solution.py:12
  93.0 19.3 %collective-permute-start = (f32[256,256]{1,0:T(8,128)S(1)}, f32[256,256]{1,0:T(8,128)S(1)}, u32[]{:S(2)}, u32[]{:S(2)}) collective-permute-start(f32[256,256]{1,0:T(8,128)S(1)} %copy.16), channel_id=1, source_target_pairs={{0,1},{1,2},{2,3},{3,4},{4,5},{5,6},{6,7},{7,8},{8,9},{9,10},{10,1... | collective-permute-start | bytes 786440 | tf_op jit(solution)/shard_map/while/body/eval_jaxpr/ppermute | solution.py:12
  112.4 19.3 %collective-permute-start = (f32[256,256]{1,0:T(8,128)S(1)}, f32[256,256]{1,0:T(8,128)S(1)}, u32[]{:S(2)}, u32[]{:S(2)}) collective-permute-start(f32[256,256]{1,0:T(8,128)S(1)} %copy.16), channel_id=1, source_target_pairs={{0,1},{1,2},{2,3},{3,4},{4,5},{5,6},{6,7},{7,8},{8,9},{9,10},{10,1... | collective-permute-start | bytes 786440 | tf_op jit(solution)/shard_map/while/body/eval_jaxpr/ppermute | solution.py:12
  131.8 20.8 %collective-permute-start = (f32[256,256]{1,0:T(8,128)S(1)}, f32[256,256]{1,0:T(8,128)S(1)}, u32[]{:S(2)}, u32[]{:S(2)}) collective-permute-start(f32[256,256]{1,0:T(8,128)S(1)} %copy.16), channel_id=1, source_target_pairs={{0,1},{1,2},{2,3},{3,4},{4,5},{5,6},{6,7},{7,8},{8,9},{9,10},{10,1... | collective-permute-start | bytes 786440 | tf_op jit(solution)/shard_map/while/body/eval_jaxpr/ppermute | solution.py:12
  141.2 11.3 %collective-permute-start.2 = (f32[256,256]{1,0:T(8,128)S(1)}, f32[256,256]{1,0:T(8,128)S(1)}, u32[]{:S(2)}, u32[]{:S(2)}) collective-permute-start(f32[256,256]{1,0:T(8,128)S(1)} %convolution_add_fusion.6), channel_id=1, source_target_pairs={{0,1},{1,2},{2,3},{3,4},{4,5},{5,6},{6,7},{7,8},{8,9},{9,10},{10,1... | collective-permute-start | bytes 786440 | tf_op jit(solution)/shard_map/while/body/eval_jaxpr/ppermute | solution.py:12
  152.6 20.4 %collective-permute-start = (f32[256,256]{1,0:T(8,128)S(1)}, f32[256,256]{1,0:T(8,128)S(1)}, u32[]{:S(2)}, u32[]{:S(2)}) collective-permute-start(f32[256,256]{1,0:T(8,128)S(1)} %copy.16), channel_id=1, source_target_pairs={{0,1},{1,2},{2,3},{3,4},{4,5},{5,6},{6,7},{7,8},{8,9},{9,10},{10,1... | collective-permute-start | bytes 786440 | tf_op jit(solution)/shard_map/while/body/eval_jaxpr/ppermute | solution.py:12
  160.6 12.3 %collective-permute-start.2 = (f32[256,256]{1,0:T(8,128)S(1)}, f32[256,256]{1,0:T(8,128)S(1)}, u32[]{:S(2)}, u32[]{:S(2)}) collective-permute-start(f32[256,256]{1,0:T(8,128)S(1)} %convolution_add_fusion.6), channel_id=1, source_target_pairs={{0,1},{1,2},{2,3},{3,4},{4,5},{5,6},{6,7},{7,8},{8,9},{9,10},{10,1... | collective-permute-start | bytes 786440 | tf_op jit(solution)/shard_map/while/body/eval_jaxpr/ppermute | solution.py:12
  162.8 10.2 %collective-permute-start.1 = (f32[256]{0:T(256)S(1)}, f32[256]{0:T(256)S(1)}, u32[]{:S(2)}, u32[]{:S(2)}) collective-permute-start(f32[256]{0:T(256)S(1)} %copy.17), channel_id=1, source_target_pairs={{0,1},{1,2},{2,3},{3,4},{4,5},{5,6},{6,7},{7,8},{8,9},{9,10},{10,1... | collective-permute-start | bytes 3080 | tf_op jit(solution)/shard_map/while/body/eval_jaxpr/ppermute | solution.py:12
  173.0 16.1 %collective-permute-start = (f32[256,256]{1,0:T(8,128)S(1)}, f32[256,256]{1,0:T(8,128)S(1)}, u32[]{:S(2)}, u32[]{:S(2)}) collective-permute-start(f32[256,256]{1,0:T(8,128)S(1)} %copy.16), channel_id=1, source_target_pairs={{0,1},{1,2},{2,3},{3,4},{4,5},{5,6},{6,7},{7,8},{8,9},{9,10},{10,1... | collective-permute-start | bytes 786440 | tf_op jit(solution)/shard_map/while/body/eval_jaxpr/ppermute | solution.py:12
  178.1 10.9 %collective-permute-start.2 = (f32[256,256]{1,0:T(8,128)S(1)}, f32[256,256]{1,0:T(8,128)S(1)}, u32[]{:S(2)}, u32[]{:S(2)}) collective-permute-start(f32[256,256]{1,0:T(8,128)S(1)} %convolution_add_fusion.6), channel_id=1, source_target_pairs={{0,1},{1,2},{2,3},{3,4},{4,5},{5,6},{6,7},{7,8},{8,9},{9,10},{10,1... | collective-permute-start | bytes 786440 | tf_op jit(solution)/shard_map/while/body/eval_jaxpr/ppermute | solution.py:12
  189.1 20.0 %collective-permute-start = (f32[256,256]{1,0:T(8,128)S(1)}, f32[256,256]{1,0:T(8,128)S(1)}, u32[]{:S(2)}, u32[]{:S(2)}) collective-permute-start(f32[256,256]{1,0:T(8,128)S(1)} %copy.16), channel_id=1, source_target_pairs={{0,1},{1,2},{2,3},{3,4},{4,5},{5,6},{6,7},{7,8},{8,9},{9,10},{10,1... | collective-permute-start | bytes 786440 | tf_op jit(solution)/shard_map/while/body/eval_jaxpr/ppermute | solution.py:12
  196.9 12.3 %collective-permute-start.2 = (f32[256,256]{1,0:T(8,128)S(1)}, f32[256,256]{1,0:T(8,128)S(1)}, u32[]{:S(2)}, u32[]{:S(2)}) collective-permute-start(f32[256,256]{1,0:T(8,128)S(1)} %convolution_add_fusion.6), channel_id=1, source_target_pairs={{0,1},{1,2},{2,3},{3,4},{4,5},{5,6},{6,7},{7,8},{8,9},{9,10},{10,1... | collective-permute-start | bytes 786440 | tf_op jit(solution)/shard_map/while/body/eval_jaxpr/ppermute | solution.py:12
  199.0 10.1 %collective-permute-start.1 = (f32[256]{0:T(256)S(1)}, f32[256]{0:T(256)S(1)}, u32[]{:S(2)}, u32[]{:S(2)}) collective-permute-start(f32[256]{0:T(256)S(1)} %copy.17), channel_id=1, source_target_pairs={{0,1},{1,2},{2,3},{3,4},{4,5},{5,6},{6,7},{7,8},{8,9},{9,10},{10,1... | collective-permute-start | bytes 3080 | tf_op jit(solution)/shard_map/while/body/eval_jaxpr/ppermute | solution.py:12
  209.1 20.1 %collective-permute-start = (f32[256,256]{1,0:T(8,128)S(1)}, f32[256,256]{1,0:T(8,128)S(1)}, u32[]{:S(2)}, u32[]{:S(2)}) collective-permute-start(f32[256,256]{1,0:T(8,128)S(1)} %copy.16), channel_id=1, source_target_pairs={{0,1},{1,2},{2,3},{3,4},{4,5},{5,6},{6,7},{7,8},{8,9},{9,10},{10,1... | collective-permute-start | bytes 786440 | tf_op jit(solution)/shard_map/while/body/eval_jaxpr/ppermute | solution.py:12
  215.5 13.7 %collective-permute-start.2 = (f32[256,256]{1,0:T(8,128)S(1)}, f32[256,256]{1,0:T(8,128)S(1)}, u32[]{:S(2)}, u32[]{:S(2)}) collective-permute-start(f32[256,256]{1,0:T(8,128)S(1)} %convolution_add_fusion.6), channel_id=1, source_target_pairs={{0,1},{1,2},{2,3},{3,4},{4,5},{5,6},{6,7},{7,8},{8,9},{9,10},{10,1... | collective-permute-start | bytes 786440 | tf_op jit(solution)/shard_map/while/body/eval_jaxpr/ppermute | solution.py:12
  229.2 19.0 %collective-permute-start = (f32[256,256]{1,0:T(8,128)S(1)}, f32[256,256]{1,0:T(8,128)S(1)}, u32[]{:S(2)}, u32[]{:S(2)}) collective-permute-start(f32[256,256]{1,0:T(8,128)S(1)} %copy.16), channel_id=1, source_target_pairs={{0,1},{1,2},{2,3},{3,4},{4,5},{5,6},{6,7},{7,8},{8,9},{9,10},{10,1... | collective-permute-start | bytes 786440 | tf_op jit(solution)/shard_map/while/body/eval_jaxpr/ppermute | solution.py:12
  237.0 11.2 %collective-permute-start.2 = (f32[256,256]{1,0:T(8,128)S(1)}, f32[256,256]{1,0:T(8,128)S(1)}, u32[]{:S(2)}, u32[]{:S(2)}) collective-permute-start(f32[256,256]{1,0:T(8,128)S(1)} %convolution_add_fusion.6), channel_id=1, source_target_pairs={{0,1},{1,2},{2,3},{3,4},{4,5},{5,6},{6,7},{7,8},{8,9},{9,10},{10,1... | collective-permute-start | bytes 786440 | tf_op jit(solution)/shard_map/while/body/eval_jaxpr/ppermute | solution.py:12
  248.3 21.0 %collective-permute-start = (f32[256,256]{1,0:T(8,128)S(1)}, f32[256,256]{1,0:T(8,128)S(1)}, u32[]{:S(2)}, u32[]{:S(2)}) collective-permute-start(f32[256,256]{1,0:T(8,128)S(1)} %copy.16), channel_id=1, source_target_pairs={{0,1},{1,2},{2,3},{3,4},{4,5},{5,6},{6,7},{7,8},{8,9},{9,10},{10,1... | collective-permute-start | bytes 786440 | tf_op jit(solution)/shard_map/while/body/eval_jaxpr/ppermute | solution.py:12
  257.7 11.5 %collective-permute-start.2 = (f32[256,256]{1,0:T(8,128)S(1)}, f32[256,256]{1,0:T(8,128)S(1)}, u32[]{:S(2)}, u32[]{:S(2)}) collective-permute-start(f32[256,256]{1,0:T(8,128)S(1)} %convolution_add_fusion.6), channel_id=1, source_target_pairs={{0,1},{1,2},{2,3},{3,4},{4,5},{5,6},{6,7},{7,8},{8,9},{9,10},{10,1... | collective-permute-start | bytes 786440 | tf_op jit(solution)/shard_map/while/body/eval_jaxpr/ppermute | solution.py:12
  269.3 19.4 %collective-permute-start = (f32[256,256]{1,0:T(8,128)S(1)}, f32[256,256]{1,0:T(8,128)S(1)}, u32[]{:S(2)}, u32[]{:S(2)}) collective-permute-start(f32[256,256]{1,0:T(8,128)S(1)} %copy.16), channel_id=1, source_target_pairs={{0,1},{1,2},{2,3},{3,4},{4,5},{5,6},{6,7},{7,8},{8,9},{9,10},{10,1... | collective-permute-start | bytes 786440 | tf_op jit(solution)/shard_map/while/body/eval_jaxpr/ppermute | solution.py:12
  278.0 10.6 %collective-permute-start.2 = (f32[256,256]{1,0:T(8,128)S(1)}, f32[256,256]{1,0:T(8,128)S(1)}, u32[]{:S(2)}, u32[]{:S(2)}) collective-permute-start(f32[256,256]{1,0:T(8,128)S(1)} %convolution_add_fusion.6), channel_id=1, source_target_pairs={{0,1},{1,2},{2,3},{3,4},{4,5},{5,6},{6,7},{7,8},{8,9},{9,10},{10,1... | collective-permute-start | bytes 786440 | tf_op jit(solution)/shard_map/while/body/eval_jaxpr/ppermute | solution.py:12
  288.7 20.0 %collective-permute-start = (f32[256,256]{1,0:T(8,128)S(1)}, f32[256,256]{1,0:T(8,128)S(1)}, u32[]{:S(2)}, u32[]{:S(2)}) collective-permute-start(f32[256,256]{1,0:T(8,128)S(1)} %copy.16), channel_id=1, source_target_pairs={{0,1},{1,2},{2,3},{3,4},{4,5},{5,6},{6,7},{7,8},{8,9},{9,10},{10,1... | collective-permute-start | bytes 786440 | tf_op jit(solution)/shard_map/while/body/eval_jaxpr/ppermute | solution.py:12
  298.1 10.6 %collective-permute-start.2 = (f32[256,256]{1,0:T(8,128)S(1)}, f32[256,256]{1,0:T(8,128)S(1)}, u32[]{:S(2)}, u32[]{:S(2)}) collective-permute-start(f32[256,256]{1,0:T(8,128)S(1)} %convolution_add_fusion.6), channel_id=1, source_target_pairs={{0,1},{1,2},{2,3},{3,4},{4,5},{5,6},{6,7},{7,8},{8,9},{9,10},{10,1... | collective-permute-start | bytes 786440 | tf_op jit(solution)/shard_map/while/body/eval_jaxpr/ppermute | solution.py:12
  311.6 10.2 %collective-permute-start.3 = (f32[256,256]{1,0:T(8,128)S(1)}, f32[256,256]{1,0:T(8,128)S(1)}, u32[]{:S(2)}, u32[]{:S(2)}) collective-permute-start(f32[256,256]{1,0:T(8,128)S(1)} %convolution_add_fusion.2), channel_id=1, source_target_pairs={{0,1},{1,2},{2,3},{3,4},{4,5},{5,6},{6,7},{7,8},{8,9},{9,10},{10,1... | collective-permute-start | bytes 786440 | tf_op jit(solution)/shard_map/ppermute | solution.py:12
  (16 other events, 123.9 us)
Sparse Core Ops, SparseCore 0:
  322.6 226.5 all-reduce.1
where the time goes:
time: 562 us; the launch traced here: 558 us
  waiting for transfers between devices  243 us (43%)
  starting transfers between devices  216 us (38%)
  matrix products  75.7 us (13%)
  between operations  14.8 us (3%)
    psum x1, waiting for transfers between devices, body(): col_total = lax.psum(col_sum, 'row')  225 us
    ppermute x46, starting transfers between devices, shifted(): return lax.ppermute(value, axis, pairs)  216 us
    dot_general x16, matrix products, panel_terms(): jnp.dot(cell.T, row_embed, precision=lax.Precision.HIGHEST, preferred_ele...  28.3 us
    dot_general x16, matrix products, panel_terms(): jnp.dot(cell, panel, precision=lax.Precision.HIGHEST, preferred_element_t...  25.6 us
    dot_general x16, matrix products, panel_terms(): jnp.dot(row_embed, panel.T, precision=lax.Precision.HIGHEST, preferred_el...  21.9 us
    ppermute x46, waiting for transfers between devices, shifted(): return lax.ppermute(value, axis, pairs)  17.9 us
  transfers between devices with their start and end apart: 47, of which 10 were waited for; matrix products, arithmetic and copies ran while one was open for 13% of the time, Pallas kernels for 0%

commit v1 on v0

v1 whole, which is shorter than its diff:
```python
import functools
import math

import jax
import jax.numpy as jnp
import numpy as np
from jax import lax
from jax.experimental import pallas as pl
from jax.experimental.pallas import tpu as pltpu
from jax.sharding import Mesh, PartitionSpec as P

AXES = ("xlo", "y", "core", "z", "xhi")
SIZES = (2, 8, 2, 8, 2)
DIM = 256
ROWS = 256
SLICE = 64
PACK = 72


def pairs_to(move):
    pairs = []
    for target in range(math.prod(SIZES)):
        at = dict(zip(AXES, (int(i) for i in np.unravel_index(target, SIZES))))
        at.update(move(at))
        pairs.append((int(np.ravel_multi_index([at[a] for a in AXES], SIZES)), target))
    return pairs


def core_swap(at):
    return {"core": 1 - at["core"]}


def x_pair(at):
    return {"xlo": 1 - at["xlo"]}


def x_next(at):
    return {"xlo": 1 - at["xlo"], "xhi": 1 - at["xhi"]}


def x_far(at):
    return {"xhi": 1 - at["xhi"]}


def fetch(value, move):
    return lax.ppermute(value, AXES, pairs_to(move))


def split(value):
    high = value.astype(jnp.bfloat16)
    return high, (value - high.astype(jnp.float32)).astype(jnp.bfloat16)


def dot3(a, b, dims):
    one = functools.partial(
        lax.dot_general, dimension_numbers=(dims, ((), ())), preferred_element_type=jnp.float32
    )
    return one(a[0], b[0]) + (one(a[0], b[1]) + one(a[1], b[0]))


def cells_kernel(
    where, c_own_a, c_own_b, c_oth_a, c_oth_b, rb_own, rb_oth, s_own, s_pair, s_next, s_far,
    r_own, r_oth, g_own, g_pair, g_next, g_far,
    rh, rl, th, tl, emb, logs, gs,
):
    step = pl.program_id(0)

    @pl.when(step == 0)
    def _():
        for k, ref in enumerate((rb_own, rb_oth)):
            high, low = split(ref[:, :DIM])
            rh[k * ROWS : (k + 1) * ROWS, :] = high
            rl[k * ROWS : (k + 1) * ROWS, :] = low
            high, low = split(ref[:, :DIM].T)
            th[:, k * ROWS : (k + 1) * ROWS] = high
            tl[:, k * ROWS : (k + 1) * ROWS] = low
        r_own[...] = jnp.zeros_like(r_own)
        r_oth[...] = jnp.zeros_like(r_oth)

    off = pl.multiple_of(where[2] * SLICE, SLICE)
    rest = pl.multiple_of((1 - where[2]) * SLICE, SLICE)
    emb[pl.ds(off, SLICE), :] = s_own[0, :SLICE, :]
    emb[pl.ds(rest, SLICE), :] = s_pair[0, :SLICE, :]
    emb[pl.ds(2 * SLICE + off, SLICE), :] = s_far[0, :SLICE, :]
    emb[pl.ds(2 * SLICE + rest, SLICE), :] = s_next[0, :SLICE, :]
    logs[:, :128] = s_own[0, SLICE:, :128] + s_pair[0, SLICE:, :128]
    logs[:, 128:] = s_far[0, SLICE:, :128] + s_next[0, SLICE:, :128]
    e = split(emb[...])
    log_col = logs[0:1, :]
    total = None
    for k, (c_a, c_b, rb, r_out) in enumerate(
        ((c_own_a, c_own_b, rb_own, r_own), (c_oth_a, c_oth_b, rb_oth, r_oth))
    ):
        part = slice(k * ROWS, (k + 1) * ROWS)
        score = dot3((rh[part, :], rl[part, :]), e, ((1,), (1,)))
        gap = score - rb[:, DIM : DIM + 1] + log_col
        cnt = jnp.concatenate([c_a[...], c_b[...]], axis=1)
        x = cnt.astype(jnp.float32)
        weight = 0.1 + 0.25 * jnp.sqrt(x)
        cell = jnp.where(
            cnt > 0,
            weight * (gap - jnp.log(jnp.maximum(x, 1.0))),
            1.0 / (1.0 + jnp.exp(-gap)),
        )
        cell = split(cell)
        r_out[...] += dot3(cell, e, ((1,), (0,)))
        term = dot3((th[:, part], tl[:, part]), cell, ((1,), (0,)))
        total = term if total is None else total + term
    gs[...] = total.T
    g_own[0] = gs[pl.ds(off, SLICE), :]
    g_pair[0] = gs[pl.ds(rest, SLICE), :]
    g_far[0] = gs[pl.ds(2 * SLICE + off, SLICE), :]
    g_next[0] = gs[pl.ds(2 * SLICE + rest, SLICE), :]


def cells(where, counts, counts_oth, rb, rb_oth, slices):
    def block(same):
        def at(z, w):
            xhi = w[1] if same else 1 - w[1]
            return (0, z * 4 + xhi * 2 + w[0])

        return pl.BlockSpec((ROWS, 128), at)

    whole = pl.BlockSpec((ROWS, DIM + 128), lambda z, w: (0, 0))
    pack = pl.BlockSpec((1, PACK, DIM), lambda z, w: (z, 0, 0))
    r_out = pl.BlockSpec((ROWS, DIM), lambda z, w: (0, 0))
    g_out = pl.BlockSpec((1, SLICE, DIM), lambda z, w: (z, 0, 0))
    f32 = jnp.float32
    return pl.pallas_call(
        cells_kernel,
        grid_spec=pltpu.PrefetchScalarGridSpec(
            num_scalar_prefetch=1,
            grid=(8,),
            in_specs=[block(True), block(False), block(True), block(False), whole, whole] + [pack] * 4,
            out_specs=[r_out] * 2 + [g_out] * 4,
            scratch_shapes=[
                pltpu.VMEM((2 * ROWS, DIM), jnp.bfloat16),
                pltpu.VMEM((2 * ROWS, DIM), jnp.bfloat16),
                pltpu.VMEM((DIM, 2 * ROWS), jnp.bfloat16),
                pltpu.VMEM((DIM, 2 * ROWS), jnp.bfloat16),
                pltpu.VMEM((4 * SLICE, DIM), f32),
                pltpu.VMEM((PACK - SLICE, DIM), f32),
                pltpu.VMEM((4 * SLICE, DIM), f32),
            ],
        ),
        out_shape=[jax.ShapeDtypeStruct((ROWS, DIM), f32)] * 2
        + [jax.ShapeDtypeStruct((8, SLICE, DIM), f32)] * 4,
        compiler_params=pltpu.CompilerParams(vmem_limit_bytes=40 * 2**20),
        cost_estimate=pl.CostEstimate(
            flops=3 * 3 * 2 * 512 * 2048 * 256, bytes_accessed=10 * 2**20, transcendentals=4 * 2**20
        ),
    )(where, counts, counts, counts_oth, counts_oth, rb, rb_oth, *slices)


def body(counts, row_marg, col_marg, log_total, row_embed, col_embed):
    core, xlo, xhi = (lax.axis_index(a) for a in ("core", "xlo", "xhi"))
    where = jnp.stack([core, xhi, xlo]).astype(jnp.int32)

    counts_oth = fetch(counts, core_swap)
    base_row = log_total[0] - jnp.log(row_marg.astype(jnp.float32))
    rb = jnp.concatenate([row_embed, jnp.broadcast_to(base_row[:, None], (ROWS, 128))], axis=1)
    rb_oth = fetch(rb, core_swap)

    start = (core * 2 + xlo) * SLICE
    embeds = lax.dynamic_slice_in_dim(col_embed, start, SLICE, 0)
    log_col = jnp.log(lax.dynamic_slice_in_dim(col_marg, start, SLICE, 0).astype(jnp.float32))
    log_row = lax.dynamic_update_slice(jnp.zeros((DIM,), jnp.float32), log_col, (xlo * SLICE,))
    pack = jnp.concatenate(
        [embeds, jnp.broadcast_to(log_row[None, :], (PACK - SLICE, DIM))], axis=0
    )
    own = lax.all_to_all(jnp.broadcast_to(pack[None], (8, PACK, DIM)), "z", 0, 0)
    slices = [own] + [fetch(own, move) for move in (x_pair, x_next, x_far)]

    r_own, r_oth, g_own, g_pair, g_next, g_far = cells(where, counts, counts_oth, rb, rb_oth, slices)

    g = g_own + fetch(g_pair, x_pair) + fetch(g_next, x_next) + fetch(g_far, x_far)
    row_grad = (r_own + fetch(r_oth, core_swap)) * (1.0 / 64.0)
    g = lax.all_to_all(g.reshape(64, 8, DIM), ("z", "y"), 0, 0)
    g = jnp.sum(g, axis=0) * (1.0 / math.sqrt(131072.0))
    col_grad = lax.all_to_all(jnp.broadcast_to(g[None], (32, 8, DIM)), ("core", "xlo", "y"), 0, 0)
    return row_grad, col_grad.reshape(256, DIM)


def solution(mesh):
    fine = Mesh(mesh.devices.reshape(SIZES), AXES)
    both = ("xlo", "y", "core", "z", "xhi")
    col = ("z", "xhi")
    return jax.shard_map(
        body,
        mesh=fine,
        in_specs=(P(both, None), P(both), P(col), P(), P(both, None), P(col, None)),
        out_specs=(P(both, None), P(col, None)),
        check_vma=False,
    )
```

time: 562 us -> 159 us (0.28)
  waiting for transfers between devices: 243 us -> 65.8 us
  starting transfers between devices: 216 us -> 40.7 us
  matrix products: 75.7 us -> 0 us
  blocking collectives: 0 us -> 26.7 us
  Pallas kernels: 0 us -> 14.8 us
  between operations: 14.8 us -> 1.49 us
    psum x1 -> x0, waiting for transfers between devices: 225 us -> none  [body(): col_total = lax.psum(col_sum, 'row')]
    ppermute x46 -> x9, starting transfers between devices: 216 us -> 25.1 us  [fetch(): return lax.ppermute(value, AXES, pairs_to(move))]
    dot_general x48 -> x0, matrix products: 75.7 us -> none  [the longest x16 28.3 us: panel_terms(): jnp.dot(cell.T, row_embed, precision=lax.Precision.HIGHEST, preferred_ele...]
    all_to_all x0 -> x1, blocking collectives: none -> 26.7 us  [body(): g = lax.all_to_all(g.reshape(64, 8, DIM), ('z', 'y'), 0, 0)]
    all_to_all x0 -> x2, waiting for transfers between devices: none -> 25.1 us  [the longest x1 19 us: body(): lax.all_to_all(jnp.broadcast_to(pack[None], (8, PACK, DIM)), 'z', 0, 0)]
    ppermute x46 -> x9, waiting for transfers between devices: 17.9 us -> 40.7 us  [fetch(): return lax.ppermute(value, AXES, pairs_to(move))]
    all_to_all x0 -> x2, starting transfers between devices: none -> 15.6 us  [the longest x1 10.3 us: body(): lax.all_to_all(jnp.broadcast_to(pack[None], (8, PACK, DIM)), 'z', 0, 0)]
    pallas_call x0 -> x1, Pallas kernels: none -> 14.8 us  [cells(): pl.pallas_call(cells_kernel, grid_spec=pltpu.PrefetchScalarGridSpec(num_s...]
  transfers between devices with their start and end apart: 47 -> 11, of which waited for: 10 -> 8; matrix products, arithmetic and copies ran while one was open for 13% -> 3% of each run, Pallas kernels for 0% -> 0%
where the time goes in v1:
time: 159 us
  waiting for transfers between devices  65.8 us (41%)
  starting transfers between devices  40.7 us (26%)
  blocking collectives  26.7 us (17%)
  Pallas kernels  14.8 us (9%)
  local copies, waits for them, and re-layouts  4.59 us (3%)
  other arithmetic  4.51 us (3%)
    ppermute x9, waiting for transfers between devices, fetch(): return lax.ppermute(value, AXES, pairs_to(move))  40.7 us
    all_to_all x1, blocking collectives, body(): g = lax.all_to_all(g.reshape(64, 8, DIM), ('z', 'y'), 0, 0)  26.7 us
    ppermute x9, starting transfers between devices, fetch(): return lax.ppermute(value, AXES, pairs_to(move))  25.1 us
    all_to_all x1, waiting for transfers between devices, body(): lax.all_to_all(jnp.broadcast_to(pack[None], (8, PACK, DIM)), 'z', 0, 0)  19 us
    pallas_call x1, Pallas kernels, cells(): pl.pallas_call(cells_kernel, grid_spec=pltpu.PrefetchScalarGridSpec(num_s...  14.8 us
    all_to_all x1, starting transfers between devices, body(): lax.all_to_all(jnp.broadcast_to(pack[None], (8, PACK, DIM)), 'z', 0, 0)  10.3 us
    all_to_all x1, waiting for transfers between devices, body(): lax.all_to_all(jnp.broadcast_to(g[None], (32, 8, DIM)), ('core', 'xlo', '...  6.17 us
    all_to_all x1, starting transfers between devices, body(): lax.all_to_all(jnp.broadcast_to(g[None], (32, 8, DIM)), ('core', 'xlo', '...  5.27 us
  transfers between devices with their start and end apart: 11, of which 8 were waited for; matrix products, arithmetic and copies ran while one was open for 3% of the time, Pallas kernels for 0%

profile of v1, /device:TPU:6, one launch (start us, length us, event | category | flops | bytes accessed | tf_op | source)
XLA Modules:
  0.0 158.5 jit_solution(13816382666553454016)
XLA Ops:
  0.6 2.1 %collective-permute-start = (s32[256,4096]{1,0:T(8,128)}, s32[256,4096]{1,0:T(8,128)}, u32[]{:S(2)}, u32[]{:S(2)}) collective-permute-start(s32[256,4096]{1,0:T(8,128)} %c_own_b.1), channel_id=1, source_target_pairs={{16,0},{17,1},{18,2},{19,3},{20,4},{21,5},{22,6},{23,7},{24,8},{25... | collective-permute-start | bytes 12582920 | tf_op jit(solution)/shard_map/ppermute | solution.py:46
  2.7 0.9 log_dynamic-update-slice_fusion
  3.6 0.9 broadcast_in_dim.13
  4.5 10.3 %all-to-all-start = ((f32[8,72,256]{2,1,0:T(8,128)}), f32[8,72,256]{2,1,0:T(8,128)S(1)}, u32[]{:S(2)}, u32[]{:S(2)}) async-start(f32[8,72,256]{2,1,0:T(8,128)} %broadcast_in_dim.13), calls=%async_computation | async-start | bytes 1179648 | tf_op jit(solution)/shard_map/all_to_all | solution.py:171
  15.4 19.0 %all-to-all-done.s_own = f32[8,72,256]{2,1,0:T(8,128)S(1)} async-done(((f32[8,72,256]{2,1,0:T(8,128)}), f32[8,72,256]{2,1,0:T(8,128)S(1)}, u32[]{:S(2)}, u32[]{:S(2)}) %all-to-all-start) | async-done | bytes 589856 | tf_op jit(solution)/shard_map/all_to_all | solution.py:171
  34.4 3.3 %collective-permute-start.4 = (f32[8,72,256]{2,1,0:T(8,128)S(1)}, f32[8,72,256]{2,1,0:T(8,128)S(1)}, u32[]{:S(2)}, u32[]{:S(2)}) collective-permute-start(f32[8,72,256]{2,1,0:T(8,128)S(1)} %all-to-all-done.s_own), channel_id=1, source_target_pairs={{1,0},{0,1},{3,2},{2,3},{5,4},{4,5},{7,6},{6,7},{9,8},{8,9},{11,10... | collective-permute-start | bytes 1769480 | tf_op jit(solution)/shard_map/ppermute | solution.py:46
  37.7 4.0 %collective-permute-start.3 = (f32[8,72,256]{2,1,0:T(8,128)S(1)}, f32[8,72,256]{2,1,0:T(8,128)S(1)}, u32[]{:S(2)}, u32[]{:S(2)}) collective-permute-start(f32[8,72,256]{2,1,0:T(8,128)S(1)} %all-to-all-done.s_own), channel_id=1, source_target_pairs={{257,0},{256,1},{259,2},{258,3},{261,4},{260,5},{263,6},{262,7},{2... | collective-permute-start | bytes 1769480 | tf_op jit(solution)/shard_map/ppermute | solution.py:46
  41.7 1.9 %collective-permute-start.2 = (f32[8,72,256]{2,1,0:T(8,128)S(1)}, f32[8,72,256]{2,1,0:T(8,128)S(1)}, u32[]{:S(2)}, u32[]{:S(2)}) collective-permute-start(f32[8,72,256]{2,1,0:T(8,128)S(1)} %all-to-all-done.s_own), channel_id=1, source_target_pairs={{256,0},{257,1},{258,2},{259,3},{260,4},{261,5},{262,6},{263,7},{2... | collective-permute-start | bytes 1769480 | tf_op jit(solution)/shard_map/ppermute | solution.py:46
  43.7 0.7 log_subtract_fusion
  44.3 0.1 broadcast_in_dim.10
  44.4 1.0 pad_maximum_fusion.rb_own
  45.4 1.9 %collective-permute-start.1 = (f32[256,384]{1,0:T(8,128)S(1)}, f32[256,384]{1,0:T(8,128)S(1)}, u32[]{:S(2)}, u32[]{:S(2)}) collective-permute-start(f32[256,384]{1,0:T(8,128)S(1)} %pad_maximum_fusion.rb_own), channel_id=1, source_target_pairs={{16,0},{17,1},{18,2},{19,3},{20,4},{21,5},{22,6},{23,7},{24,8},{25... | collective-permute-start | bytes 1179656 | tf_op jit(solution)/shard_map/ppermute | solution.py:46
  47.4 0.1 pad_add_fusion.where
  47.4 1.6 %collective-permute-done.1.rb_oth = f32[256,384]{1,0:T(8,128)S(1)} collective-permute-done((f32[256,384]{1,0:T(8,128)S(1)}, f32[256,384]{1,0:T(8,128)S(1)}, u32[]{:S(2)}, u32[]{:S(2)}) %collective-permute-start.1) | collective-permute-done | bytes 393248 | tf_op jit(solution)/shard_map/ppermute | solution.py:46
  49.0 5.0 %collective-permute-done.4.s_far = f32[8,72,256]{2,1,0:T(8,128)S(1)} collective-permute-done((f32[8,72,256]{2,1,0:T(8,128)S(1)}, f32[8,72,256]{2,1,0:T(8,128)S(1)}, u32[]{:S(2)}, u32[]{:S(2)}) %collective-permute-start.4) | collective-permute-done | bytes 589856 | tf_op jit(solution)/shard_map/ppermute | solution.py:46
  54.0 11.7 %collective-permute-done.3.s_next = f32[8,72,256]{2,1,0:T(8,128)S(1)} collective-permute-done((f32[8,72,256]{2,1,0:T(8,128)S(1)}, f32[8,72,256]{2,1,0:T(8,128)S(1)}, u32[]{:S(2)}, u32[]{:S(2)}) %collective-permute-start.3) | collective-permute-done | bytes 589856 | tf_op jit(solution)/shard_map/ppermute | solution.py:46
  65.7 2.2 %copy-done.1 = s32[256,4096]{1,0:T(8,128)S(1)} copy-done((s32[256,4096]{1,0:T(8,128)S(1)}, s32[256,4096]{1,0:T(8,128)}, u32[]{:S(2)}) %copy-start.1) | copy-done | bytes 4194328
  67.9 14.8 %shard_map.77 = (f32[256,256]{1,0:T(8,128)S(1)}, f32[256,256]{1,0:T(8,128)S(1)}, f32[8,64,256]{2,1,0:T(8,128)S(1)}, f32[8,64,256]{2,1,0:T(8,128)S(1)}, f32[8,64,...) custom-call(s32[3]{0:T(128)S(1)} %pad_add_fusion.where, s32[256,4096]{1,0:T(8,128)S(1)} %copy-done.1, ...), custom_call_target="tpu_custom_call" | custom-call | flops 4831838208 | bytes 10485760 | tf_op jit(solution)/shard_map/pallas_call | solution.py:129
  82.8 2.7 %collective-permute-start.6 = (f32[8,64,256]{2,1,0:T(8,128)S(1)}, f32[8,64,256]{2,1,0:T(8,128)S(1)}, u32[]{:S(2)}, u32[]{:S(2)}) collective-permute-start(f32[8,64,256]{2,1,0:T(8,128)S(1)} %get-tuple-element.11), channel_id=1, source_target_pairs={{256,0},{257,1},{258,2},{259,3},{260,4},{261,5},{262,6},{263,7},{2... | collective-permute-start | bytes 1572872 | tf_op jit(solution)/shard_map/ppermute | solution.py:46
  85.5 3.1 %collective-permute-start.7 = (f32[8,64,256]{2,1,0:T(8,128)S(1)}, f32[8,64,256]{2,1,0:T(8,128)S(1)}, u32[]{:S(2)}, u32[]{:S(2)}) collective-permute-start(f32[8,64,256]{2,1,0:T(8,128)S(1)} %get-tuple-element.12), channel_id=1, source_target_pairs={{257,0},{256,1},{259,2},{258,3},{261,4},{260,5},{263,6},{262,7},{2... | collective-permute-start | bytes 1572872 | tf_op jit(solution)/shard_map/ppermute | solution.py:46
  88.7 4.0 %collective-permute-start.8 = (f32[8,64,256]{2,1,0:T(8,128)S(1)}, f32[8,64,256]{2,1,0:T(8,128)S(1)}, u32[]{:S(2)}, u32[]{:S(2)}) collective-permute-start(f32[8,64,256]{2,1,0:T(8,128)S(1)} %get-tuple-element.13), channel_id=1, source_target_pairs={{1,0},{0,1},{3,2},{2,3},{5,4},{4,5},{7,6},{6,7},{9,8},{8,9},{11,10... | collective-permute-start | bytes 1572872 | tf_op jit(solution)/shard_map/ppermute | solution.py:46
  92.6 6.8 %collective-permute-done.6 = f32[8,64,256]{2,1,0:T(8,128)S(1)} collective-permute-done((f32[8,64,256]{2,1,0:T(8,128)S(1)}, f32[8,64,256]{2,1,0:T(8,128)S(1)}, u32[]{:S(2)}, u32[]{:S(2)}) %collective-permute-start.6) | collective-permute-done | bytes 524320 | tf_op jit(solution)/shard_map/ppermute | solution.py:46
  99.5 14.0 %collective-permute-done.7 = f32[8,64,256]{2,1,0:T(8,128)S(1)} collective-permute-done((f32[8,64,256]{2,1,0:T(8,128)S(1)}, f32[8,64,256]{2,1,0:T(8,128)S(1)}, u32[]{:S(2)}, u32[]{:S(2)}) %collective-permute-start.7) | collective-permute-done | bytes 524320 | tf_op jit(solution)/shard_map/ppermute | solution.py:46
  113.4 0.1 add_add_fusion
  113.6 26.7 %all_to_all.15 = f32[64,8,256]{2,1,0:T(8,128)S(1)} all-to-all(f32[64,8,256]{2,1,0:T(8,128)S(1)} %bitcast.7), channel_id=1, replica_groups=mesh['xlo'=2,'y'=8,'core'=2,'z'=8,'xhi'=2] {'z','y'}, dimensions={0} | all-to-all | bytes 1048576 | tf_op jit(solution)/shard_map/all_to_all | solution.py:178
  140.3 0.7 broadcast_in_dim.14
  141.1 5.3 %all-to-all-start.2 = ((f32[32,8,256]{2,1,0:T(8,128)}), f32[32,8,256]{2,1,0:T(8,128)S(1)}, u32[]{:S(2)}, u32[]{:S(2)}) async-start(f32[32,8,256]{2,1,0:T(8,128)} %broadcast_in_dim.14), calls=%async_computation.2 | async-start | bytes 524288 | tf_op jit(solution)/shard_map/all_to_all | solution.py:180
  146.3 2.1 %collective-permute-start.5 = (f32[256,256]{1,0:T(8,128)}, f32[256,256]{1,0:T(8,128)S(1)}, u32[]{:S(2)}, u32[]{:S(2)}) collective-permute-start(f32[256,256]{1,0:T(8,128)} %copy-done.3), channel_id=1, source_target_pairs={{16,0},{17,1},{18,2},{19,3},{20,4},{21,5},{22,6},{23,7},{24,8},{25... | collective-permute-start | bytes 786440 | tf_op jit(solution)/shard_map/ppermute | solution.py:46
  148.4 1.6 collective-permute-done.5
  150.0 1.7 %add_multiply_fusion = f32[256,256]{1,0:T(8,128)} fusion(f32[256,256]{1,0:T(8,128)} %copy-done.2, f32[256,256]{1,0:T(8,128)S(1)} %collective-permute-done.5), kind=kLoop, calls=%fused_computation.2 | loop fusion | flops 131072 | bytes 786432 | tf_op jit(solution)/shard_map/mul | solution.py:177
  151.7 6.2 %all-to-all-done.2 = f32[32,8,256]{2,1,0:T(8,128)S(1)} async-done(((f32[32,8,256]{2,1,0:T(8,128)}), f32[32,8,256]{2,1,0:T(8,128)S(1)}, u32[]{:S(2)}, u32[]{:S(2)}) %all-to-all-start.2) | async-done | bytes 262176 | tf_op jit(solution)/shard_map/all_to_all | solution.py:180
  157.8 0.7 copy.11
  (16 shorter events, 0.1 us)
Async XLA Ops:
  0.6 3.0 %copy-start = (f32[256,256]{1,0:T(8,128)S(1)}, f32[256,256]{1,0:T(8,128)}, u32[]{:S(2)}) copy-start(f32[256,256]{1,0:T(8,128)} %param.11) | copy-start | bytes 786436
  0.6 65.1 %collective-permute-start = (s32[256,4096]{1,0:T(8,128)}, s32[256,4096]{1,0:T(8,128)}, u32[]{:S(2)}, u32[]{:S(2)}) collective-permute-start(s32[256,4096]{1,0:T(8,128)} %c_own_b.1), channel_id=1, source_target_pairs={{16,0},{17,1},{18,2},{19,3},{20,4},{21,5},{22,6},{23,7},{24,8},{25... | collective-permute-start | bytes 12582920 | tf_op jit(solution)/shard_map/ppermute | solution.py:46
  4.5 29.9 %all-to-all-start = ((f32[8,72,256]{2,1,0:T(8,128)}), f32[8,72,256]{2,1,0:T(8,128)S(1)}, u32[]{:S(2)}, u32[]{:S(2)}) async-start(f32[8,72,256]{2,1,0:T(8,128)} %broadcast_in_dim.13), calls=%async_computation | async-start | bytes 1179648 | tf_op jit(solution)/shard_map/all_to_all | solution.py:171
  34.4 19.6 %collective-permute-start.4 = (f32[8,72,256]{2,1,0:T(8,128)S(1)}, f32[8,72,256]{2,1,0:T(8,128)S(1)}, u32[]{:S(2)}, u32[]{:S(2)}) collective-permute-start(f32[8,72,256]{2,1,0:T(8,128)S(1)} %all-to-all-done.s_own), channel_id=1, source_target_pairs={{1,0},{0,1},{3,2},{2,3},{5,4},{4,5},{7,6},{6,7},{9,8},{8,9},{11,10... | collective-permute-start | bytes 1769480 | tf_op jit(solution)/shard_map/ppermute | solution.py:46
  37.7 28.0 %collective-permute-start.3 = (f32[8,72,256]{2,1,0:T(8,128)S(1)}, f32[8,72,256]{2,1,0:T(8,128)S(1)}, u32[]{:S(2)}, u32[]{:S(2)}) collective-permute-start(f32[8,72,256]{2,1,0:T(8,128)S(1)} %all-to-all-done.s_own), channel_id=1, source_target_pairs={{257,0},{256,1},{259,2},{258,3},{261,4},{260,5},{263,6},{262,7},{2... | collective-permute-start | bytes 1769480 | tf_op jit(solution)/shard_map/ppermute | solution.py:46
  41.7 24.0 %collective-permute-start.2 = (f32[8,72,256]{2,1,0:T(8,128)S(1)}, f32[8,72,256]{2,1,0:T(8,128)S(1)}, u32[]{:S(2)}, u32[]{:S(2)}) collective-permute-start(f32[8,72,256]{2,1,0:T(8,128)S(1)} %all-to-all-done.s_own), channel_id=1, source_target_pairs={{256,0},{257,1},{258,2},{259,3},{260,4},{261,5},{262,6},{263,7},{2... | collective-permute-start | bytes 1769480 | tf_op jit(solution)/shard_map/ppermute | solution.py:46
  45.4 3.6 %collective-permute-start.1 = (f32[256,384]{1,0:T(8,128)S(1)}, f32[256,384]{1,0:T(8,128)S(1)}, u32[]{:S(2)}, u32[]{:S(2)}) collective-permute-start(f32[256,384]{1,0:T(8,128)S(1)} %pad_maximum_fusion.rb_own), channel_id=1, source_target_pairs={{16,0},{17,1},{18,2},{19,3},{20,4},{21,5},{22,6},{23,7},{24,8},{25... | collective-permute-start | bytes 1179656 | tf_op jit(solution)/shard_map/ppermute | solution.py:46
  65.7 2.2 %copy-start.1 = (s32[256,4096]{1,0:T(8,128)S(1)}, s32[256,4096]{1,0:T(8,128)}, u32[]{:S(2)}) copy-start(s32[256,4096]{1,0:T(8,128)} %c_own_b.1) | copy-start | bytes 12582916
  82.8 30.8 %copy-start.2 = (f32[256,256]{1,0:T(8,128)}, f32[256,256]{1,0:T(8,128)S(1)}, u32[]{:S(2)}) copy-start(f32[256,256]{1,0:T(8,128)S(1)} %get-tuple-element.8) | copy-start | bytes 786436
  82.8 30.8 %copy-start.3 = (f32[256,256]{1,0:T(8,128)}, f32[256,256]{1,0:T(8,128)S(1)}, u32[]{:S(2)}) copy-start(f32[256,256]{1,0:T(8,128)S(1)} %get-tuple-element.9) | copy-start | bytes 786436
  82.8 16.7 %collective-permute-start.6 = (f32[8,64,256]{2,1,0:T(8,128)S(1)}, f32[8,64,256]{2,1,0:T(8,128)S(1)}, u32[]{:S(2)}, u32[]{:S(2)}) collective-permute-start(f32[8,64,256]{2,1,0:T(8,128)S(1)} %get-tuple-element.11), channel_id=1, source_target_pairs={{256,0},{257,1},{258,2},{259,3},{260,4},{261,5},{262,6},{263,7},{2... | collective-permute-start | bytes 1572872 | tf_op jit(solution)/shard_map/ppermute | solution.py:46
  85.5 27.9 %collective-permute-start.7 = (f32[8,64,256]{2,1,0:T(8,128)S(1)}, f32[8,64,256]{2,1,0:T(8,128)S(1)}, u32[]{:S(2)}, u32[]{:S(2)}) collective-permute-start(f32[8,64,256]{2,1,0:T(8,128)S(1)} %get-tuple-element.12), channel_id=1, source_target_pairs={{257,0},{256,1},{259,2},{258,3},{261,4},{260,5},{263,6},{262,7},{2... | collective-permute-start | bytes 1572872 | tf_op jit(solution)/shard_map/ppermute | solution.py:46
  88.7 24.8 %collective-permute-start.8 = (f32[8,64,256]{2,1,0:T(8,128)S(1)}, f32[8,64,256]{2,1,0:T(8,128)S(1)}, u32[]{:S(2)}, u32[]{:S(2)}) collective-permute-start(f32[8,64,256]{2,1,0:T(8,128)S(1)} %get-tuple-element.13), channel_id=1, source_target_pairs={{1,0},{0,1},{3,2},{2,3},{5,4},{4,5},{7,6},{6,7},{9,8},{8,9},{11,10... | collective-permute-start | bytes 1572872 | tf_op jit(solution)/shard_map/ppermute | solution.py:46
  141.1 16.8 %all-to-all-start.2 = ((f32[32,8,256]{2,1,0:T(8,128)}), f32[32,8,256]{2,1,0:T(8,128)S(1)}, u32[]{:S(2)}, u32[]{:S(2)}) async-start(f32[32,8,256]{2,1,0:T(8,128)} %broadcast_in_dim.14), calls=%async_computation.2 | async-start | bytes 524288 | tf_op jit(solution)/shard_map/all_to_all | solution.py:180
  146.3 3.6 %collective-permute-start.5 = (f32[256,256]{1,0:T(8,128)}, f32[256,256]{1,0:T(8,128)S(1)}, u32[]{:S(2)}, u32[]{:S(2)}) collective-permute-start(f32[256,256]{1,0:T(8,128)} %copy-done.3), channel_id=1, source_target_pairs={{16,0},{17,1},{18,2},{19,3},{20,4},{21,5},{22,6},{23,7},{24,8},{25... | collective-permute-start | bytes 786440 | tf_op jit(solution)/shard_map/ppermute | solution.py:46

commit v2 on v1

v2 whole, which is shorter than its diff:
```python
import functools
import math

import jax
import jax.numpy as jnp
import numpy as np
from jax import lax
from jax.experimental import pallas as pl
from jax.experimental.pallas import tpu as pltpu
from jax.sharding import Mesh, PartitionSpec as P

AXES = ("xlo", "y", "core", "z", "xhi")
SIZES = (2, 8, 2, 8, 2)
DIM = 256
ROWS = 256
SLICE = 64
PACK = 72
GROUP = 4


def pairs_to(move):
    pairs = []
    for target in range(math.prod(SIZES)):
        at = dict(zip(AXES, (int(i) for i in np.unravel_index(target, SIZES))))
        at.update(move(at))
        pairs.append((int(np.ravel_multi_index([at[a] for a in AXES], SIZES)), target))
    return pairs


def core_swap(at):
    return {"core": 1 - at["core"]}


def x_pair(at):
    return {"xlo": 1 - at["xlo"]}


def x_next(at):
    return {"xlo": 1 - at["xlo"], "xhi": 1 - at["xhi"]}


def side_a(at):
    return x_next(at) if at["core"] else x_pair(at)


def side_b(at):
    return x_pair(at) if at["core"] else x_next(at)


def fetch(value, move):
    return lax.ppermute(value, AXES, pairs_to(move))


def split(value):
    high = value.astype(jnp.bfloat16)
    return high, (value - high.astype(jnp.float32)).astype(jnp.bfloat16)


def dot3(a, b, dims):
    one = functools.partial(
        lax.dot_general, dimension_numbers=(dims, ((), ())), preferred_element_type=jnp.float32
    )
    return one(a[0], b[0]) + (one(a[0], b[1]) + one(a[1], b[0]))


def rows_kernel(rb_own, rb_oth, rh, rl, th, tl):
    for k, ref in enumerate((rb_own, rb_oth)):
        part = slice(k * ROWS, (k + 1) * ROWS)
        value = ref[:, :DIM]
        rh[part, :], rl[part, :] = split(value)
        th[:, part], tl[:, part] = split(value.T)


def prepare_rows(rb_own, rb_oth):
    tall = jax.ShapeDtypeStruct((2 * ROWS, DIM), jnp.bfloat16)
    wide = jax.ShapeDtypeStruct((DIM, 2 * ROWS), jnp.bfloat16)
    return pl.pallas_call(
        rows_kernel,
        out_shape=[tall, tall, wide, wide],
        compiler_params=pltpu.CompilerParams(vmem_limit_bytes=16 * 2**20),
        cost_estimate=pl.CostEstimate(flops=2**22, bytes_accessed=2**21, transcendentals=0),
    )(rb_own, rb_oth)


def cells_kernel(adds_r, adds_g, where, *refs):
    counts = (refs[:GROUP], refs[GROUP : 2 * GROUP])
    rb, (rh, rl, th, tl, pack) = refs[8:10], refs[10:15]
    rest = list(refs[15:])
    r_in = (rest.pop(0), rest.pop(0)) if adds_r else None
    g_in = rest.pop(0) if adds_g else None
    r_out, g_out = rest[:2], rest[2]
    step = pl.program_id(0)

    @pl.when(step == 0)
    def _():
        for k in range(2):
            r_out[k][...] = r_in[k][...] if adds_r else jnp.zeros_like(r_out[k])

    xlo = where[2]
    near, far = xlo * SLICE, (1 - xlo) * SLICE
    e = split(pack[:, :SLICE, :].reshape(GROUP * SLICE, DIM))
    half = lax.broadcasted_iota(jnp.int32, (ROWS, 128), 1) < SLICE
    logs = [pack[i, SLICE : SLICE + 1, :128] for i in range(GROUP)]
    log_col = jnp.concatenate(
        [jnp.where(half[:1], logs[i], logs[i + 1]) for i in (0, 2)], axis=1
    )
    total = None
    for k in range(2):
        part = slice(k * ROWS, (k + 1) * ROWS)
        score = dot3((rh[part, :], rl[part, :]), e, ((1,), (1,)))
        gap = score - rb[k][:, DIM : DIM + 1] + log_col
        cnt = jnp.concatenate(
            [
                jnp.where(
                    half,
                    pltpu.roll(counts[k][i][...], near, 1),
                    pltpu.roll(counts[k][i + 1][...], far, 1),
                )
                for i in (0, 2)
            ],
            axis=1,
        )
        x = cnt.astype(jnp.float32)
        weight = 0.1 + 0.25 * jnp.sqrt(x)
        cell = jnp.where(
            cnt > 0,
            weight * (gap - jnp.log(jnp.maximum(x, 1.0))),
            1.0 / (1.0 + jnp.exp(-gap)),
        )
        cell = split(cell)
        r_out[k][...] += dot3(cell, e, ((1,), (0,)))
        term = dot3((th[:, part], tl[:, part]), cell, ((1,), (0,)))
        total = term if total is None else total + term
    total = total.T.reshape(GROUP, SLICE, DIM)
    g_out[...] = total + g_in[...] if adds_g else total


def cells(where, counts, rows, pack, r_in=None, g_in=None):
    def block(i):
        return pl.BlockSpec((ROWS, 128), lambda j, w: (0, (j * GROUP + i) * 4 + w[1] * 2 + w[0]))

    def whole(shape):
        return pl.BlockSpec(shape, lambda j, w: (0, 0))

    f32 = jnp.float32
    tall, wide = whole((2 * ROWS, DIM)), whole((DIM, 2 * ROWS))
    r_spec = whole((ROWS, DIM))
    g_spec = pl.BlockSpec((GROUP, SLICE, DIM), lambda j, w: (j, 0, 0))
    rb_spec = whole((ROWS, DIM + 128))
    in_specs = [block(i) for i in range(GROUP)] * 2 + [rb_spec] * 2 + [tall, tall, wide, wide]
    in_specs.append(pl.BlockSpec((GROUP, PACK, DIM), lambda j, w: (j, 0, 0)))
    args = [counts[0]] * GROUP + [counts[1]] * GROUP + list(rows) + [pack]
    if r_in is not None:
        in_specs += [r_spec] * 2
        args += list(r_in)
    if g_in is not None:
        in_specs.append(g_spec)
        args.append(g_in)
    r_one, r_two, g = pl.pallas_call(
        functools.partial(cells_kernel, r_in is not None, g_in is not None),
        grid_spec=pltpu.PrefetchScalarGridSpec(
            num_scalar_prefetch=1,
            grid=(8 // GROUP,),
            in_specs=in_specs,
            out_specs=[r_spec] * 2 + [g_spec],
        ),
        out_shape=[jax.ShapeDtypeStruct((ROWS, DIM), f32)] * 2
        + [jax.ShapeDtypeStruct((8, SLICE, DIM), f32)],
        compiler_params=pltpu.CompilerParams(vmem_limit_bytes=50 * 2**20),
        cost_estimate=pl.CostEstimate(
            flops=4 * 10**9, bytes_accessed=4 * 2**20, transcendentals=2**20
        ),
    )(where, *args)
    return (r_one, r_two), g


def body(counts, row_marg, col_marg, log_total, row_embed, col_embed):
    core, xlo, xhi = (lax.axis_index(a) for a in ("core", "xlo", "xhi"))

    def slice_at(hi, lo):
        return jnp.stack([core, hi, lo]).astype(jnp.int32)

    at_own = slice_at(xhi, xlo)
    at_a = slice_at(jnp.where(core == 0, xhi, 1 - xhi), 1 - xlo)
    at_b = slice_at(jnp.where(core == 0, 1 - xhi, xhi), 1 - xlo)
    at_far = slice_at(1 - xhi, xlo)

    start = (core * 2 + xlo) * SLICE
    embeds = lax.dynamic_slice_in_dim(col_embed, start, SLICE, 0)
    log_col = jnp.log(lax.dynamic_slice_in_dim(col_marg, start, SLICE, 0).astype(jnp.float32))
    log_row = jnp.concatenate([log_col] * 4)
    pack = jnp.concatenate(
        [embeds, jnp.broadcast_to(log_row[None, :], (PACK - SLICE, DIM))], axis=0
    )
    s_own = lax.all_to_all(jnp.broadcast_to(pack[None], (8, PACK, DIM)), "z", 0, 0)

    counts = (counts, fetch(counts, core_swap))
    base_row = log_total[0] - jnp.log(row_marg.astype(jnp.float32))
    rb = jnp.concatenate([row_embed, jnp.broadcast_to(base_row[:, None], (ROWS, 128))], axis=1)
    rb_oth = fetch(rb, core_swap)
    rows = (rb, rb_oth, *prepare_rows(rb, rb_oth))
    s_own, rows = lax.optimization_barrier((s_own, rows))

    s_a, s_b = fetch(s_own, side_a), fetch(s_own, side_b)
    r, g_own = cells(at_own, counts, rows, s_own)
    sent = fetch(g_own, side_b)
    s_far = fetch(s_a, side_b)
    r, g_a = cells(at_a, counts, rows, s_a, r)
    from_a = fetch(g_a, side_b)
    r, g_b = cells(at_b, counts, rows, s_b, r, sent)
    from_b = fetch(g_b, side_a)
    r, g = cells(at_far, counts, rows, s_far, r)
    g = g + from_a + from_b

    g = lax.all_to_all(g.reshape(64, 8, DIM), ("z", "y"), 0, 0)
    row_grad = (r[0] + fetch(r[1], core_swap)) * (1.0 / 64.0)
    g = jnp.sum(g, axis=0) * (1.0 / math.sqrt(131072.0))
    g = fetch(g, x_next)
    g = lax.all_to_all(jnp.broadcast_to(g[None], (32, 8, DIM)), ("core", "xlo", "y"), 0, 0)
    g = g.reshape(2, 2, SLICE, DIM)
    col_grad = jnp.stack([g[:, 1], g[:, 0]], axis=1)
    return row_grad, col_grad.reshape(256, DIM)


def solution(mesh):
    fine = Mesh(mesh.devices.reshape(SIZES), AXES)
    both = ("xlo", "y", "core", "z", "xhi")
    col = ("z", "xhi")
    return jax.shard_map(
        body,
        mesh=fine,
        in_specs=(P(both, None), P(both), P(col), P(), P(both, None), P(col, None)),
        out_specs=(P(both, None), P(col, None)),
        check_vma=False,
    )
```

time: 159 us -> 134 us (0.84); the launches traced: 159 us -> 131 us
  waiting for transfers between devices: 65.8 us -> 29.5 us
  Pallas kernels: 14.8 us -> 21.4 us
  starting transfers between devices: 40.7 us -> 45.8 us
  blocking collectives: 26.7 us -> 25 us
    ppermute x9 -> x10, waiting for transfers between devices: 40.7 us -> 8.83 us  [fetch(): return lax.ppermute(value, AXES, pairs_to(move))]
    pallas_call x1 -> x5, Pallas kernels: 14.8 us -> 21.4 us  [the longest x4 21.2 us: cells(): pl.pallas_call(functools.partial(cells_kernel, r_in is not None, g_in is...]
    all_to_all x1, waiting for transfers between devices: 19 us -> 13.4 us  [body(): lax.all_to_all(jnp.broadcast_to(pack[None], (8, PACK, DIM)), 'z', 0, 0)]
    ppermute x9 -> x10, starting transfers between devices: 25.1 us -> 30.1 us  [fetch(): return lax.ppermute(value, AXES, pairs_to(move))]
    all_to_all x1, blocking collectives: 26.7 us -> 25 us  [body(): g = lax.all_to_all(g.reshape(64, 8, DIM), ('z', 'y'), 0, 0)]
  transfers between devices with their start and end apart: 11 -> 12, of which waited for: 8 -> 7; matrix products, arithmetic and copies ran while one was open for 3% -> 3% of each run, Pallas kernels for 0% -> 16%
where the time goes in v2:
time: 134 us; the launch traced here: 131 us
  starting transfers between devices  45.8 us (34%)
  waiting for transfers between devices  29.5 us (22%)
  blocking collectives  25 us (19%)
  Pallas kernels  21.4 us (16%)
  other arithmetic  4.46 us (3%)
  local copies, waits for them, and re-layouts  3.36 us (3%)
  between operations  1.53 us (1%)
    ppermute x10, starting transfers between devices, fetch(): return lax.ppermute(value, AXES, pairs_to(move))  30.1 us
    all_to_all x1, blocking collectives, body(): g = lax.all_to_all(g.reshape(64, 8, DIM), ('z', 'y'), 0, 0)  25 us
    pallas_call x4, Pallas kernels, cells(): pl.pallas_call(functools.partial(cells_kernel, r_in is not None, g_in is...  21.2 us
    all_to_all x1, waiting for transfers between devices, body(): lax.all_to_all(jnp.broadcast_to(pack[None], (8, PACK, DIM)), 'z', 0, 0)  13.4 us
    all_to_all x1, starting transfers between devices, body(): lax.all_to_all(jnp.broadcast_to(pack[None], (8, PACK, DIM)), 'z', 0, 0)  10.3 us
    ppermute x10, waiting for transfers between devices, fetch(): return lax.ppermute(value, AXES, pairs_to(move))  8.83 us
    all_to_all x1, waiting for transfers between devices, body(): lax.all_to_all(jnp.broadcast_to(g[None], (32, 8, DIM)), ('core', 'xlo', '...  7.33 us
    all_to_all x1, starting transfers between devices, body(): lax.all_to_all(jnp.broadcast_to(g[None], (32, 8, DIM)), ('core', 'xlo', '...  5.34 us
  transfers between devices with their start and end apart: 12, of which 7 were waited for; matrix products, arithmetic and copies ran while one was open for 3% of the time, Pallas kernels for 16%

profile of v2, /device:TPU:6, one launch (start us, length us, event | category | flops | bytes accessed | tf_op | source)
XLA Modules:
  0.0 131.1 jit_solution(2858757108670789114)
XLA Ops:
  0.6 2.1 %collective-permute-start = (s32[256,4096]{1,0:T(8,128)}, s32[256,4096]{1,0:T(8,128)}, u32[]{:S(2)}, u32[]{:S(2)}) collective-permute-start(s32[256,4096]{1,0:T(8,128)} %refs_3_.7), channel_id=1, source_target_pairs={{16,0},{17,1},{18,2},{19,3},{20,4},{21,5},{22,6},{23,7},{24,8},{25... | collective-permute-start | bytes 12582920 | tf_op jit(solution)/shard_map/ppermute | solution.py:51
  2.7 0.8 convert_log_fusion
  3.6 0.9 broadcast_in_dim.9
  4.5 10.3 %all-to-all-start = ((f32[8,72,256]{2,1,0:T(8,128)}), f32[8,72,256]{2,1,0:T(8,128)S(1)}, u32[]{:S(2)}, u32[]{:S(2)}) async-start(f32[8,72,256]{2,1,0:T(8,128)} %broadcast_in_dim.9), calls=%async_computation | async-start | bytes 1179648 | tf_op jit(solution)/shard_map/all_to_all | solution.py:195
  15.4 0.7 log_subtract_fusion
  16.2 1.0 pad_maximum_fusion.rb_own.refs_8_
  17.2 2.1 %collective-permute-start.1 = (f32[256,384]{1,0:T(8,128)S(1)}, f32[256,384]{1,0:T(8,128)S(1)}, u32[]{:S(2)}, u32[]{:S(2)}) collective-permute-start(f32[256,384]{1,0:T(8,128)S(1)} %pad_maximum_fusion.rb_own.refs_8_), channel_id=1, source_target_pairs={{16,0},{17,1},{18,2},{19,3},{20,4},{21,5},{22,6},{23,7},{24,8},{25... | collective-permute-start | bytes 1179656 | tf_op jit(solution)/shard_map/ppermute | solution.py:51
  19.4 1.4 %collective-permute-done.1.rb_oth.refs_9_ = f32[256,384]{1,0:T(8,128)S(1)} collective-permute-done((f32[256,384]{1,0:T(8,128)S(1)}, f32[256,384]{1,0:T(8,128)S(1)}, u32[]{:S(2)}, u32[]{:S(2)}) %collective-permute-start.1) | collective-permute-done | bytes 393248 | tf_op jit(solution)/shard_map/ppermute | solution.py:51
  21.0 13.4 %all-to-all-done.refs_14_ = f32[8,72,256]{2,1,0:T(8,128)S(1)} async-done(((f32[8,72,256]{2,1,0:T(8,128)}), f32[8,72,256]{2,1,0:T(8,128)S(1)}, u32[]{:S(2)}, u32[]{:S(2)}) %all-to-all-start) | async-done | bytes 589856 | tf_op jit(solution)/shard_map/all_to_all | solution.py:195
  34.4 2.7 %collective-permute-start.2 = (f32[8,72,256]{2,1,0:T(8,128)S(1)}, f32[8,72,256]{2,1,0:T(8,128)S(1)}, u32[]{:S(2)}, u32[]{:S(2)}) collective-permute-start(f32[8,72,256]{2,1,0:T(8,128)S(1)} %all-to-all-done.refs_14_), channel_id=1, source_target_pairs={{256,0},{257,1},{258,2},{259,3},{260,4},{261,5},{262,6},{263,7},{2... | collective-permute-start | bytes 1769480 | tf_op jit(solution)/shard_map/ppermute | solution.py:51
  37.1 3.0 %collective-permute-start.4 = (f32[8,72,256]{2,1,0:T(8,128)S(1)}, f32[8,72,256]{2,1,0:T(8,128)}, u32[]{:S(2)}, u32[]{:S(2)}) collective-permute-start(f32[8,72,256]{2,1,0:T(8,128)S(1)} %all-to-all-done.refs_14_), channel_id=1, source_target_pairs={{257,0},{256,1},{259,2},{258,3},{261,4},{260,5},{263,6},{262,7},{2... | collective-permute-start | bytes 1769480 | tf_op jit(solution)/shard_map/ppermute | solution.py:51
  40.2 5.7 %shard_map.78 = (f32[256,256]{1,0:T(8,128)S(1)}, f32[256,256]{1,0:T(8,128)S(1)}, f32[8,64,256]{2,1,0:T(8,128)}) custom-call(s32[3]{0:T(128)S(1)} %add_add_fusion.4.where, s32[256,4096]{1,0:T(8,128)} %refs_3_.7, s32[256,4096]{1,0:T(8,128)} %refs_3_.7, s32[256,4096]{1,0:T(8,128)} %refs_3_.7, s32[256,4096]{1,0:T(8,128)} %refs_3_.7, ...), custom_call_target="tpu_custom_call" | custom-call | flops 4000000000 | bytes 4194304 | tf_op jit(solution)/shard_map/pallas_call | solution.py:159
  45.9 0.7 copy-done.1
  46.6 4.0 %collective-permute-start.5 = (f32[8,64,256]{2,1,0:T(8,128)}, f32[8,64,256]{2,1,0:T(8,128)}, u32[]{:S(2)}, u32[]{:S(2)}) collective-permute-start(f32[8,64,256]{2,1,0:T(8,128)} %get-tuple-element.40), channel_id=1, source_target_pairs={{257,0},{256,1},{259,2},{258,3},{261,4},{260,5},{263,6},{262,7},{2... | collective-permute-start | bytes 1572872 | tf_op jit(solution)/shard_map/ppermute | solution.py:51
  51.3 2.6 %collective-permute-start.3 = (f32[8,72,256]{2,1,0:T(8,128)S(1)}, f32[8,72,256]{2,1,0:T(8,128)S(1)}, u32[]{:S(2)}, u32[]{:S(2)}) collective-permute-start(f32[8,72,256]{2,1,0:T(8,128)S(1)} %collective-permute-done.2.refs_14_), channel_id=1, source_target_pairs={{257,0},{256,1},{259,2},{258,3},{261,4},{260,5},{263,6},{262,7},{2... | collective-permute-start | bytes 1769480 | tf_op jit(solution)/shard_map/ppermute | solution.py:51
  53.8 0.9 copy-done.2
  54.8 5.1 %shard_map.79 = (f32[256,256]{1,0:T(8,128)S(1)}, f32[256,256]{1,0:T(8,128)S(1)}, f32[8,64,256]{2,1,0:T(8,128)S(1)}) custom-call(s32[3]{0:T(128)S(1)} %add_add_fusion.3.where, s32[256,4096]{1,0:T(8,128)} %refs_3_.7, s32[256,4096]{1,0:T(8,128)} %refs_3_.7, s32[256,4096]{1,0:T(8,128)} %refs_3_.7, s32[256,4096]{1,0:T(8,128)} %refs_3_.7, ...), custom_call_target="tpu_custom_call" | custom-call | flops 4000000000 | bytes 4194304 | tf_op jit(solution)/shard_map/pallas_call | solution.py:159
  59.9 4.5 %collective-permute-start.7 = (f32[8,64,256]{2,1,0:T(8,128)S(1)}, f32[8,64,256]{2,1,0:T(8,128)S(1)}, u32[]{:S(2)}, u32[]{:S(2)}) collective-permute-start(f32[8,64,256]{2,1,0:T(8,128)S(1)} %get-tuple-element.46), channel_id=1, source_target_pairs={{257,0},{256,1},{259,2},{258,3},{261,4},{260,5},{263,6},{262,7},{2... | collective-permute-start | bytes 1572872 | tf_op jit(solution)/shard_map/ppermute | solution.py:51
  64.4 5.3 %shard_map.80 = (f32[256,256]{1,0:T(8,128)S(1)}, f32[256,256]{1,0:T(8,128)S(1)}, f32[8,64,256]{2,1,0:T(8,128)S(1)}) custom-call(s32[3]{0:T(128)S(1)} %add_add_fusion.2.where, s32[256,4096]{1,0:T(8,128)} %refs_3_.7, s32[256,4096]{1,0:T(8,128)} %refs_3_.7, s32[256,4096]{1,0:T(8,128)} %refs_3_.7, s32[256,4096]{1,0:T(8,128)} %refs_3_.7, ...), custom_call_target="tpu_custom_call" | custom-call | flops 4000000000 | bytes 4194304 | tf_op jit(solution)/shard_map/pallas_call | solution.py:159
  69.7 1.9 %collective-permute-start.8 = (f32[8,64,256]{2,1,0:T(8,128)S(1)}, f32[8,64,256]{2,1,0:T(8,128)S(1)}, u32[]{:S(2)}, u32[]{:S(2)}) collective-permute-start(f32[8,64,256]{2,1,0:T(8,128)S(1)} %get-tuple-element.47), channel_id=1, source_target_pairs={{256,0},{257,1},{258,2},{259,3},{260,4},{261,5},{262,6},{263,7},{2... | collective-permute-start | bytes 1572872 | tf_op jit(solution)/shard_map/ppermute | solution.py:51
  71.7 5.1 %shard_map.81 = (f32[256,256]{1,0:T(8,128)S(1)}, f32[256,256]{1,0:T(8,128)S(1)}, f32[8,64,256]{2,1,0:T(8,128)S(1)}) custom-call(s32[3]{0:T(128)S(1)} %add_add_fusion.1.where, s32[256,4096]{1,0:T(8,128)} %refs_3_.7, s32[256,4096]{1,0:T(8,128)} %refs_3_.7, s32[256,4096]{1,0:T(8,128)} %refs_3_.7, s32[256,4096]{1,0:T(8,128)} %refs_3_.7, ...), custom_call_target="tpu_custom_call" | custom-call | flops 4000000000 | bytes 4194304 | tf_op jit(solution)/shard_map/pallas_call | solution.py:159
  76.8 4.0 %collective-permute-done.8 = f32[8,64,256]{2,1,0:T(8,128)S(1)} collective-permute-done((f32[8,64,256]{2,1,0:T(8,128)S(1)}, f32[8,64,256]{2,1,0:T(8,128)S(1)}, u32[]{:S(2)}, u32[]{:S(2)}) %collective-permute-start.8) | collective-permute-done | bytes 524320 | tf_op jit(solution)/shard_map/ppermute | solution.py:51
  80.9 25.0 %all_to_all.15 = f32[64,8,256]{2,1,0:T(8,128)S(1)} all-to-all(f32[64,8,256]{2,1,0:T(8,128)S(1)} %bitcast.12), channel_id=1, replica_groups=mesh['xlo'=2,'y'=8,'core'=2,'z'=8,'xhi'=2] {'z','y'}, dimensions={0} | all-to-all | bytes 1048576 | tf_op jit(solution)/shard_map/all_to_all | solution.py:215
  106.0 5.1 %collective-permute-start.9 = (f32[8,256]{1,0:T(8,128)S(1)}, f32[8,256]{1,0:T(8,128)S(1)}, u32[]{:S(2)}, u32[]{:S(2)}) collective-permute-start(f32[8,256]{1,0:T(8,128)S(1)} %broadcast_multiply_fusion), channel_id=1, source_target_pairs={{257,0},{256,1},{259,2},{258,3},{261,4},{260,5},{263,6},{262,7},{2... | collective-permute-start | bytes 24584 | tf_op jit(solution)/shard_map/ppermute | solution.py:51
  111.1 1.6 %collective-permute-done.9 = f32[8,256]{1,0:T(8,128)S(1)} collective-permute-done((f32[8,256]{1,0:T(8,128)S(1)}, f32[8,256]{1,0:T(8,128)S(1)}, u32[]{:S(2)}, u32[]{:S(2)}) %collective-permute-start.9) | collective-permute-done | bytes 8224 | tf_op jit(solution)/shard_map/ppermute | solution.py:51
  112.7 0.7 broadcast_in_dim.11
  113.5 5.3 %all-to-all-start.2 = ((f32[32,8,256]{2,1,0:T(8,128)}), f32[32,8,256]{2,1,0:T(8,128)S(1)}, u32[]{:S(2)}, u32[]{:S(2)}) async-start(f32[32,8,256]{2,1,0:T(8,128)} %broadcast_in_dim.11), calls=%async_computation.2 | async-start | bytes 524288 | tf_op jit(solution)/shard_map/all_to_all | solution.py:219
  118.8 2.1 %collective-permute-start.6 = (f32[256,256]{1,0:T(8,128)S(1)}, f32[256,256]{1,0:T(8,128)S(1)}, u32[]{:S(2)}, u32[]{:S(2)}) collective-permute-start(f32[256,256]{1,0:T(8,128)S(1)} %get-tuple-element.44), channel_id=1, source_target_pairs={{16,0},{17,1},{18,2},{19,3},{20,4},{21,5},{22,6},{23,7},{24,8},{25... | collective-permute-start | bytes 786440 | tf_op jit(solution)/shard_map/ppermute | solution.py:51
  120.9 1.4 %collective-permute-done.6 = f32[256,256]{1,0:T(8,128)S(1)} collective-permute-done((f32[256,256]{1,0:T(8,128)S(1)}, f32[256,256]{1,0:T(8,128)S(1)}, u32[]{:S(2)}, u32[]{:S(2)}) %collective-permute-start.6) | collective-permute-done | bytes 262176 | tf_op jit(solution)/shard_map/ppermute | solution.py:51
  122.2 0.7 add_multiply_fusion
  123.0 7.3 %all-to-all-done.2 = f32[32,8,256]{2,1,0:T(8,128)S(1)} async-done(((f32[32,8,256]{2,1,0:T(8,128)}), f32[32,8,256]{2,1,0:T(8,128)S(1)}, u32[]{:S(2)}, u32[]{:S(2)}) %all-to-all-start.2) | async-done | bytes 262176 | tf_op jit(solution)/shard_map/all_to_all | solution.py:219
  130.3 0.7 pad_maximum_fusion.1
  (24 shorter events, 1.4 us)
Async XLA Ops:
  0.6 2.9 %copy-start = (f32[256,256]{1,0:T(8,128)S(1)}, f32[256,256]{1,0:T(8,128)}, u32[]{:S(2)}) copy-start(f32[256,256]{1,0:T(8,128)} %param.11) | copy-start | bytes 786436
  0.6 39.5 %collective-permute-start = (s32[256,4096]{1,0:T(8,128)}, s32[256,4096]{1,0:T(8,128)}, u32[]{:S(2)}, u32[]{:S(2)}) collective-permute-start(s32[256,4096]{1,0:T(8,128)} %refs_3_.7), channel_id=1, source_target_pairs={{16,0},{17,1},{18,2},{19,3},{20,4},{21,5},{22,6},{23,7},{24,8},{25... | collective-permute-start | bytes 12582920 | tf_op jit(solution)/shard_map/ppermute | solution.py:51
  4.5 29.9 %all-to-all-start = ((f32[8,72,256]{2,1,0:T(8,128)}), f32[8,72,256]{2,1,0:T(8,128)S(1)}, u32[]{:S(2)}, u32[]{:S(2)}) async-start(f32[8,72,256]{2,1,0:T(8,128)} %broadcast_in_dim.9), calls=%async_computation | async-start | bytes 1179648 | tf_op jit(solution)/shard_map/all_to_all | solution.py:195
  17.2 3.6 %collective-permute-start.1 = (f32[256,384]{1,0:T(8,128)S(1)}, f32[256,384]{1,0:T(8,128)S(1)}, u32[]{:S(2)}, u32[]{:S(2)}) collective-permute-start(f32[256,384]{1,0:T(8,128)S(1)} %pad_maximum_fusion.rb_own.refs_8_), channel_id=1, source_target_pairs={{16,0},{17,1},{18,2},{19,3},{20,4},{21,5},{22,6},{23,7},{24,8},{25... | collective-permute-start | bytes 1179656 | tf_op jit(solution)/shard_map/ppermute | solution.py:51
  34.4 16.9 %collective-permute-start.2 = (f32[8,72,256]{2,1,0:T(8,128)S(1)}, f32[8,72,256]{2,1,0:T(8,128)S(1)}, u32[]{:S(2)}, u32[]{:S(2)}) collective-permute-start(f32[8,72,256]{2,1,0:T(8,128)S(1)} %all-to-all-done.refs_14_), channel_id=1, source_target_pairs={{256,0},{257,1},{258,2},{259,3},{260,4},{261,5},{262,6},{263,7},{2... | collective-permute-start | bytes 1769480 | tf_op jit(solution)/shard_map/ppermute | solution.py:51
  37.1 27.3 %collective-permute-start.4 = (f32[8,72,256]{2,1,0:T(8,128)S(1)}, f32[8,72,256]{2,1,0:T(8,128)}, u32[]{:S(2)}, u32[]{:S(2)}) collective-permute-start(f32[8,72,256]{2,1,0:T(8,128)S(1)} %all-to-all-done.refs_14_), channel_id=1, source_target_pairs={{257,0},{256,1},{259,2},{258,3},{261,4},{260,5},{263,6},{262,7},{2... | collective-permute-start | bytes 1769480 | tf_op jit(solution)/shard_map/ppermute | solution.py:51
  45.9 0.7 copy-start.1
  46.6 17.8 %collective-permute-start.5 = (f32[8,64,256]{2,1,0:T(8,128)}, f32[8,64,256]{2,1,0:T(8,128)}, u32[]{:S(2)}, u32[]{:S(2)}) collective-permute-start(f32[8,64,256]{2,1,0:T(8,128)} %get-tuple-element.40), channel_id=1, source_target_pairs={{257,0},{256,1},{259,2},{258,3},{261,4},{260,5},{263,6},{262,7},{2... | collective-permute-start | bytes 1572872 | tf_op jit(solution)/shard_map/ppermute | solution.py:51
  51.3 20.5 %collective-permute-start.3 = (f32[8,72,256]{2,1,0:T(8,128)S(1)}, f32[8,72,256]{2,1,0:T(8,128)S(1)}, u32[]{:S(2)}, u32[]{:S(2)}) collective-permute-start(f32[8,72,256]{2,1,0:T(8,128)S(1)} %collective-permute-done.2.refs_14_), channel_id=1, source_target_pairs={{257,0},{256,1},{259,2},{258,3},{261,4},{260,5},{263,6},{262,7},{2... | collective-permute-start | bytes 1769480 | tf_op jit(solution)/shard_map/ppermute | solution.py:51
  53.8 1.0 copy-start.2
  59.9 16.9 %collective-permute-start.7 = (f32[8,64,256]{2,1,0:T(8,128)S(1)}, f32[8,64,256]{2,1,0:T(8,128)S(1)}, u32[]{:S(2)}, u32[]{:S(2)}) collective-permute-start(f32[8,64,256]{2,1,0:T(8,128)S(1)} %get-tuple-element.46), channel_id=1, source_target_pairs={{257,0},{256,1},{259,2},{258,3},{261,4},{260,5},{263,6},{262,7},{2... | collective-permute-start | bytes 1572872 | tf_op jit(solution)/shard_map/ppermute | solution.py:51
  69.7 11.1 %collective-permute-start.8 = (f32[8,64,256]{2,1,0:T(8,128)S(1)}, f32[8,64,256]{2,1,0:T(8,128)S(1)}, u32[]{:S(2)}, u32[]{:S(2)}) collective-permute-start(f32[8,64,256]{2,1,0:T(8,128)S(1)} %get-tuple-element.47), channel_id=1, source_target_pairs={{256,0},{257,1},{258,2},{259,3},{260,4},{261,5},{262,6},{263,7},{2... | collective-permute-start | bytes 1572872 | tf_op jit(solution)/shard_map/ppermute | solution.py:51
  106.0 6.8 %collective-permute-start.9 = (f32[8,256]{1,0:T(8,128)S(1)}, f32[8,256]{1,0:T(8,128)S(1)}, u32[]{:S(2)}, u32[]{:S(2)}) collective-permute-start(f32[8,256]{1,0:T(8,128)S(1)} %broadcast_multiply_fusion), channel_id=1, source_target_pairs={{257,0},{256,1},{259,2},{258,3},{261,4},{260,5},{263,6},{262,7},{2... | collective-permute-start | bytes 24584 | tf_op jit(solution)/shard_map/ppermute | solution.py:51
  113.5 16.8 %all-to-all-start.2 = ((f32[32,8,256]{2,1,0:T(8,128)}), f32[32,8,256]{2,1,0:T(8,128)S(1)}, u32[]{:S(2)}, u32[]{:S(2)}) async-start(f32[32,8,256]{2,1,0:T(8,128)} %broadcast_in_dim.11), calls=%async_computation.2 | async-start | bytes 524288 | tf_op jit(solution)/shard_map/all_to_all | solution.py:219
  118.8 3.4 %collective-permute-start.6 = (f32[256,256]{1,0:T(8,128)S(1)}, f32[256,256]{1,0:T(8,128)S(1)}, u32[]{:S(2)}, u32[]{:S(2)}) collective-permute-start(f32[256,256]{1,0:T(8,128)S(1)} %get-tuple-element.44), channel_id=1, source_target_pairs={{16,0},{17,1},{18,2},{19,3},{20,4},{21,5},{22,6},{23,7},{24,8},{25... | collective-permute-start | bytes 786440 | tf_op jit(solution)/shard_map/ppermute | solution.py:51

commit v3 on v2

v3 whole, which is shorter than its diff:
```python
import functools
import math

import jax
import jax.numpy as jnp
import numpy as np
from jax import lax
from jax.experimental import pallas as pl
from jax.experimental.pallas import tpu as pltpu
from jax.sharding import Mesh, PartitionSpec as P

AXES = ("xlo", "y", "core", "z", "xhi")
SIZES = (2, 8, 2, 8, 2)
DIM = 256
ROWS = 256
SLICE = 64
PACK = 72
STRIP = 64
GROUP = 4


def pairs_to(move):
    pairs = []
    for target in range(math.prod(SIZES)):
        at = dict(zip(AXES, (int(i) for i in np.unravel_index(target, SIZES))))
        at.update(move(at))
        pairs.append((int(np.ravel_multi_index([at[a] for a in AXES], SIZES)), target))
    return pairs


def x_far(at):
    return {"xhi": 1 - at["xhi"]}


def core_swap(at):
    return {"core": 1 - at["core"]}


def x_pair(at):
    return {"xlo": 1 - at["xlo"]}


def x_next(at):
    return {"xlo": 1 - at["xlo"], "xhi": 1 - at["xhi"]}


def side_a(at):
    return x_next(at) if at["core"] else x_pair(at)


def side_b(at):
    return x_pair(at) if at["core"] else x_next(at)


def fetch(value, move):
    return lax.ppermute(value, AXES, pairs_to(move))


def split(value):
    high = value.astype(jnp.bfloat16)
    return high, (value - high.astype(jnp.float32)).astype(jnp.bfloat16)


def dot(a, b, dims):
    return lax.dot_general(
        a, b, dimension_numbers=(dims, ((), ())), preferred_element_type=jnp.float32
    )


def left(pair, axis):
    return jnp.concatenate([pair[0], pair[0], pair[1]], axis=axis)


def right(pair, axis):
    return jnp.concatenate([pair[0], pair[1], pair[0]], axis=axis)


def pack_kernel(embed, marg, out):
    start = (2 * lax.axis_index("core") + lax.axis_index("xlo")) * SLICE
    out[:, :SLICE, :] = jnp.broadcast_to(
        embed[pl.ds(pl.multiple_of(start, SLICE), SLICE), :][None], (8, SLICE, DIM)
    )
    logs = jnp.log(marg[...].astype(jnp.float32))
    out[:, SLICE:, :] = jnp.broadcast_to(logs[None], (8, PACK - SLICE, DIM))


def pack_slice(col_embed, col_marg):
    return pl.pallas_call(
        pack_kernel,
        out_shape=jax.ShapeDtypeStruct((8, PACK, DIM), jnp.float32),
        compiler_params=pltpu.CompilerParams(vmem_limit_bytes=60 * 2**20),
    )(col_embed, col_marg.reshape(1, DIM))


def prepare_kernel(table, c_own, c_oth, rb_own, rb_oth, *outs):
    weight_out, shift_out, tall_out, wide_out = outs[:4], outs[4:8], outs[8], outs[9]
    step = pl.program_id(0)
    steps = pl.num_programs(0)

    @pl.when(step == 0)
    def _():
        for k, rb in enumerate((rb_own, rb_oth)):
            part = slice(k * ROWS, (k + 1) * ROWS)
            value = rb[:, :DIM]
            tall_out[part, :] = left(split(value), 1)
            wide = split(value.T)
            for n, source in enumerate((wide[0], wide[0], wide[1])):
                start = n * 2 * ROWS + k * ROWS
                wide_out[:, start : start + ROWS] = source

    def work(counts, rb, block):
        half = lax.broadcasted_iota(jnp.int32, (STRIP, 128), 1) < SLICE
        base = rb[pl.ds(pl.multiple_of(block * STRIP, STRIP), STRIP), DIM:]
        for which in range(4):
            core, xhi, xlo = (table[which * 3 + i] for i in range(3))
            near, far = xlo * SLICE, (1 - xlo) * SLICE
            for n in range(4):
                tiles = [
                    counts[:, pl.ds(pl.multiple_of((z * 4 + xhi * 2 + core) * 128, 128), 128)]
                    for z in (2 * n, 2 * n + 1)
                ]
                cnt = jnp.where(half, pltpu.roll(tiles[0], near, 1), pltpu.roll(tiles[1], far, 1))
                x = jnp.maximum(cnt, 1).astype(jnp.float32)
                weight = jnp.where(cnt > 0, 0.1 + 0.25 * (x * lax.rsqrt(x)), 0.0)
                weight_out[which][:, n * 128 : (n + 1) * 128] = weight
                shift_out[which][:, n * 128 : (n + 1) * 128] = jnp.log(x) + base

    @pl.when(step < steps // 2)
    def _():
        work(c_own, rb_own, step)

    @pl.when(step >= steps // 2)
    def _():
        work(c_oth, rb_oth, step - steps // 2)


def prepare(table, counts, rb):
    half = ROWS // STRIP

    def whole(shape):
        return pl.BlockSpec(shape, lambda i, w: (0, 0))

    columns = counts[0].shape[1]
    cell_spec = pl.BlockSpec((STRIP, 2 * DIM), lambda i, w: (i, 0))
    cell_shape = jax.ShapeDtypeStruct((2 * ROWS, 2 * DIM), jnp.float32)
    *cell, tall, wide = pl.pallas_call(
        prepare_kernel,
        grid_spec=pltpu.PrefetchScalarGridSpec(
            num_scalar_prefetch=1,
            grid=(2 * half,),
            in_specs=[
                pl.BlockSpec((STRIP, columns), lambda i, w: (jnp.minimum(i, half - 1), 0)),
                pl.BlockSpec((STRIP, columns), lambda i, w: (jnp.maximum(i - half, 0), 0)),
            ]
            + [whole((ROWS, DIM + 128))] * 2,
            out_specs=[cell_spec] * 8 + [whole((2 * ROWS, 3 * DIM)), whole((DIM, 6 * ROWS))],
        ),
        out_shape=[cell_shape] * 8
        + [
            jax.ShapeDtypeStruct((2 * ROWS, 3 * DIM), jnp.bfloat16),
            jax.ShapeDtypeStruct((DIM, 6 * ROWS), jnp.bfloat16),
        ],
        compiler_params=pltpu.CompilerParams(vmem_limit_bytes=48 * 2**20),
        cost_estimate=pl.CostEstimate(flops=4 * 10**9, bytes_accessed=2**23, transcendentals=2**20),
    )(table, *counts, *rb)
    return cell[:4], cell[4:], tall, wide


def cells_kernel(which, adds_r, adds_g, table, weight, shift, tall, wide, pack, *rest):
    rest = list(rest)
    r_in = rest.pop(0) if adds_r else None
    g_in = rest.pop(0) if adds_g else None
    r_out, g_out = rest
    offset = (2 * table[3 * which] + table[3 * which + 2]) * SLICE
    near, far = lax.rem(DIM - offset, DIM), lax.rem(DIM + SLICE - offset, DIM)
    half = lax.broadcasted_iota(jnp.int32, (1, 128), 1) < SLICE
    r_sum = None
    for j in range(8 // GROUP):
        part = slice(j * DIM, (j + 1) * DIM)
        here = pack[j * GROUP : (j + 1) * GROUP]
        e = split(here[:, :SLICE, :].reshape(DIM, DIM))
        logs = [here[i, SLICE : SLICE + 8, :] for i in range(GROUP)]
        log_col = jnp.concatenate(
            [
                jnp.where(
                    half,
                    pltpu.roll(logs[i], near, 1)[:1, :128],
                    pltpu.roll(logs[i + 1], far, 1)[:1, :128],
                )
                for i in (0, 2)
            ],
            axis=1,
        )
        gap = dot(tall[...], right(e, 1), ((1,), (1,))) + log_col - shift[:, part]
        w = weight[:, part]
        cell = split(jnp.where(w > 0.0, w * gap, 0.5 + 0.5 * jnp.tanh(0.5 * gap)))
        r_term = dot(left(cell, 1), right(e, 0), ((1,), (0,)))
        r_sum = r_term if r_sum is None else r_sum + r_term
        total = dot(wide[...], right(cell, 0), ((1,), (0,))).T.reshape(GROUP, SLICE, DIM)
        if adds_g:
            total += g_in[j * GROUP : (j + 1) * GROUP]
        g_out[j * GROUP : (j + 1) * GROUP] = total
    r_out[...] = r_sum + r_in[...] if adds_r else r_sum


def cells(which, table, prepared, pack, r_in=None, g_in=None):
    vmem = pl.BlockSpec(memory_space=pltpu.VMEM)
    weights, shifts, tall, wide = prepared
    args = [weights[which], shifts[which], tall, wide, pack] + [a for a in (r_in, g_in) if a is not None]
    return pl.pallas_call(
        functools.partial(cells_kernel, which, r_in is not None, g_in is not None),
        in_specs=[pl.BlockSpec(memory_space=pltpu.SMEM)] + [vmem] * len(args),
        out_specs=[vmem] * 2,
        out_shape=[
            jax.ShapeDtypeStruct((2 * ROWS, DIM), jnp.float32),
            jax.ShapeDtypeStruct((8, SLICE, DIM), jnp.float32),
        ],
        compiler_params=pltpu.CompilerParams(vmem_limit_bytes=32 * 2**20),
        cost_estimate=pl.CostEstimate(
            flops=3 * 10**9, bytes_accessed=2**22, transcendentals=2**18
        ),
    )(table, *args)


def body(counts, row_marg, col_marg, log_total, row_embed, col_embed):
    core, xlo, xhi = (lax.axis_index(a) for a in ("core", "xlo", "xhi"))
    table = jnp.stack(
        [core, xhi, xlo]
        + [core, jnp.where(core == 0, xhi, 1 - xhi), 1 - xlo]
        + [core, jnp.where(core == 0, 1 - xhi, xhi), 1 - xlo]
        + [core, 1 - xhi, xlo]
    ).astype(jnp.int32)

    pack, row_marg = lax.optimization_barrier((pack_slice(col_embed, col_marg), row_marg))
    s_own = lax.all_to_all(pack, "z", 0, 0)

    base_row = log_total[0] - jnp.log(row_marg.astype(jnp.float32))
    rb = jnp.concatenate([row_embed, jnp.broadcast_to(base_row[:, None], (ROWS, 128))], axis=1)
    rb, counts = lax.optimization_barrier((rb, counts))
    prepared = prepare(table, (counts, fetch(counts, core_swap)), (rb, fetch(rb, core_swap)))
    weights, shifts, tall, wide = prepared
    s_own, tall = lax.optimization_barrier((s_own, tall))
    prepared = (weights, shifts, tall, wide)

    s_a, s_b = fetch(s_own, side_a), fetch(s_own, side_b)
    r, g_own = cells(0, table, prepared, s_own)
    sent = fetch(g_own, side_b)
    s_far = fetch(s_a, side_b)
    r, g_a = cells(1, table, prepared, s_a, r)
    from_a = fetch(g_a, side_b)
    r, g_b = cells(2, table, prepared, s_b, r, sent)
    from_b = fetch(g_b, side_a)
    r, g = cells(3, table, prepared, s_far, r)
    g = g + from_a + from_b

    g = lax.all_to_all(g.reshape(64, 8, DIM), ("z", "y"), 0, 0)
    row_grad = (r[:ROWS] + fetch(r[ROWS:], core_swap)) * (1.0 / 64.0)
    g = jnp.sum(g, axis=0) * (1.0 / math.sqrt(131072.0))
    g = fetch(g, x_far)
    g = lax.all_to_all(jnp.broadcast_to(g[None], (32, 8, DIM)), ("core", "xlo", "y"), 0, 0)
    return row_grad, g.reshape(256, DIM)


def solution(mesh):
    fine = Mesh(mesh.devices.reshape(SIZES), AXES)
    both = ("xlo", "y", "core", "z", "xhi")
    col = ("z", "xhi")
    return jax.shard_map(
        body,
        mesh=fine,
        in_specs=(P(both, None), P(both), P(col), P(), P(both, None), P(col, None)),
        out_specs=(P(both, None), P(col, None)),
        check_vma=False,
    )
```

time: 134 us -> 139 us (1.037)
  local copies, waits for them, and re-layouts: 3.36 us -> 9.12 us
  blocking collectives: 25 us -> 29.8 us
  waiting for transfers between devices: 29.5 us -> 26.6 us
  other arithmetic: 4.46 us -> 2.58 us
  Pallas kernels: 21.4 us -> 23.2 us
  starting transfers between devices: 45.8 us -> 44 us
    all_to_all x1, waiting for transfers between devices: 13.4 us -> 3.28 us  [body(): s_own = lax.all_to_all(pack, 'z', 0, 0)]
    ppermute x10, waiting for transfers between devices: 8.83 us -> 16 us  [fetch(): return lax.ppermute(value, AXES, pairs_to(move))]
    unnamed x6 -> x23, local copies, waits for them, and re-layouts: 1.66 us -> 8.2 us
    all_to_all x1, blocking collectives: 25 us -> 29.8 us  [body(): g = lax.all_to_all(g.reshape(64, 8, DIM), ('z', 'y'), 0, 0)]
    pallas_call x5 -> x6, Pallas kernels: 21.4 us -> 23.2 us  [the longest x4 11.5 us: cells(): pl.pallas_call(functools.partial(cells_kernel, which, r_in is not None, g...]
    ppermute x10, starting transfers between devices: 30.1 us -> 28.5 us  [fetch(): return lax.ppermute(value, AXES, pairs_to(move))]
  transfers between devices with their start and end apart: 12 -> 12, of which waited for: 7 -> 7; matrix products, arithmetic and copies ran while one was open for 3% -> 1% of each run, Pallas kernels for 16% -> 16%
where the time goes in v3:
time: 139 us; the launch traced here: 137 us
  starting transfers between devices  44 us (32%)
  blocking collectives  29.8 us (21%)
  waiting for transfers between devices  26.6 us (19%)
  Pallas kernels  23.2 us (17%)
  local copies, waits for them, and re-layouts  9.12 us (7%)
  other arithmetic  2.58 us (2%)
  between operations  1.52 us (1%)
    all_to_all x1, blocking collectives, body(): g = lax.all_to_all(g.reshape(64, 8, DIM), ('z', 'y'), 0, 0)  29.8 us
    ppermute x10, starting transfers between devices, fetch(): return lax.ppermute(value, AXES, pairs_to(move))  28.5 us
    ppermute x10, waiting for transfers between devices, fetch(): return lax.ppermute(value, AXES, pairs_to(move))  16 us
    pallas_call x4, Pallas kernels, cells(): pl.pallas_call(functools.partial(cells_kernel, which, r_in is not None, g...  11.5 us
    all_to_all x1, starting transfers between devices, body(): s_own = lax.all_to_all(pack, 'z', 0, 0)  10.3 us
    pallas_call x1, Pallas kernels, prepare(): pl.pallas_call(prepare_kernel, grid_spec=pltpu.PrefetchScalarGridSpec(num...  9.94 us
    unnamed x23, local copies, waits for them, and re-layouts  8.2 us
    all_to_all x1, waiting for transfers between devices, body(): lax.all_to_all(jnp.broadcast_to(g[None], (32, 8, DIM)), ('core', 'xlo', '...  7.3 us
  transfers between devices with their start and end apart: 12, of which 7 were waited for; matrix products, arithmetic and copies ran while one was open for 1% of the time, Pallas kernels for 16%

profile of v3, /device:TPU:6, one launch (start us, length us, event | category | flops | bytes accessed | tf_op | source)
XLA Modules:
  0.0 136.8 jit_solution(4297854940276394193)
XLA Ops:
  1.3 1.8 %shard_map.77 = f32[8,72,256]{2,1,0:T(8,128)} custom-call(f32[256,256]{1,0:T(8,128)} %embed.1, s32[1,256]{1,0:T(1,128)} %bitcast.14), custom_call_target="tpu_custom_call" | custom-call | tf_op jit(solution)/shard_map/pallas_call | solution.py:88
  3.9 1.0 pad_maximum_fusion.rb_own
  4.9 1.9 %collective-permute-start = (s32[256,4096]{1,0:T(8,128)}, s32[256,4096]{1,0:T(8,128)}, u32[]{:S(2)}, u32[]{:S(2)}) collective-permute-start(s32[256,4096]{1,0:T(8,128)} %c_own), channel_id=1, source_target_pairs={{16,0},{17,1},{18,2},{19,3},{20,4},{21,5},{22,6},{23,7},{24,8},{25... | collective-permute-start | bytes 12582920 | tf_op jit(solution)/shard_map/ppermute | solution.py:56
  6.8 10.3 %all-to-all-start = ((f32[8,72,256]{2,1,0:T(8,128)}), f32[8,72,256]{2,1,0:T(8,128)S(1)}, u32[]{:S(2)}, u32[]{:S(2)}) async-start(f32[8,72,256]{2,1,0:T(8,128)} %shard_map.77), calls=%async_computation | async-start | bytes 1179648 | tf_op jit(solution)/shard_map/all_to_all | solution.py:235
  17.1 2.1 %collective-permute-start.1 = (f32[256,384]{1,0:T(8,128)S(1)}, f32[256,384]{1,0:T(8,128)S(1)}, u32[]{:S(2)}, u32[]{:S(2)}) collective-permute-start(f32[256,384]{1,0:T(8,128)S(1)} %pad_maximum_fusion.rb_own), channel_id=1, source_target_pairs={{16,0},{17,1},{18,2},{19,3},{20,4},{21,5},{22,6},{23,7},{24,8},{25... | collective-permute-start | bytes 1179656 | tf_op jit(solution)/shard_map/ppermute | solution.py:56
  19.4 1.4 %collective-permute-done.1.rb_oth = f32[256,384]{1,0:T(8,128)S(1)} collective-permute-done((f32[256,384]{1,0:T(8,128)S(1)}, f32[256,384]{1,0:T(8,128)S(1)}, u32[]{:S(2)}, u32[]{:S(2)}) %collective-permute-start.1) | collective-permute-done | bytes 393248 | tf_op jit(solution)/shard_map/ppermute | solution.py:56
  20.7 9.9 %shard_map.78 = (f32[512,512]{1,0:T(8,128)S(1)}, f32[512,512]{1,0:T(8,128)S(1)}, f32[512,512]{1,0:T(8,128)S(1)}, f32[512,512]{1,0:T(8,128)}, f32[512,512]{1,0:T(...) custom-call(s32[12]{0:T(128)S(1)} %stack.36.table, ...), custom_call_target="tpu_custom_call" | custom-call | flops 4000000000 | bytes 8388608 | tf_op jit(solution)/shard_map/pallas_call | solution.py:146
  30.7 1.0 copy-done.4
  33.4 3.3 %all-to-all-done.pack = f32[8,72,256]{2,1,0:T(8,128)S(1)} async-done(((f32[8,72,256]{2,1,0:T(8,128)}), f32[8,72,256]{2,1,0:T(8,128)S(1)}, u32[]{:S(2)}, u32[]{:S(2)}) %all-to-all-start) | async-done | bytes 589856 | tf_op jit(solution)/shard_map/all_to_all | solution.py:235
  36.7 2.7 %collective-permute-start.2 = (f32[8,72,256]{2,1,0:T(8,128)S(1)}, f32[8,72,256]{2,1,0:T(8,128)S(1)}, u32[]{:S(2)}, u32[]{:S(2)}) collective-permute-start(f32[8,72,256]{2,1,0:T(8,128)S(1)} %all-to-all-done.pack), channel_id=1, source_target_pairs={{256,0},{257,1},{258,2},{259,3},{260,4},{261,5},{262,6},{263,7},{2... | collective-permute-start | bytes 1769480 | tf_op jit(solution)/shard_map/ppermute | solution.py:56
  39.5 3.0 %collective-permute-start.4 = (f32[8,72,256]{2,1,0:T(8,128)S(1)}, f32[8,72,256]{2,1,0:T(8,128)S(1)}, u32[]{:S(2)}, u32[]{:S(2)}) collective-permute-start(f32[8,72,256]{2,1,0:T(8,128)S(1)} %all-to-all-done.pack), channel_id=1, source_target_pairs={{257,0},{256,1},{259,2},{258,3},{261,4},{260,5},{263,6},{262,7},{2... | collective-permute-start | bytes 1769480 | tf_op jit(solution)/shard_map/ppermute | solution.py:56
  42.5 1.2 copy-done.5
  43.8 1.2 copy-done.6
  45.0 1.1 copy-done.8
  46.1 1.1 copy-done.10
  47.2 2.9 %shard_map.79 = (f32[512,256]{1,0:T(8,128)S(1)}, f32[8,64,256]{2,1,0:T(8,128)S(1)}) custom-call(s32[12]{0:T(128)S(1)} %stack.36.table, f32[512,512]{1,0:T(8,128)S(1)} %copy-done.5, f32[512,512]{1,0:T(8,128)S(1)} %copy-done.6, bf16[512,768]{1,0:T(8,128)(2,1)S(1)} %copy-done.8, bf16[256,1536]{1,0:T(8,128)(2,1)S(1)} %copy-done.10, ...), custom_call_target="tpu_custom_call" | custom-call | flops 3000000000 | bytes 4194304 | tf_op jit(solution)/shard_map/pallas_call | solution.py:210
  50.1 4.0 %collective-permute-start.5 = (f32[8,64,256]{2,1,0:T(8,128)S(1)}, f32[8,64,256]{2,1,0:T(8,128)S(1)}, u32[]{:S(2)}, u32[]{:S(2)}) collective-permute-start(f32[8,64,256]{2,1,0:T(8,128)S(1)} %get-tuple-element.44), channel_id=1, source_target_pairs={{257,0},{256,1},{259,2},{258,3},{261,4},{260,5},{263,6},{262,7},{2... | collective-permute-start | bytes 1572872 | tf_op jit(solution)/shard_map/ppermute | solution.py:56
  54.1 3.1 %collective-permute-start.3 = (f32[8,72,256]{2,1,0:T(8,128)S(1)}, f32[8,72,256]{2,1,0:T(8,128)S(1)}, u32[]{:S(2)}, u32[]{:S(2)}) collective-permute-start(f32[8,72,256]{2,1,0:T(8,128)S(1)} %collective-permute-done.2.pack), channel_id=1, source_target_pairs={{257,0},{256,1},{259,2},{258,3},{261,4},{260,5},{263,6},{262,7},{2... | collective-permute-start | bytes 1769480 | tf_op jit(solution)/shard_map/ppermute | solution.py:56
  57.2 2.9 %shard_map.80 = (f32[512,256]{1,0:T(8,128)S(1)}, f32[8,64,256]{2,1,0:T(8,128)S(1)}) custom-call(s32[12]{0:T(128)S(1)} %stack.36.table, f32[512,512]{1,0:T(8,128)S(1)} %get-tuple-element.38.weight, f32[512,512]{1,0:T(8,128)S(1)} %copy-done.3, bf16[512,768]{1,0:T(8,128)(2,1)S(1)} %copy-done.8, bf16[256,1536]{1,0:T(8,128)(2,1)S(1)} %copy-done.10, ...), custom_call_target="tpu_custom_call" | custom-call | flops 3000000000 | bytes 4194304 | tf_op jit(solution)/shard_map/pallas_call | solution.py:210
  60.1 2.3 %collective-permute-done.5.rest_1_ = f32[8,64,256]{2,1,0:T(8,128)S(1)} collective-permute-done((f32[8,64,256]{2,1,0:T(8,128)S(1)}, f32[8,64,256]{2,1,0:T(8,128)S(1)}, u32[]{:S(2)}, u32[]{:S(2)}) %collective-permute-start.5) | collective-permute-done | bytes 524320 | tf_op jit(solution)/shard_map/ppermute | solution.py:56
  62.4 2.9 %shard_map.81 = (f32[512,256]{1,0:T(8,128)S(1)}, f32[8,64,256]{2,1,0:T(8,128)S(1)}) custom-call(s32[12]{0:T(128)S(1)} %stack.36.table, f32[512,512]{1,0:T(8,128)S(1)} %get-tuple-element.36.weight, f32[512,512]{1,0:T(8,128)S(1)} %copy-done.2, bf16[512,768]{1,0:T(8,128)(2,1)S(1)} %copy-done.8, bf16[256,1536]{1,0:T(8,128)(2,1)S(1)} %copy-done.10, ...), custom_call_target="tpu_custom_call" | custom-call | flops 3000000000 | bytes 4194304 | tf_op jit(solution)/shard_map/pallas_call | solution.py:210
  65.3 1.9 %collective-permute-start.8 = (f32[8,64,256]{2,1,0:T(8,128)S(1)}, f32[8,64,256]{2,1,0:T(8,128)S(1)}, u32[]{:S(2)}, u32[]{:S(2)}) collective-permute-start(f32[8,64,256]{2,1,0:T(8,128)S(1)} %get-tuple-element.49), channel_id=1, source_target_pairs={{256,0},{257,1},{258,2},{259,3},{260,4},{261,5},{262,6},{263,7},{2... | collective-permute-start | bytes 1572872 | tf_op jit(solution)/shard_map/ppermute | solution.py:56
  67.2 4.0 %collective-permute-start.7 = (f32[8,64,256]{2,1,0:T(8,128)S(1)}, f32[8,64,256]{2,1,0:T(8,128)S(1)}, u32[]{:S(2)}, u32[]{:S(2)}) collective-permute-start(f32[8,64,256]{2,1,0:T(8,128)S(1)} %get-tuple-element.48), channel_id=1, source_target_pairs={{257,0},{256,1},{259,2},{258,3},{261,4},{260,5},{263,6},{262,7},{2... | collective-permute-start | bytes 1572872 | tf_op jit(solution)/shard_map/ppermute | solution.py:56
  71.3 2.9 %shard_map.82 = (f32[512,256]{1,0:T(8,128)S(1)}, f32[8,64,256]{2,1,0:T(8,128)S(1)}) custom-call(s32[12]{0:T(128)S(1)} %stack.36.table, f32[512,512]{1,0:T(8,128)S(1)} %copy-done, f32[512,512]{1,0:T(8,128)S(1)} %copy-done.1, bf16[512,768]{1,0:T(8,128)(2,1)S(1)} %copy-done.8, bf16[256,1536]{1,0:T(8,128)(2,1)S(1)} %copy-done.10, ...), custom_call_target="tpu_custom_call" | custom-call | flops 3000000000 | bytes 4194304 | tf_op jit(solution)/shard_map/pallas_call | solution.py:210
  74.1 7.5 %collective-permute-done.8 = f32[8,64,256]{2,1,0:T(8,128)S(1)} collective-permute-done((f32[8,64,256]{2,1,0:T(8,128)S(1)}, f32[8,64,256]{2,1,0:T(8,128)S(1)}, u32[]{:S(2)}, u32[]{:S(2)}) %collective-permute-start.8) | collective-permute-done | bytes 524320 | tf_op jit(solution)/shard_map/ppermute | solution.py:56
  81.7 29.8 %all_to_all.15 = f32[64,8,256]{2,1,0:T(8,128)S(1)} all-to-all(f32[64,8,256]{2,1,0:T(8,128)S(1)} %bitcast.12), channel_id=1, replica_groups=mesh['xlo'=2,'y'=8,'core'=2,'z'=8,'xhi'=2] {'z','y'}, dimensions={0} | all-to-all | bytes 1048576 | tf_op jit(solution)/shard_map/all_to_all | solution.py:256
  111.6 3.6 %collective-permute-start.9 = (f32[8,256]{1,0:T(8,128)S(1)}, f32[8,256]{1,0:T(8,128)S(1)}, u32[]{:S(2)}, u32[]{:S(2)}) collective-permute-start(f32[8,256]{1,0:T(8,128)S(1)} %broadcast_multiply_fusion), channel_id=1, source_target_pairs={{1,0},{0,1},{3,2},{2,3},{5,4},{4,5},{7,6},{6,7},{9,8},{8,9},{11,10... | collective-permute-start | bytes 24584 | tf_op jit(solution)/shard_map/ppermute | solution.py:56
  115.2 3.4 %collective-permute-done.9 = f32[8,256]{1,0:T(8,128)S(1)} collective-permute-done((f32[8,256]{1,0:T(8,128)S(1)}, f32[8,256]{1,0:T(8,128)S(1)}, u32[]{:S(2)}, u32[]{:S(2)}) %collective-permute-start.9) | collective-permute-done | bytes 8224 | tf_op jit(solution)/shard_map/ppermute | solution.py:56
  119.4 5.2 %all-to-all-start.2 = ((f32[32,8,256]{2,1,0:T(8,128)}), f32[32,8,256]{2,1,0:T(8,128)S(1)}, u32[]{:S(2)}, u32[]{:S(2)}) async-start(f32[32,8,256]{2,1,0:T(8,128)} %broadcast_in_dim.5), calls=%async_computation.2 | async-start | bytes 524288 | tf_op jit(solution)/shard_map/all_to_all | solution.py:260
  124.7 2.1 %collective-permute-start.6 = (f32[256,256]{1,0:T(8,128)S(1)}, f32[256,256]{1,0:T(8,128)S(1)}, u32[]{:S(2)}, u32[]{:S(2)}) collective-permute-start(f32[256,256]{1,0:T(8,128)S(1)} %slice.7), channel_id=1, source_target_pairs={{16,0},{17,1},{18,2},{19,3},{20,4},{21,5},{22,6},{23,7},{24,8},{25... | collective-permute-start | bytes 786440 | tf_op jit(solution)/shard_map/ppermute | solution.py:56
  126.7 1.4 collective-permute-done.6
  128.8 7.3 %all-to-all-done.2 = f32[32,8,256]{2,1,0:T(8,128)S(1)} async-done(((f32[32,8,256]{2,1,0:T(8,128)}), f32[32,8,256]{2,1,0:T(8,128)S(1)}, u32[]{:S(2)}, u32[]{:S(2)}) %all-to-all-start.2) | async-done | bytes 262176 | tf_op jit(solution)/shard_map/all_to_all | solution.py:260
  (32 shorter events, 5.0 us)
Async XLA Ops:
  4.9 15.9 %collective-permute-start = (s32[256,4096]{1,0:T(8,128)}, s32[256,4096]{1,0:T(8,128)}, u32[]{:S(2)}, u32[]{:S(2)}) collective-permute-start(s32[256,4096]{1,0:T(8,128)} %c_own), channel_id=1, source_target_pairs={{16,0},{17,1},{18,2},{19,3},{20,4},{21,5},{22,6},{23,7},{24,8},{25... | collective-permute-start | bytes 12582920 | tf_op jit(solution)/shard_map/ppermute | solution.py:56
  6.8 29.9 %all-to-all-start = ((f32[8,72,256]{2,1,0:T(8,128)}), f32[8,72,256]{2,1,0:T(8,128)S(1)}, u32[]{:S(2)}, u32[]{:S(2)}) async-start(f32[8,72,256]{2,1,0:T(8,128)} %shard_map.77), calls=%async_computation | async-start | bytes 1179648 | tf_op jit(solution)/shard_map/all_to_all | solution.py:235
  17.1 3.6 %collective-permute-start.1 = (f32[256,384]{1,0:T(8,128)S(1)}, f32[256,384]{1,0:T(8,128)S(1)}, u32[]{:S(2)}, u32[]{:S(2)}) collective-permute-start(f32[256,384]{1,0:T(8,128)S(1)} %pad_maximum_fusion.rb_own), channel_id=1, source_target_pairs={{16,0},{17,1},{18,2},{19,3},{20,4},{21,5},{22,6},{23,7},{24,8},{25... | collective-permute-start | bytes 1179656 | tf_op jit(solution)/shard_map/ppermute | solution.py:56
  30.7 1.0 copy-start.4
  31.7 0.9 copy-start.7
  32.6 0.9 copy-start.9
  36.7 17.4 %collective-permute-start.2 = (f32[8,72,256]{2,1,0:T(8,128)S(1)}, f32[8,72,256]{2,1,0:T(8,128)S(1)}, u32[]{:S(2)}, u32[]{:S(2)}) collective-permute-start(f32[8,72,256]{2,1,0:T(8,128)S(1)} %all-to-all-done.pack), channel_id=1, source_target_pairs={{256,0},{257,1},{258,2},{259,3},{260,4},{261,5},{262,6},{263,7},{2... | collective-permute-start | bytes 1769480 | tf_op jit(solution)/shard_map/ppermute | solution.py:56
  39.5 22.9 %collective-permute-start.4 = (f32[8,72,256]{2,1,0:T(8,128)S(1)}, f32[8,72,256]{2,1,0:T(8,128)S(1)}, u32[]{:S(2)}, u32[]{:S(2)}) collective-permute-start(f32[8,72,256]{2,1,0:T(8,128)S(1)} %all-to-all-done.pack), channel_id=1, source_target_pairs={{257,0},{256,1},{259,2},{258,3},{261,4},{260,5},{263,6},{262,7},{2... | collective-permute-start | bytes 1769480 | tf_op jit(solution)/shard_map/ppermute | solution.py:56
  42.5 1.2 copy-start.5
  43.7 1.2 copy-start.6
  45.0 1.1 copy-start.8
  46.1 1.1 copy-start.10
  47.2 9.9 %copy-start.3 = (f32[512,512]{1,0:T(8,128)S(1)}, f32[512,512]{1,0:T(8,128)}, u32[]{:S(2)}) copy-start(f32[512,512]{1,0:T(8,128)} %get-tuple-element.39.shift) | copy-start | bytes 3145732
  50.1 12.3 %collective-permute-start.5 = (f32[8,64,256]{2,1,0:T(8,128)S(1)}, f32[8,64,256]{2,1,0:T(8,128)S(1)}, u32[]{:S(2)}, u32[]{:S(2)}) collective-permute-start(f32[8,64,256]{2,1,0:T(8,128)S(1)} %get-tuple-element.44), channel_id=1, source_target_pairs={{257,0},{256,1},{259,2},{258,3},{261,4},{260,5},{263,6},{262,7},{2... | collective-permute-start | bytes 1572872 | tf_op jit(solution)/shard_map/ppermute | solution.py:56
  54.1 17.1 %collective-permute-start.3 = (f32[8,72,256]{2,1,0:T(8,128)S(1)}, f32[8,72,256]{2,1,0:T(8,128)S(1)}, u32[]{:S(2)}, u32[]{:S(2)}) collective-permute-start(f32[8,72,256]{2,1,0:T(8,128)S(1)} %collective-permute-done.2.pack), channel_id=1, source_target_pairs={{257,0},{256,1},{259,2},{258,3},{261,4},{260,5},{263,6},{262,7},{2... | collective-permute-start | bytes 1769480 | tf_op jit(solution)/shard_map/ppermute | solution.py:56
  57.2 5.2 %copy-start.2 = (f32[512,512]{1,0:T(8,128)S(1)}, f32[512,512]{1,0:T(8,128)}, u32[]{:S(2)}) copy-start(f32[512,512]{1,0:T(8,128)} %get-tuple-element.37.shift) | copy-start | bytes 3145732
  62.4 8.8 %copy-start = (f32[512,512]{1,0:T(8,128)S(1)}, f32[512,512]{1,0:T(8,128)}, u32[]{:S(2)}) copy-start(f32[512,512]{1,0:T(8,128)} %get-tuple-element.29.weight) | copy-start | bytes 3145732
  62.4 8.9 %copy-start.1 = (f32[512,512]{1,0:T(8,128)S(1)}, f32[512,512]{1,0:T(8,128)}, u32[]{:S(2)}) copy-start(f32[512,512]{1,0:T(8,128)} %get-tuple-element.30.shift) | copy-start | bytes 3145732
  65.3 16.3 %collective-permute-start.8 = (f32[8,64,256]{2,1,0:T(8,128)S(1)}, f32[8,64,256]{2,1,0:T(8,128)S(1)}, u32[]{:S(2)}, u32[]{:S(2)}) collective-permute-start(f32[8,64,256]{2,1,0:T(8,128)S(1)} %get-tuple-element.49), channel_id=1, source_target_pairs={{256,0},{257,1},{258,2},{259,3},{260,4},{261,5},{262,6},{263,7},{2... | collective-permute-start | bytes 1572872 | tf_op jit(solution)/shard_map/ppermute | solution.py:56
  67.2 14.4 %collective-permute-start.7 = (f32[8,64,256]{2,1,0:T(8,128)S(1)}, f32[8,64,256]{2,1,0:T(8,128)S(1)}, u32[]{:S(2)}, u32[]{:S(2)}) collective-permute-start(f32[8,64,256]{2,1,0:T(8,128)S(1)} %get-tuple-element.48), channel_id=1, source_target_pairs={{257,0},{256,1},{259,2},{258,3},{261,4},{260,5},{263,6},{262,7},{2... | collective-permute-start | bytes 1572872 | tf_op jit(solution)/shard_map/ppermute | solution.py:56
  111.6 7.0 %collective-permute-start.9 = (f32[8,256]{1,0:T(8,128)S(1)}, f32[8,256]{1,0:T(8,128)S(1)}, u32[]{:S(2)}, u32[]{:S(2)}) collective-permute-start(f32[8,256]{1,0:T(8,128)S(1)} %broadcast_multiply_fusion), channel_id=1, source_target_pairs={{1,0},{0,1},{3,2},{2,3},{5,4},{4,5},{7,6},{6,7},{9,8},{8,9},{11,10... | collective-permute-start | bytes 24584 | tf_op jit(solution)/shard_map/ppermute | solution.py:56
  119.4 16.7 %all-to-all-start.2 = ((f32[32,8,256]{2,1,0:T(8,128)}), f32[32,8,256]{2,1,0:T(8,128)S(1)}, u32[]{:S(2)}, u32[]{:S(2)}) async-start(f32[32,8,256]{2,1,0:T(8,128)} %broadcast_in_dim.5), calls=%async_computation.2 | async-start | bytes 524288 | tf_op jit(solution)/shard_map/all_to_all | solution.py:260
  124.7 3.4 %collective-permute-start.6 = (f32[256,256]{1,0:T(8,128)S(1)}, f32[256,256]{1,0:T(8,128)S(1)}, u32[]{:S(2)}, u32[]{:S(2)}) collective-permute-start(f32[256,256]{1,0:T(8,128)S(1)} %slice.7), channel_id=1, source_target_pairs={{16,0},{17,1},{18,2},{19,3},{20,4},{21,5},{22,6},{23,7},{24,8},{25... | collective-permute-start | bytes 786440 | tf_op jit(solution)/shard_map/ppermute | solution.py:56

commit v4 on v3

--- a/solution.py
+++ b/solution.py
@@ -93,7 +93,7 @@
 
 
 def prepare_kernel(table, c_own, c_oth, rb_own, rb_oth, *outs):
-    weight_out, shift_out, tall_out, wide_out = outs[:4], outs[4:8], outs[8], outs[9]
+    count_out, (rh, rl, th, tl, base) = outs[:4], outs[4:]
     step = pl.program_id(0)
     steps = pl.num_programs(0)
 
@@ -102,15 +102,12 @@
         for k, rb in enumerate((rb_own, rb_oth)):
             part = slice(k * ROWS, (k + 1) * ROWS)
             value = rb[:, :DIM]
-            tall_out[part, :] = left(split(value), 1)
-            wide = split(value.T)
-            for n, source in enumerate((wide[0], wide[0], wide[1])):
-                start = n * 2 * ROWS + k * ROWS
-                wide_out[:, start : start + ROWS] = source
-
-    def work(counts, rb, block):
+            rh[part, :], rl[part, :] = split(value)
+            th[:, part], tl[:, part] = split(value.T)
+            base[part, :] = rb[:, DIM:]
+
+    def work(counts):
         half = lax.broadcasted_iota(jnp.int32, (STRIP, 128), 1) < SLICE
-        base = rb[pl.ds(pl.multiple_of(block * STRIP, STRIP), STRIP), DIM:]
         for which in range(4):
             core, xhi, xlo = (table[which * 3 + i] for i in range(3))
             near, far = xlo * SLICE, (1 - xlo) * SLICE
@@ -120,18 +117,15 @@
                     for z in (2 * n, 2 * n + 1)
                 ]
                 cnt = jnp.where(half, pltpu.roll(tiles[0], near, 1), pltpu.roll(tiles[1], far, 1))
-                x = jnp.maximum(cnt, 1).astype(jnp.float32)
-                weight = jnp.where(cnt > 0, 0.1 + 0.25 * (x * lax.rsqrt(x)), 0.0)
-                weight_out[which][:, n * 128 : (n + 1) * 128] = weight
-                shift_out[which][:, n * 128 : (n + 1) * 128] = jnp.log(x) + base
+                count_out[which][:, n * 128 : (n + 1) * 128] = cnt.astype(jnp.float32)
 
     @pl.when(step < steps // 2)
     def _():
-        work(c_own, rb_own, step)
+        work(c_own)
 
     @pl.when(step >= steps // 2)
     def _():
-        work(c_oth, rb_oth, step - steps // 2)
+        work(c_oth)
 
 
 def prepare(table, counts, rb):
@@ -141,9 +135,9 @@
         return pl.BlockSpec(shape, lambda i, w: (0, 0))
 
     columns = counts[0].shape[1]
-    cell_spec = pl.BlockSpec((STRIP, 2 * DIM), lambda i, w: (i, 0))
-    cell_shape = jax.ShapeDtypeStruct((2 * ROWS, 2 * DIM), jnp.float32)
-    *cell, tall, wide = pl.pallas_call(
+    tall, wide, base = (2 * ROWS, DIM), (DIM, 2 * ROWS), (2 * ROWS, 128)
+    bf16 = jnp.bfloat16
+    outs = pl.pallas_call(
         prepare_kernel,
         grid_spec=pltpu.PrefetchScalarGridSpec(
             num_scalar_prefetch=1,
@@ -153,20 +147,22 @@
                 pl.BlockSpec((STRIP, columns), lambda i, w: (jnp.maximum(i - half, 0), 0)),
             ]
             + [whole((ROWS, DIM + 128))] * 2,
-            out_specs=[cell_spec] * 8 + [whole((2 * ROWS, 3 * DIM)), whole((DIM, 6 * ROWS))],
+            out_specs=[pl.BlockSpec((STRIP, 2 * DIM), lambda i, w: (i, 0))] * 4
+            + [whole(tall)] * 2
+            + [whole(wide)] * 2
+            + [whole(base)],
         ),
-        out_shape=[cell_shape] * 8
-        + [
-            jax.ShapeDtypeStruct((2 * ROWS, 3 * DIM), jnp.bfloat16),
-            jax.ShapeDtypeStruct((DIM, 6 * ROWS), jnp.bfloat16),
-        ],
+        out_shape=[jax.ShapeDtypeStruct((2 * ROWS, 2 * DIM), jnp.float32)] * 4
+        + [jax.ShapeDtypeStruct(tall, bf16)] * 2
+        + [jax.ShapeDtypeStruct(wide, bf16)] * 2
+        + [jax.ShapeDtypeStruct(base, jnp.float32)],
         compiler_params=pltpu.CompilerParams(vmem_limit_bytes=48 * 2**20),
-        cost_estimate=pl.CostEstimate(flops=4 * 10**9, bytes_accessed=2**23, transcendentals=2**20),
+        cost_estimate=pl.CostEstimate(flops=2**22, bytes_accessed=2**21, transcendentals=0),
     )(table, *counts, *rb)
-    return cell[:4], cell[4:], tall, wide
-
-
-def cells_kernel(which, adds_r, adds_g, table, weight, shift, tall, wide, pack, *rest):
+    return outs[:4], outs[4:]
+
+
+def cells_kernel(which, adds_r, adds_g, table, count, rh, rl, th, tl, base, pack, *rest):
     rest = list(rest)
     r_in = rest.pop(0) if adds_r else None
     g_in = rest.pop(0) if adds_g else None
@@ -174,6 +170,7 @@
     offset = (2 * table[3 * which] + table[3 * which + 2]) * SLICE
     near, far = lax.rem(DIM - offset, DIM), lax.rem(DIM + SLICE - offset, DIM)
     half = lax.broadcasted_iota(jnp.int32, (1, 128), 1) < SLICE
+    tall, wide = left((rh[...], rl[...]), 1), left((th[...], tl[...]), 1)
     r_sum = None
     for j in range(8 // GROUP):
         part = slice(j * DIM, (j + 1) * DIM)
@@ -191,12 +188,18 @@
             ],
             axis=1,
         )
-        gap = dot(tall[...], right(e, 1), ((1,), (1,))) + log_col - shift[:, part]
-        w = weight[:, part]
-        cell = split(jnp.where(w > 0.0, w * gap, 0.5 + 0.5 * jnp.tanh(0.5 * gap)))
+        gap = dot(tall, right(e, 1), ((1,), (1,))) + log_col - base[:, :1]
+        cnt = count[:, part]
+        x = jnp.maximum(cnt, 1.0)
+        cell = jnp.where(
+            cnt > 0.0,
+            (0.1 + 0.25 * (x * lax.rsqrt(x))) * (gap - jnp.log(x)),
+            0.5 + 0.5 * jnp.tanh(0.5 * gap),
+        )
+        cell = split(cell)
         r_term = dot(left(cell, 1), right(e, 0), ((1,), (0,)))
         r_sum = r_term if r_sum is None else r_sum + r_term
-        total = dot(wide[...], right(cell, 0), ((1,), (0,))).T.reshape(GROUP, SLICE, DIM)
+        total = dot(wide, right(cell, 0), ((1,), (0,))).T.reshape(GROUP, SLICE, DIM)
         if adds_g:
             total += g_in[j * GROUP : (j + 1) * GROUP]
         g_out[j * GROUP : (j + 1) * GROUP] = total
@@ -205,8 +208,8 @@
 
 def cells(which, table, prepared, pack, r_in=None, g_in=None):
     vmem = pl.BlockSpec(memory_space=pltpu.VMEM)
-    weights, shifts, tall, wide = prepared
-    args = [weights[which], shifts[which], tall, wide, pack] + [a for a in (r_in, g_in) if a is not None]
+    counts, rows = prepared
+    args = [counts[which], *rows, pack] + [a for a in (r_in, g_in) if a is not None]
     return pl.pallas_call(
         functools.partial(cells_kernel, which, r_in is not None, g_in is not None),
         in_specs=[pl.BlockSpec(memory_space=pltpu.SMEM)] + [vmem] * len(args),
@@ -217,7 +220,7 @@
         ],
         compiler_params=pltpu.CompilerParams(vmem_limit_bytes=32 * 2**20),
         cost_estimate=pl.CostEstimate(
-            flops=3 * 10**9, bytes_accessed=2**22, transcendentals=2**18
+            flops=4 * 10**9, bytes_accessed=4 * 2**20, transcendentals=2**20
         ),
     )(table, *args)
 
@@ -231,16 +234,13 @@
         + [core, 1 - xhi, xlo]
     ).astype(jnp.int32)
 
-    pack, row_marg = lax.optimization_barrier((pack_slice(col_embed, col_marg), row_marg))
-    s_own = lax.all_to_all(pack, "z", 0, 0)
-
+    s_own = lax.all_to_all(pack_slice(col_embed, col_marg), "z", 0, 0)
     base_row = log_total[0] - jnp.log(row_marg.astype(jnp.float32))
     rb = jnp.concatenate([row_embed, jnp.broadcast_to(base_row[:, None], (ROWS, 128))], axis=1)
-    rb, counts = lax.optimization_barrier((rb, counts))
-    prepared = prepare(table, (counts, fetch(counts, core_swap)), (rb, fetch(rb, core_swap)))
-    weights, shifts, tall, wide = prepared
-    s_own, tall = lax.optimization_barrier((s_own, tall))
-    prepared = (weights, shifts, tall, wide)
+    s_own, rb, rb_oth, counts_oth = lax.optimization_barrier(
+        (s_own, rb, fetch(rb, core_swap), fetch(counts, core_swap))
+    )
+    prepared = prepare(table, (counts, counts_oth), (rb, rb_oth))
 
     s_a, s_b = fetch(s_own, side_a), fetch(s_own, side_b)
     r, g_own = cells(0, table, prepared, s_own)

time: 139 us -> 137 us (0.986)
  waiting for transfers between devices: 26.6 us -> 35.1 us
  local copies, waits for them, and re-layouts: 9.12 us -> 1.63 us
  blocking collectives: 29.8 us -> 27.9 us
    all_to_all x1, waiting for transfers between devices: 3.28 us -> 13.6 us  [body(): s_own = lax.all_to_all(pack_slice(col_embed, col_marg), 'z', 0, 0)]
    unnamed x23 -> x3, local copies, waits for them, and re-layouts: 8.2 us -> 0.71 us
    all_to_all x1, blocking collectives: 29.8 us -> 27.9 us  [body(): g = lax.all_to_all(g.reshape(64, 8, DIM), ('z', 'y'), 0, 0)]
    ppermute x10, waiting for transfers between devices: 16 us -> 14.2 us  [fetch(): return lax.ppermute(value, AXES, pairs_to(move))]
  transfers between devices with their start and end apart: 12 -> 12, of which waited for: 7 -> 6; matrix products, arithmetic and copies ran while one was open for 1% -> 2% of each run, Pallas kernels for 16% -> 17%
where the time goes in v4:
time: 137 us; the launch traced here: 135 us
  starting transfers between devices  43.3 us (32%)
  waiting for transfers between devices  35.1 us (26%)
  blocking collectives  27.9 us (20%)
  Pallas kernels  23 us (17%)
  other arithmetic  2.59 us (2%)
  local copies, waits for them, and re-layouts  1.63 us (1%)
  between operations  1.5 us (1%)
    all_to_all x1, blocking collectives, body(): g = lax.all_to_all(g.reshape(64, 8, DIM), ('z', 'y'), 0, 0)  27.9 us
    ppermute x10, starting transfers between devices, fetch(): return lax.ppermute(value, AXES, pairs_to(move))  27.8 us
    ppermute x10, waiting for transfers between devices, fetch(): return lax.ppermute(value, AXES, pairs_to(move))  14.2 us
    all_to_all x1, waiting for transfers between devices, body(): s_own = lax.all_to_all(pack_slice(col_embed, col_marg), 'z', 0, 0)  13.6 us
    pallas_call x4, Pallas kernels, cells(): pl.pallas_call(functools.partial(cells_kernel, which, r_in is not None, g...  12.2 us
    all_to_all x1, starting transfers between devices, body(): s_own = lax.all_to_all(pack_slice(col_embed, col_marg), 'z', 0, 0)  10.3 us
    pallas_call x1, Pallas kernels, prepare(): pl.pallas_call(prepare_kernel, grid_spec=pltpu.PrefetchScalarGridSpec(num...  8.94 us
    all_to_all x1, waiting for transfers between devices, body(): lax.all_to_all(jnp.broadcast_to(g[None], (32, 8, DIM)), ('core', 'xlo', '...  7.3 us
  transfers between devices with their start and end apart: 12, of which 6 were waited for; matrix products, arithmetic and copies ran while one was open for 2% of the time, Pallas kernels for 17%

profile of v4, /device:TPU:6, one launch (start us, length us, event | category | flops | bytes accessed | tf_op | source)
XLA Modules:
  0.0 135.1 jit_solution(9429927704100823047)
XLA Ops:
  0.6 1.9 %collective-permute-start.1 = (s32[256,4096]{1,0:T(8,128)}, s32[256,4096]{1,0:T(8,128)}, u32[]{:S(2)}, u32[]{:S(2)}) collective-permute-start(s32[256,4096]{1,0:T(8,128)} %c_own.1), channel_id=1, source_target_pairs={{16,0},{17,1},{18,2},{19,3},{20,4},{21,5},{22,6},{23,7},{24,8},{25... | collective-permute-start | bytes 12582920 | tf_op jit(solution)/shard_map/ppermute | solution.py:56
  2.6 1.8 %shard_map.77 = f32[8,72,256]{2,1,0:T(8,128)} custom-call(f32[256,256]{1,0:T(8,128)} %embed.1, s32[1,256]{1,0:T(1,128)} %bitcast.14), custom_call_target="tpu_custom_call" | custom-call | tf_op jit(solution)/shard_map/pallas_call | solution.py:88
  4.4 10.3 %all-to-all-start = ((f32[8,72,256]{2,1,0:T(8,128)}), f32[8,72,256]{2,1,0:T(8,128)S(1)}, u32[]{:S(2)}, u32[]{:S(2)}) async-start(f32[8,72,256]{2,1,0:T(8,128)} %shard_map.77), calls=%async_computation | async-start | bytes 1179648 | tf_op jit(solution)/shard_map/all_to_all | solution.py:237
  15.4 0.7 log_subtract_fusion
  16.0 0.1 broadcast_in_dim.4
  16.1 1.0 pad_maximum_fusion.rb_own
  17.1 2.1 %collective-permute-start = (f32[256,384]{1,0:T(8,128)S(1)}, f32[256,384]{1,0:T(8,128)S(1)}, u32[]{:S(2)}, u32[]{:S(2)}) collective-permute-start(f32[256,384]{1,0:T(8,128)S(1)} %pad_maximum_fusion.rb_own), channel_id=1, source_target_pairs={{16,0},{17,1},{18,2},{19,3},{20,4},{21,5},{22,6},{23,7},{24,8},{25... | collective-permute-start | bytes 1179656 | tf_op jit(solution)/shard_map/ppermute | solution.py:56
  19.3 1.5 %collective-permute-done.rb_oth = f32[256,384]{1,0:T(8,128)S(1)} collective-permute-done((f32[256,384]{1,0:T(8,128)S(1)}, f32[256,384]{1,0:T(8,128)S(1)}, u32[]{:S(2)}, u32[]{:S(2)}) %collective-permute-start) | collective-permute-done | bytes 393248 | tf_op jit(solution)/shard_map/ppermute | solution.py:56
  20.7 13.6 %all-to-all-done.pack = f32[8,72,256]{2,1,0:T(8,128)S(1)} async-done(((f32[8,72,256]{2,1,0:T(8,128)}), f32[8,72,256]{2,1,0:T(8,128)S(1)}, u32[]{:S(2)}, u32[]{:S(2)}) %all-to-all-start) | async-done | bytes 589856 | tf_op jit(solution)/shard_map/all_to_all | solution.py:237
  34.3 2.7 %collective-permute-start.2 = (f32[8,72,256]{2,1,0:T(8,128)S(1)}, f32[8,72,256]{2,1,0:T(8,128)S(1)}, u32[]{:S(2)}, u32[]{:S(2)}) collective-permute-start(f32[8,72,256]{2,1,0:T(8,128)S(1)} %all-to-all-done.pack), channel_id=1, source_target_pairs={{256,0},{257,1},{258,2},{259,3},{260,4},{261,5},{262,6},{263,7},{2... | collective-permute-start | bytes 1769480 | tf_op jit(solution)/shard_map/ppermute | solution.py:56
  37.1 3.0 %collective-permute-start.4 = (f32[8,72,256]{2,1,0:T(8,128)S(1)}, f32[8,72,256]{2,1,0:T(8,128)S(1)}, u32[]{:S(2)}, u32[]{:S(2)}) collective-permute-start(f32[8,72,256]{2,1,0:T(8,128)S(1)} %all-to-all-done.pack), channel_id=1, source_target_pairs={{257,0},{256,1},{259,2},{258,3},{261,4},{260,5},{263,6},{262,7},{2... | collective-permute-start | bytes 1769480 | tf_op jit(solution)/shard_map/ppermute | solution.py:56
  40.2 8.9 %shard_map.78 = (f32[512,512]{1,0:T(8,128)S(1)}, f32[512,512]{1,0:T(8,128)S(1)}, f32[512,512]{1,0:T(8,128)S(1)}, f32[512,512]{1,0:T(8,128)}, bf16[512,256]{1,0:T...) custom-call(s32[12]{0:T(128)S(1)} %stack.36.table, ...), custom_call_target="tpu_custom_call" | custom-call | flops 4194304 | bytes 2097152 | tf_op jit(solution)/shard_map/pallas_call | solution.py:140
  49.1 3.1 %shard_map.79 = (f32[512,256]{1,0:T(8,128)S(1)}, f32[8,64,256]{2,1,0:T(8,128)S(1)}) custom-call(s32[12]{0:T(128)S(1)} %stack.36.table, f32[512,512]{1,0:T(8,128)S(1)} %get-tuple-element.35.count, bf16[512,256]{1,0:T(8,128)(2,1)S(1)} %get-tuple-element.27.rh, bf16[512,256]{1,0:T(8,128)(2,1)S(1)} %get-tuple-element.28.rl, ...), custom_call_target="tpu_custom_call" | custom-call | flops 4000000000 | bytes 4194304 | tf_op jit(solution)/shard_map/pallas_call | solution.py:213
  52.2 4.0 %collective-permute-start.5 = (f32[8,64,256]{2,1,0:T(8,128)S(1)}, f32[8,64,256]{2,1,0:T(8,128)S(1)}, u32[]{:S(2)}, u32[]{:S(2)}) collective-permute-start(f32[8,64,256]{2,1,0:T(8,128)S(1)} %get-tuple-element.38), channel_id=1, source_target_pairs={{257,0},{256,1},{259,2},{258,3},{261,4},{260,5},{263,6},{262,7},{2... | collective-permute-start | bytes 1572872 | tf_op jit(solution)/shard_map/ppermute | solution.py:56
  56.2 3.0 %collective-permute-start.3 = (f32[8,72,256]{2,1,0:T(8,128)S(1)}, f32[8,72,256]{2,1,0:T(8,128)S(1)}, u32[]{:S(2)}, u32[]{:S(2)}) collective-permute-start(f32[8,72,256]{2,1,0:T(8,128)S(1)} %collective-permute-done.2.pack), channel_id=1, source_target_pairs={{257,0},{256,1},{259,2},{258,3},{261,4},{260,5},{263,6},{262,7},{2... | collective-permute-start | bytes 1769480 | tf_op jit(solution)/shard_map/ppermute | solution.py:56
  59.3 3.1 %shard_map.80 = (f32[512,256]{1,0:T(8,128)S(1)}, f32[8,64,256]{2,1,0:T(8,128)S(1)}) custom-call(s32[12]{0:T(128)S(1)} %stack.36.table, f32[512,512]{1,0:T(8,128)S(1)} %get-tuple-element.34.count, bf16[512,256]{1,0:T(8,128)(2,1)S(1)} %get-tuple-element.27.rh, bf16[512,256]{1,0:T(8,128)(2,1)S(1)} %get-tuple-element.28.rl, ...), custom_call_target="tpu_custom_call" | custom-call | flops 4000000000 | bytes 4194304 | tf_op jit(solution)/shard_map/pallas_call | solution.py:213
  62.4 4.0 %collective-permute-start.7 = (f32[8,64,256]{2,1,0:T(8,128)S(1)}, f32[8,64,256]{2,1,0:T(8,128)S(1)}, u32[]{:S(2)}, u32[]{:S(2)}) collective-permute-start(f32[8,64,256]{2,1,0:T(8,128)S(1)} %get-tuple-element.42), channel_id=1, source_target_pairs={{257,0},{256,1},{259,2},{258,3},{261,4},{260,5},{263,6},{262,7},{2... | collective-permute-start | bytes 1572872 | tf_op jit(solution)/shard_map/ppermute | solution.py:56
  66.4 3.1 %shard_map.81 = (f32[512,256]{1,0:T(8,128)S(1)}, f32[8,64,256]{2,1,0:T(8,128)S(1)}) custom-call(s32[12]{0:T(128)S(1)} %stack.36.table, f32[512,512]{1,0:T(8,128)S(1)} %get-tuple-element.33.count, bf16[512,256]{1,0:T(8,128)(2,1)S(1)} %get-tuple-element.27.rh, bf16[512,256]{1,0:T(8,128)(2,1)S(1)} %get-tuple-element.28.rl, ...), custom_call_target="tpu_custom_call" | custom-call | flops 4000000000 | bytes 4194304 | tf_op jit(solution)/shard_map/pallas_call | solution.py:213
  69.5 1.9 %collective-permute-start.8 = (f32[8,64,256]{2,1,0:T(8,128)S(1)}, f32[8,64,256]{2,1,0:T(8,128)S(1)}, u32[]{:S(2)}, u32[]{:S(2)}) collective-permute-start(f32[8,64,256]{2,1,0:T(8,128)S(1)} %get-tuple-element.43), channel_id=1, source_target_pairs={{256,0},{257,1},{258,2},{259,3},{260,4},{261,5},{262,6},{263,7},{2... | collective-permute-start | bytes 1572872 | tf_op jit(solution)/shard_map/ppermute | solution.py:56
  71.4 3.1 %shard_map.82 = (f32[512,256]{1,0:T(8,128)S(1)}, f32[8,64,256]{2,1,0:T(8,128)S(1)}) custom-call(s32[12]{0:T(128)S(1)} %stack.36.table, f32[512,512]{1,0:T(8,128)S(1)} %copy-done, bf16[512,256]{1,0:T(8,128)(2,1)S(1)} %get-tuple-element.27.rh, bf16[512,256]{1,0:T(8,128)(2,1)S(1)} %get-tuple-element.28.rl, bf16[256,512]{1,0:T(8,128)(2,1)S(1)} %get-tuple-element.29.th, ...), custom_call_target="tpu_custom_call" | custom-call | flops 4000000000 | bytes 4194304 | tf_op jit(solution)/shard_map/pallas_call | solution.py:213
  74.5 7.3 %collective-permute-done.7 = f32[8,64,256]{2,1,0:T(8,128)S(1)} collective-permute-done((f32[8,64,256]{2,1,0:T(8,128)S(1)}, f32[8,64,256]{2,1,0:T(8,128)S(1)}, u32[]{:S(2)}, u32[]{:S(2)}) %collective-permute-start.7) | collective-permute-done | bytes 524320 | tf_op jit(solution)/shard_map/ppermute | solution.py:56
  81.8 0.1 add_add_fusion
  81.9 27.9 %all_to_all.15 = f32[64,8,256]{2,1,0:T(8,128)S(1)} all-to-all(f32[64,8,256]{2,1,0:T(8,128)S(1)} %bitcast.12), channel_id=1, replica_groups=mesh['xlo'=2,'y'=8,'core'=2,'z'=8,'xhi'=2] {'z','y'}, dimensions={0} | all-to-all | bytes 1048576 | tf_op jit(solution)/shard_map/all_to_all | solution.py:256
  109.9 2.9 %collective-permute-start.9 = (f32[8,256]{1,0:T(8,128)S(1)}, f32[8,256]{1,0:T(8,128)S(1)}, u32[]{:S(2)}, u32[]{:S(2)}) collective-permute-start(f32[8,256]{1,0:T(8,128)S(1)} %broadcast_multiply_fusion), channel_id=1, source_target_pairs={{1,0},{0,1},{3,2},{2,3},{5,4},{4,5},{7,6},{6,7},{9,8},{8,9},{11,10... | collective-permute-start | bytes 24584 | tf_op jit(solution)/shard_map/ppermute | solution.py:56
  112.8 4.1 %collective-permute-done.9 = f32[8,256]{1,0:T(8,128)S(1)} collective-permute-done((f32[8,256]{1,0:T(8,128)S(1)}, f32[8,256]{1,0:T(8,128)S(1)}, u32[]{:S(2)}, u32[]{:S(2)}) %collective-permute-start.9) | collective-permute-done | bytes 8224 | tf_op jit(solution)/shard_map/ppermute | solution.py:56
  116.9 0.7 broadcast_in_dim.5
  117.7 5.2 %all-to-all-start.2 = ((f32[32,8,256]{2,1,0:T(8,128)}), f32[32,8,256]{2,1,0:T(8,128)S(1)}, u32[]{:S(2)}, u32[]{:S(2)}) async-start(f32[32,8,256]{2,1,0:T(8,128)} %broadcast_in_dim.5), calls=%async_computation.2 | async-start | bytes 524288 | tf_op jit(solution)/shard_map/all_to_all | solution.py:260
  122.9 2.1 %collective-permute-start.6 = (f32[256,256]{1,0:T(8,128)S(1)}, f32[256,256]{1,0:T(8,128)S(1)}, u32[]{:S(2)}, u32[]{:S(2)}) collective-permute-start(f32[256,256]{1,0:T(8,128)S(1)} %slice.7), channel_id=1, source_target_pairs={{16,0},{17,1},{18,2},{19,3},{20,4},{21,5},{22,6},{23,7},{24,8},{25... | collective-permute-start | bytes 786440 | tf_op jit(solution)/shard_map/ppermute | solution.py:56
  125.0 1.4 %collective-permute-done.6 = f32[256,256]{1,0:T(8,128)S(1)} collective-permute-done((f32[256,256]{1,0:T(8,128)S(1)}, f32[256,256]{1,0:T(8,128)S(1)}, u32[]{:S(2)}, u32[]{:S(2)}) %collective-permute-start.6) | collective-permute-done | bytes 262176 | tf_op jit(solution)/shard_map/ppermute | solution.py:56
  126.3 0.7 add_multiply_fusion
  127.1 7.3 %all-to-all-done.2 = f32[32,8,256]{2,1,0:T(8,128)S(1)} async-done(((f32[32,8,256]{2,1,0:T(8,128)}), f32[32,8,256]{2,1,0:T(8,128)S(1)}, u32[]{:S(2)}, u32[]{:S(2)}) %all-to-all-start.2) | async-done | bytes 262176 | tf_op jit(solution)/shard_map/all_to_all | solution.py:260
  134.4 0.7 copy.10
  (12 shorter events, 0.2 us)
Async XLA Ops:
  0.6 33.7 %collective-permute-start.1 = (s32[256,4096]{1,0:T(8,128)}, s32[256,4096]{1,0:T(8,128)}, u32[]{:S(2)}, u32[]{:S(2)}) collective-permute-start(s32[256,4096]{1,0:T(8,128)} %c_own.1), channel_id=1, source_target_pairs={{16,0},{17,1},{18,2},{19,3},{20,4},{21,5},{22,6},{23,7},{24,8},{25... | collective-permute-start | bytes 12582920 | tf_op jit(solution)/shard_map/ppermute | solution.py:56
  4.4 29.9 %all-to-all-start = ((f32[8,72,256]{2,1,0:T(8,128)}), f32[8,72,256]{2,1,0:T(8,128)S(1)}, u32[]{:S(2)}, u32[]{:S(2)}) async-start(f32[8,72,256]{2,1,0:T(8,128)} %shard_map.77), calls=%async_computation | async-start | bytes 1179648 | tf_op jit(solution)/shard_map/all_to_all | solution.py:237
  17.1 3.6 %collective-permute-start = (f32[256,384]{1,0:T(8,128)S(1)}, f32[256,384]{1,0:T(8,128)S(1)}, u32[]{:S(2)}, u32[]{:S(2)}) collective-permute-start(f32[256,384]{1,0:T(8,128)S(1)} %pad_maximum_fusion.rb_own), channel_id=1, source_target_pairs={{16,0},{17,1},{18,2},{19,3},{20,4},{21,5},{22,6},{23,7},{24,8},{25... | collective-permute-start | bytes 1179656 | tf_op jit(solution)/shard_map/ppermute | solution.py:56
  34.3 21.9 %collective-permute-start.2 = (f32[8,72,256]{2,1,0:T(8,128)S(1)}, f32[8,72,256]{2,1,0:T(8,128)S(1)}, u32[]{:S(2)}, u32[]{:S(2)}) collective-permute-start(f32[8,72,256]{2,1,0:T(8,128)S(1)} %all-to-all-done.pack), channel_id=1, source_target_pairs={{256,0},{257,1},{258,2},{259,3},{260,4},{261,5},{262,6},{263,7},{2... | collective-permute-start | bytes 1769480 | tf_op jit(solution)/shard_map/ppermute | solution.py:56
  37.1 29.2 %collective-permute-start.4 = (f32[8,72,256]{2,1,0:T(8,128)S(1)}, f32[8,72,256]{2,1,0:T(8,128)S(1)}, u32[]{:S(2)}, u32[]{:S(2)}) collective-permute-start(f32[8,72,256]{2,1,0:T(8,128)S(1)} %all-to-all-done.pack), channel_id=1, source_target_pairs={{257,0},{256,1},{259,2},{258,3},{261,4},{260,5},{263,6},{262,7},{2... | collective-permute-start | bytes 1769480 | tf_op jit(solution)/shard_map/ppermute | solution.py:56
  52.2 14.2 %collective-permute-start.5 = (f32[8,64,256]{2,1,0:T(8,128)S(1)}, f32[8,64,256]{2,1,0:T(8,128)S(1)}, u32[]{:S(2)}, u32[]{:S(2)}) collective-permute-start(f32[8,64,256]{2,1,0:T(8,128)S(1)} %get-tuple-element.38), channel_id=1, source_target_pairs={{257,0},{256,1},{259,2},{258,3},{261,4},{260,5},{263,6},{262,7},{2... | collective-permute-start | bytes 1572872 | tf_op jit(solution)/shard_map/ppermute | solution.py:56
  56.2 15.2 %collective-permute-start.3 = (f32[8,72,256]{2,1,0:T(8,128)S(1)}, f32[8,72,256]{2,1,0:T(8,128)S(1)}, u32[]{:S(2)}, u32[]{:S(2)}) collective-permute-start(f32[8,72,256]{2,1,0:T(8,128)S(1)} %collective-permute-done.2.pack), channel_id=1, source_target_pairs={{257,0},{256,1},{259,2},{258,3},{261,4},{260,5},{263,6},{262,7},{2... | collective-permute-start | bytes 1769480 | tf_op jit(solution)/shard_map/ppermute | solution.py:56
  62.4 19.4 %collective-permute-start.7 = (f32[8,64,256]{2,1,0:T(8,128)S(1)}, f32[8,64,256]{2,1,0:T(8,128)S(1)}, u32[]{:S(2)}, u32[]{:S(2)}) collective-permute-start(f32[8,64,256]{2,1,0:T(8,128)S(1)} %get-tuple-element.42), channel_id=1, source_target_pairs={{257,0},{256,1},{259,2},{258,3},{261,4},{260,5},{263,6},{262,7},{2... | collective-permute-start | bytes 1572872 | tf_op jit(solution)/shard_map/ppermute | solution.py:56
  66.4 5.0 %copy-start = (f32[512,512]{1,0:T(8,128)S(1)}, f32[512,512]{1,0:T(8,128)}, u32[]{:S(2)}) copy-start(f32[512,512]{1,0:T(8,128)} %get-tuple-element.26.count) | copy-start | bytes 3145732
  69.5 12.3 %collective-permute-start.8 = (f32[8,64,256]{2,1,0:T(8,128)S(1)}, f32[8,64,256]{2,1,0:T(8,128)S(1)}, u32[]{:S(2)}, u32[]{:S(2)}) collective-permute-start(f32[8,64,256]{2,1,0:T(8,128)S(1)} %get-tuple-element.43), channel_id=1, source_target_pairs={{256,0},{257,1},{258,2},{259,3},{260,4},{261,5},{262,6},{263,7},{2... | collective-permute-start | bytes 1572872 | tf_op jit(solution)/shard_map/ppermute | solution.py:56
  109.9 7.0 %collective-permute-start.9 = (f32[8,256]{1,0:T(8,128)S(1)}, f32[8,256]{1,0:T(8,128)S(1)}, u32[]{:S(2)}, u32[]{:S(2)}) collective-permute-start(f32[8,256]{1,0:T(8,128)S(1)} %broadcast_multiply_fusion), channel_id=1, source_target_pairs={{1,0},{0,1},{3,2},{2,3},{5,4},{4,5},{7,6},{6,7},{9,8},{8,9},{11,10... | collective-permute-start | bytes 24584 | tf_op jit(solution)/shard_map/ppermute | solution.py:56
  117.7 16.7 %all-to-all-start.2 = ((f32[32,8,256]{2,1,0:T(8,128)}), f32[32,8,256]{2,1,0:T(8,128)S(1)}, u32[]{:S(2)}, u32[]{:S(2)}) async-start(f32[32,8,256]{2,1,0:T(8,128)} %broadcast_in_dim.5), calls=%async_computation.2 | async-start | bytes 524288 | tf_op jit(solution)/shard_map/all_to_all | solution.py:260
  122.9 3.4 %collective-permute-start.6 = (f32[256,256]{1,0:T(8,128)S(1)}, f32[256,256]{1,0:T(8,128)S(1)}, u32[]{:S(2)}, u32[]{:S(2)}) collective-permute-start(f32[256,256]{1,0:T(8,128)S(1)} %slice.7), channel_id=1, source_target_pairs={{16,0},{17,1},{18,2},{19,3},{20,4},{21,5},{22,6},{23,7},{24,8},{25... | collective-permute-start | bytes 786440 | tf_op jit(solution)/shard_map/ppermute | solution.py:56

commit v5 on v4

--- a/solution.py
+++ b/solution.py
@@ -92,19 +92,33 @@
     )(col_embed, col_marg.reshape(1, DIM))
 
 
-def prepare_kernel(table, c_own, c_oth, rb_own, rb_oth, *outs):
-    count_out, (rh, rl, th, tl, base) = outs[:4], outs[4:]
+def rows_kernel(rb_own, rb_oth, rh, rl, th, tl, base):
+    for k, rb in enumerate((rb_own, rb_oth)):
+        part = slice(k * ROWS, (k + 1) * ROWS)
+        value = rb[:, :DIM]
+        rh[part, :], rl[part, :] = split(value)
+        th[:, part], tl[:, part] = split(value.T)
+        base[part, :] = rb[:, DIM:]
+
+
+def prepare_rows(rb_own, rb_oth):
+    tall = jax.ShapeDtypeStruct((2 * ROWS, DIM), jnp.bfloat16)
+    wide = jax.ShapeDtypeStruct((DIM, 2 * ROWS), jnp.bfloat16)
+    base = jax.ShapeDtypeStruct((2 * ROWS, 128), jnp.float32)
+    vmem = pl.BlockSpec(memory_space=pltpu.VMEM)
+    return pl.pallas_call(
+        rows_kernel,
+        in_specs=[vmem] * 2,
+        out_specs=[vmem] * 5,
+        out_shape=[tall, tall, wide, wide, base],
+        compiler_params=pltpu.CompilerParams(vmem_limit_bytes=16 * 2**20),
+        cost_estimate=pl.CostEstimate(flops=2**22, bytes_accessed=2**21, transcendentals=0),
+    )(rb_own, rb_oth)
+
+
+def counts_kernel(table, c_own, c_oth, *count_out):
     step = pl.program_id(0)
     steps = pl.num_programs(0)
-
-    @pl.when(step == 0)
-    def _():
-        for k, rb in enumerate((rb_own, rb_oth)):
-            part = slice(k * ROWS, (k + 1) * ROWS)
-            value = rb[:, :DIM]
-            rh[part, :], rl[part, :] = split(value)
-            th[:, part], tl[:, part] = split(value.T)
-            base[part, :] = rb[:, DIM:]
 
     def work(counts):
         half = lax.broadcasted_iota(jnp.int32, (STRIP, 128), 1) < SLICE
@@ -128,38 +142,24 @@
         work(c_oth)
 
 
-def prepare(table, counts, rb):
+def prepare_counts(table, counts):
     half = ROWS // STRIP
-
-    def whole(shape):
-        return pl.BlockSpec(shape, lambda i, w: (0, 0))
-
     columns = counts[0].shape[1]
-    tall, wide, base = (2 * ROWS, DIM), (DIM, 2 * ROWS), (2 * ROWS, 128)
-    bf16 = jnp.bfloat16
-    outs = pl.pallas_call(
-        prepare_kernel,
+    return pl.pallas_call(
+        counts_kernel,
         grid_spec=pltpu.PrefetchScalarGridSpec(
             num_scalar_prefetch=1,
             grid=(2 * half,),
             in_specs=[
                 pl.BlockSpec((STRIP, columns), lambda i, w: (jnp.minimum(i, half - 1), 0)),
                 pl.BlockSpec((STRIP, columns), lambda i, w: (jnp.maximum(i - half, 0), 0)),
-            ]
-            + [whole((ROWS, DIM + 128))] * 2,
-            out_specs=[pl.BlockSpec((STRIP, 2 * DIM), lambda i, w: (i, 0))] * 4
-            + [whole(tall)] * 2
-            + [whole(wide)] * 2
-            + [whole(base)],
+            ],
+            out_specs=[pl.BlockSpec((STRIP, 2 * DIM), lambda i, w: (i, 0))] * 4,
         ),
-        out_shape=[jax.ShapeDtypeStruct((2 * ROWS, 2 * DIM), jnp.float32)] * 4
-        + [jax.ShapeDtypeStruct(tall, bf16)] * 2
-        + [jax.ShapeDtypeStruct(wide, bf16)] * 2
-        + [jax.ShapeDtypeStruct(base, jnp.float32)],
-        compiler_params=pltpu.CompilerParams(vmem_limit_bytes=48 * 2**20),
+        out_shape=[jax.ShapeDtypeStruct((2 * ROWS, 2 * DIM), jnp.float32)] * 4,
+        compiler_params=pltpu.CompilerParams(vmem_limit_bytes=54 * 2**20),
         cost_estimate=pl.CostEstimate(flops=2**22, bytes_accessed=2**21, transcendentals=0),
-    )(table, *counts, *rb)
-    return outs[:4], outs[4:]
+    )(table, *counts)
 
 
 def cells_kernel(which, adds_r, adds_g, table, count, rh, rl, th, tl, base, pack, *rest):
@@ -237,10 +237,11 @@
     s_own = lax.all_to_all(pack_slice(col_embed, col_marg), "z", 0, 0)
     base_row = log_total[0] - jnp.log(row_marg.astype(jnp.float32))
     rb = jnp.concatenate([row_embed, jnp.broadcast_to(base_row[:, None], (ROWS, 128))], axis=1)
-    s_own, rb, rb_oth, counts_oth = lax.optimization_barrier(
-        (s_own, rb, fetch(rb, core_swap), fetch(counts, core_swap))
-    )
-    prepared = prepare(table, (counts, counts_oth), (rb, rb_oth))
+    by_slice = prepare_counts(table, (counts, fetch(counts, core_swap)))
+    s_own, rb, rb_oth, by_slice = lax.optimization_barrier(
+        (s_own, rb, fetch(rb, core_swap), by_slice)
+    )
+    prepared = (by_slice, prepare_rows(rb, rb_oth))
 
     s_a, s_b = fetch(s_own, side_a), fetch(s_own, side_b)
     r, g_own = cells(0, table, prepared, s_own)
@@ -250,8 +251,8 @@
     from_a = fetch(g_a, side_b)
     r, g_b = cells(2, table, prepared, s_b, r, sent)
     from_b = fetch(g_b, side_a)
-    r, g = cells(3, table, prepared, s_far, r)
-    g = g + from_a + from_b
+    r, g = cells(3, table, prepared, s_far, r, from_a)
+    g = g + from_b
 
     g = lax.all_to_all(g.reshape(64, 8, DIM), ("z", "y"), 0, 0)
     row_grad = (r[:ROWS] + fetch(r[ROWS:], core_swap)) * (1.0 / 64.0)

time: 137 us -> 131 us (0.956)
  waiting for transfers between devices: 35.1 us -> 27.6 us
  local copies, waits for them, and re-layouts: 1.63 us -> 3.46 us
    all_to_all x1, waiting for transfers between devices: 13.6 us -> 4.72 us  [body(): s_own = lax.all_to_all(pack_slice(col_embed, col_marg), 'z', 0, 0)]
    pallas_call x1 -> x2, Pallas kernels: 8.94 us -> 9.82 us  [the longest x1 9.61 us: prepare_counts(): pl.pallas_call(counts_kernel, grid_spec=pltpu.PrefetchScalarGridSpec(num_...]
  transfers between devices with their start and end apart: 12 -> 12, of which waited for: 6 -> 6; matrix products, arithmetic and copies ran while one was open for 2% -> 2% of each run, Pallas kernels for 17% -> 18%
where the time goes in v5:
time: 131 us; the launch traced here: 130 us
  starting transfers between devices  42.9 us (33%)
  blocking collectives  27.8 us (21%)
  waiting for transfers between devices  27.6 us (21%)
  Pallas kernels  23.9 us (18%)
  local copies, waits for them, and re-layouts  3.46 us (3%)
  other arithmetic  2.55 us (2%)
  between operations  1.53 us (1%)
    all_to_all x1, blocking collectives, body(): g = lax.all_to_all(g.reshape(64, 8, DIM), ('z', 'y'), 0, 0)  27.8 us
    ppermute x10, starting transfers between devices, fetch(): return lax.ppermute(value, AXES, pairs_to(move))  27.4 us
    ppermute x10, waiting for transfers between devices, fetch(): return lax.ppermute(value, AXES, pairs_to(move))  15.6 us
    pallas_call x4, Pallas kernels, cells(): pl.pallas_call(functools.partial(cells_kernel, which, r_in is not None, g...  12.2 us
    all_to_all x1, starting transfers between devices, body(): s_own = lax.all_to_all(pack_slice(col_embed, col_marg), 'z', 0, 0)  10.3 us
    pallas_call x1, Pallas kernels, prepare_counts(): pl.pallas_call(counts_kernel, grid_spec=pltpu.PrefetchScalarGridSpec(num_...  9.61 us
    all_to_all x1, waiting for transfers between devices, body(): lax.all_to_all(jnp.broadcast_to(g[None], (32, 8, DIM)), ('core', 'xlo', '...  7.3 us
    all_to_all x1, starting transfers between devices, body(): lax.all_to_all(jnp.broadcast_to(g[None], (32, 8, DIM)), ('core', 'xlo', '...  5.28 us
  transfers between devices with their start and end apart: 12, of which 6 were waited for; matrix products, arithmetic and copies ran while one was open for 2% of the time, Pallas kernels for 18%

profile of v5, /device:TPU:6, one launch (start us, length us, event | category | flops | bytes accessed | tf_op | source)
XLA Modules:
  0.0 129.8 jit_solution(1296845935687775779)
XLA Ops:
  0.6 1.9 %collective-permute-start.1 = (s32[256,4096]{1,0:T(8,128)}, s32[256,4096]{1,0:T(8,128)}, u32[]{:S(2)}, u32[]{:S(2)}) collective-permute-start(s32[256,4096]{1,0:T(8,128)} %c_own.1), channel_id=1, source_target_pairs={{16,0},{17,1},{18,2},{19,3},{20,4},{21,5},{22,6},{23,7},{24,8},{25... | collective-permute-start | bytes 12582920 | tf_op jit(solution)/shard_map/ppermute | solution.py:56
  2.6 1.9 %shard_map.77 = f32[8,72,256]{2,1,0:T(8,128)} custom-call(f32[256,256]{1,0:T(8,128)} %embed.1, s32[1,256]{1,0:T(1,128)} %bitcast.14), custom_call_target="tpu_custom_call" | custom-call | tf_op jit(solution)/shard_map/pallas_call | solution.py:88
  4.4 10.3 %all-to-all-start = ((f32[8,72,256]{2,1,0:T(8,128)}), f32[8,72,256]{2,1,0:T(8,128)S(1)}, u32[]{:S(2)}, u32[]{:S(2)}) async-start(f32[8,72,256]{2,1,0:T(8,128)} %shard_map.77), calls=%async_computation | async-start | bytes 1179648 | tf_op jit(solution)/shard_map/all_to_all | solution.py:237
  15.4 0.7 log_subtract_fusion
  16.2 1.0 pad_maximum_fusion.rb_own
  17.2 2.1 %collective-permute-start = (f32[256,384]{1,0:T(8,128)S(1)}, f32[256,384]{1,0:T(8,128)S(1)}, u32[]{:S(2)}, u32[]{:S(2)}) collective-permute-start(f32[256,384]{1,0:T(8,128)S(1)} %pad_maximum_fusion.rb_own), channel_id=1, source_target_pairs={{16,0},{17,1},{18,2},{19,3},{20,4},{21,5},{22,6},{23,7},{24,8},{25... | collective-permute-start | bytes 1179656 | tf_op jit(solution)/shard_map/ppermute | solution.py:56
  19.3 0.7 stack.36.table
  20.0 9.6 %shard_map.78 = (f32[512,512]{1,0:T(8,128)}, f32[512,512]{1,0:T(8,128)}, f32[512,512]{1,0:T(8,128)}, f32[512,512]{1,0:T(8,128)}) custom-call(s32[12]{0:T(128)} %stack.36.table, s32[256,4096]{1,0:T(8,128)} %c_own.1, s32[256,4096]{1,0:T(8,128)} %collective-permute-done.1.c_oth), custom_call_target="tpu_custom_call" | custom-call | flops 4194304 | bytes 2097152 | tf_op jit(solution)/shard_map/pallas_call | solution.py:148
  29.6 4.7 %all-to-all-done.pack = f32[8,72,256]{2,1,0:T(8,128)S(1)} async-done(((f32[8,72,256]{2,1,0:T(8,128)}), f32[8,72,256]{2,1,0:T(8,128)S(1)}, u32[]{:S(2)}, u32[]{:S(2)}) %all-to-all-start) | async-done | bytes 589856 | tf_op jit(solution)/shard_map/all_to_all | solution.py:237
  34.4 2.7 %collective-permute-start.2 = (f32[8,72,256]{2,1,0:T(8,128)S(1)}, f32[8,72,256]{2,1,0:T(8,128)S(1)}, u32[]{:S(2)}, u32[]{:S(2)}) collective-permute-start(f32[8,72,256]{2,1,0:T(8,128)S(1)} %all-to-all-done.pack), channel_id=1, source_target_pairs={{256,0},{257,1},{258,2},{259,3},{260,4},{261,5},{262,6},{263,7},{2... | collective-permute-start | bytes 1769480 | tf_op jit(solution)/shard_map/ppermute | solution.py:56
  37.1 3.0 %collective-permute-start.4 = (f32[8,72,256]{2,1,0:T(8,128)S(1)}, f32[8,72,256]{2,1,0:T(8,128)S(1)}, u32[]{:S(2)}, u32[]{:S(2)}) collective-permute-start(f32[8,72,256]{2,1,0:T(8,128)S(1)} %all-to-all-done.pack), channel_id=1, source_target_pairs={{257,0},{256,1},{259,2},{258,3},{261,4},{260,5},{263,6},{262,7},{2... | collective-permute-start | bytes 1769480 | tf_op jit(solution)/shard_map/ppermute | solution.py:56
  40.4 1.2 copy-done.4
  41.6 3.1 %shard_map.80 = (f32[512,256]{1,0:T(8,128)S(1)}, f32[8,64,256]{2,1,0:T(8,128)S(1)}) custom-call(s32[12]{0:T(128)S(1)} %copy-done, f32[512,512]{1,0:T(8,128)S(1)} %copy-done.4, bf16[512,256]{1,0:T(8,128)(2,1)S(1)} %get-tuple-element.33.rh, bf16[512,256]{1,0:T(8,128)(2,1)S(1)} %get-tuple-element.34.rl, bf16[256,512]{1,0:T(8,128)(2,1)S(1)} %get-tuple-element.35.th, ...), custom_call_target="tpu_custom_call" | custom-call | flops 4000000000 | bytes 4194304 | tf_op jit(solution)/shard_map/pallas_call | solution.py:213
  44.7 4.0 %collective-permute-start.5 = (f32[8,64,256]{2,1,0:T(8,128)S(1)}, f32[8,64,256]{2,1,0:T(8,128)S(1)}, u32[]{:S(2)}, u32[]{:S(2)}) collective-permute-start(f32[8,64,256]{2,1,0:T(8,128)S(1)} %get-tuple-element.44), channel_id=1, source_target_pairs={{257,0},{256,1},{259,2},{258,3},{261,4},{260,5},{263,6},{262,7},{2... | collective-permute-start | bytes 1572872 | tf_op jit(solution)/shard_map/ppermute | solution.py:56
  48.7 2.6 %collective-permute-done.2.pack = f32[8,72,256]{2,1,0:T(8,128)S(1)} collective-permute-done((f32[8,72,256]{2,1,0:T(8,128)S(1)}, f32[8,72,256]{2,1,0:T(8,128)S(1)}, u32[]{:S(2)}, u32[]{:S(2)}) %collective-permute-start.2) | collective-permute-done | bytes 589856 | tf_op jit(solution)/shard_map/ppermute | solution.py:56
  51.2 1.9 %collective-permute-start.3 = (f32[8,72,256]{2,1,0:T(8,128)S(1)}, f32[8,72,256]{2,1,0:T(8,128)S(1)}, u32[]{:S(2)}, u32[]{:S(2)}) collective-permute-start(f32[8,72,256]{2,1,0:T(8,128)S(1)} %collective-permute-done.2.pack), channel_id=1, source_target_pairs={{257,0},{256,1},{259,2},{258,3},{261,4},{260,5},{263,6},{262,7},{2... | collective-permute-start | bytes 1769480 | tf_op jit(solution)/shard_map/ppermute | solution.py:56
  53.2 3.1 %shard_map.81 = (f32[512,256]{1,0:T(8,128)S(1)}, f32[8,64,256]{2,1,0:T(8,128)S(1)}) custom-call(s32[12]{0:T(128)S(1)} %copy-done, f32[512,512]{1,0:T(8,128)S(1)} %copy-done.3, bf16[512,256]{1,0:T(8,128)(2,1)S(1)} %get-tuple-element.33.rh, bf16[512,256]{1,0:T(8,128)(2,1)S(1)} %get-tuple-element.34.rl, bf16[256,512]{1,0:T(8,128)(2,1)S(1)} %get-tuple-element.35.th, ...), custom_call_target="tpu_custom_call" | custom-call | flops 4000000000 | bytes 4194304 | tf_op jit(solution)/shard_map/pallas_call | solution.py:213
  56.2 5.1 %collective-permute-start.6 = (f32[8,64,256]{2,1,0:T(8,128)S(1)}, f32[8,64,256]{2,1,0:T(8,128)S(1)}, u32[]{:S(2)}, u32[]{:S(2)}) collective-permute-start(f32[8,64,256]{2,1,0:T(8,128)S(1)} %get-tuple-element.46), channel_id=1, source_target_pairs={{257,0},{256,1},{259,2},{258,3},{261,4},{260,5},{263,6},{262,7},{2... | collective-permute-start | bytes 1572872 | tf_op jit(solution)/shard_map/ppermute | solution.py:56
  61.4 3.1 %shard_map.82 = (f32[512,256]{1,0:T(8,128)S(1)}, f32[8,64,256]{2,1,0:T(8,128)S(1)}) custom-call(s32[12]{0:T(128)S(1)} %copy-done, f32[512,512]{1,0:T(8,128)S(1)} %copy-done.2, bf16[512,256]{1,0:T(8,128)(2,1)S(1)} %get-tuple-element.33.rh, bf16[512,256]{1,0:T(8,128)(2,1)S(1)} %get-tuple-element.34.rl, bf16[256,512]{1,0:T(8,128)(2,1)S(1)} %get-tuple-element.35.th, ...), custom_call_target="tpu_custom_call" | custom-call | flops 4000000000 | bytes 4194304 | tf_op jit(solution)/shard_map/pallas_call | solution.py:213
  64.5 1.9 %collective-permute-start.8 = (f32[8,64,256]{2,1,0:T(8,128)S(1)}, f32[8,64,256]{2,1,0:T(8,128)S(1)}, u32[]{:S(2)}, u32[]{:S(2)}) collective-permute-start(f32[8,64,256]{2,1,0:T(8,128)S(1)} %get-tuple-element.49), channel_id=1, source_target_pairs={{256,0},{257,1},{258,2},{259,3},{260,4},{261,5},{262,6},{263,7},{2... | collective-permute-start | bytes 1572872 | tf_op jit(solution)/shard_map/ppermute | solution.py:56
  66.4 7.1 %collective-permute-done.6.rest_1_ = f32[8,64,256]{2,1,0:T(8,128)S(1)} collective-permute-done((f32[8,64,256]{2,1,0:T(8,128)S(1)}, f32[8,64,256]{2,1,0:T(8,128)S(1)}, u32[]{:S(2)}, u32[]{:S(2)}) %collective-permute-start.6) | collective-permute-done | bytes 524320 | tf_op jit(solution)/shard_map/ppermute | solution.py:56
  73.5 3.1 %shard_map.83 = (f32[512,256]{1,0:T(8,128)S(1)}, f32[8,64,256]{2,1,0:T(8,128)S(1)}) custom-call(s32[12]{0:T(128)S(1)} %copy-done, f32[512,512]{1,0:T(8,128)S(1)} %copy-done.1, bf16[512,256]{1,0:T(8,128)(2,1)S(1)} %get-tuple-element.33.rh, bf16[512,256]{1,0:T(8,128)(2,1)S(1)} %get-tuple-element.34.rl, bf16[256,512]{1,0:T(8,128)(2,1)S(1)} %get-tuple-element.35.th, ...), custom_call_target="tpu_custom_call" | custom-call | flops 4000000000 | bytes 4194304 | tf_op jit(solution)/shard_map/pallas_call | solution.py:213
  76.7 27.8 %all_to_all.15 = f32[64,8,256]{2,1,0:T(8,128)S(1)} all-to-all(f32[64,8,256]{2,1,0:T(8,128)S(1)} %bitcast.12), channel_id=1, replica_groups=mesh['xlo'=2,'y'=8,'core'=2,'z'=8,'xhi'=2] {'z','y'}, dimensions={0} | all-to-all | bytes 1048576 | tf_op jit(solution)/shard_map/all_to_all | solution.py:257
  104.6 2.5 %collective-permute-start.9 = (f32[8,256]{1,0:T(8,128)S(1)}, f32[8,256]{1,0:T(8,128)S(1)}, u32[]{:S(2)}, u32[]{:S(2)}) collective-permute-start(f32[8,256]{1,0:T(8,128)S(1)} %broadcast_multiply_fusion), channel_id=1, source_target_pairs={{1,0},{0,1},{3,2},{2,3},{5,4},{4,5},{7,6},{6,7},{9,8},{8,9},{11,10... | collective-permute-start | bytes 24584 | tf_op jit(solution)/shard_map/ppermute | solution.py:56
  107.1 4.5 %collective-permute-done.9 = f32[8,256]{1,0:T(8,128)S(1)} collective-permute-done((f32[8,256]{1,0:T(8,128)S(1)}, f32[8,256]{1,0:T(8,128)S(1)}, u32[]{:S(2)}, u32[]{:S(2)}) %collective-permute-start.9) | collective-permute-done | bytes 8224 | tf_op jit(solution)/shard_map/ppermute | solution.py:56
  111.6 0.7 broadcast_in_dim.5
  112.4 5.3 %all-to-all-start.2 = ((f32[32,8,256]{2,1,0:T(8,128)}), f32[32,8,256]{2,1,0:T(8,128)S(1)}, u32[]{:S(2)}, u32[]{:S(2)}) async-start(f32[32,8,256]{2,1,0:T(8,128)} %broadcast_in_dim.5), calls=%async_computation.2 | async-start | bytes 524288 | tf_op jit(solution)/shard_map/all_to_all | solution.py:261
  117.7 2.1 %collective-permute-start.7 = (f32[256,256]{1,0:T(8,128)S(1)}, f32[256,256]{1,0:T(8,128)S(1)}, u32[]{:S(2)}, u32[]{:S(2)}) collective-permute-start(f32[256,256]{1,0:T(8,128)S(1)} %slice.7), channel_id=1, source_target_pairs={{16,0},{17,1},{18,2},{19,3},{20,4},{21,5},{22,6},{23,7},{24,8},{25... | collective-permute-start | bytes 786440 | tf_op jit(solution)/shard_map/ppermute | solution.py:56
  119.7 1.4 %collective-permute-done.7 = f32[256,256]{1,0:T(8,128)S(1)} collective-permute-done((f32[256,256]{1,0:T(8,128)S(1)}, f32[256,256]{1,0:T(8,128)S(1)}, u32[]{:S(2)}, u32[]{:S(2)}) %collective-permute-start.7) | collective-permute-done | bytes 262176 | tf_op jit(solution)/shard_map/ppermute | solution.py:56
  121.1 0.7 add_multiply_fusion
  121.8 7.3 %all-to-all-done.2 = f32[32,8,256]{2,1,0:T(8,128)S(1)} async-done(((f32[32,8,256]{2,1,0:T(8,128)}), f32[32,8,256]{2,1,0:T(8,128)S(1)}, u32[]{:S(2)}, u32[]{:S(2)}) %all-to-all-start.2) | async-done | bytes 262176 | tf_op jit(solution)/shard_map/all_to_all | solution.py:261
  129.1 0.7 copy.10
  (21 shorter events, 0.5 us)
Async XLA Ops:
  0.6 19.4 %collective-permute-start.1 = (s32[256,4096]{1,0:T(8,128)}, s32[256,4096]{1,0:T(8,128)}, u32[]{:S(2)}, u32[]{:S(2)}) collective-permute-start(s32[256,4096]{1,0:T(8,128)} %c_own.1), channel_id=1, source_target_pairs={{16,0},{17,1},{18,2},{19,3},{20,4},{21,5},{22,6},{23,7},{24,8},{25... | collective-permute-start | bytes 12582920 | tf_op jit(solution)/shard_map/ppermute | solution.py:56
  4.4 29.9 %all-to-all-start = ((f32[8,72,256]{2,1,0:T(8,128)}), f32[8,72,256]{2,1,0:T(8,128)S(1)}, u32[]{:S(2)}, u32[]{:S(2)}) async-start(f32[8,72,256]{2,1,0:T(8,128)} %shard_map.77), calls=%async_computation | async-start | bytes 1179648 | tf_op jit(solution)/shard_map/all_to_all | solution.py:237
  17.2 12.5 %collective-permute-start = (f32[256,384]{1,0:T(8,128)S(1)}, f32[256,384]{1,0:T(8,128)S(1)}, u32[]{:S(2)}, u32[]{:S(2)}) collective-permute-start(f32[256,384]{1,0:T(8,128)S(1)} %pad_maximum_fusion.rb_own), channel_id=1, source_target_pairs={{16,0},{17,1},{18,2},{19,3},{20,4},{21,5},{22,6},{23,7},{24,8},{25... | collective-permute-start | bytes 1179656 | tf_op jit(solution)/shard_map/ppermute | solution.py:56
  20.0 20.4 %copy-start = (s32[12]{0:T(128)S(1)}, s32[12]{0:T(128)}, u32[]{:S(2)}) copy-start(s32[12]{0:T(128)} %stack.36.table) | copy-start | bytes 148
  34.4 16.9 %collective-permute-start.2 = (f32[8,72,256]{2,1,0:T(8,128)S(1)}, f32[8,72,256]{2,1,0:T(8,128)S(1)}, u32[]{:S(2)}, u32[]{:S(2)}) collective-permute-start(f32[8,72,256]{2,1,0:T(8,128)S(1)} %all-to-all-done.pack), channel_id=1, source_target_pairs={{256,0},{257,1},{258,2},{259,3},{260,4},{261,5},{262,6},{263,7},{2... | collective-permute-start | bytes 1769480 | tf_op jit(solution)/shard_map/ppermute | solution.py:56
  37.1 24.3 %collective-permute-start.4 = (f32[8,72,256]{2,1,0:T(8,128)S(1)}, f32[8,72,256]{2,1,0:T(8,128)S(1)}, u32[]{:S(2)}, u32[]{:S(2)}) collective-permute-start(f32[8,72,256]{2,1,0:T(8,128)S(1)} %all-to-all-done.pack), channel_id=1, source_target_pairs={{257,0},{256,1},{259,2},{258,3},{261,4},{260,5},{263,6},{262,7},{2... | collective-permute-start | bytes 1769480 | tf_op jit(solution)/shard_map/ppermute | solution.py:56
  40.4 1.2 copy-start.4
  41.6 11.6 %copy-start.3 = (f32[512,512]{1,0:T(8,128)S(1)}, f32[512,512]{1,0:T(8,128)}, u32[]{:S(2)}) copy-start(f32[512,512]{1,0:T(8,128)} %get-tuple-element.40.count) | copy-start | bytes 3145732
  44.7 16.7 %collective-permute-start.5 = (f32[8,64,256]{2,1,0:T(8,128)S(1)}, f32[8,64,256]{2,1,0:T(8,128)S(1)}, u32[]{:S(2)}, u32[]{:S(2)}) collective-permute-start(f32[8,64,256]{2,1,0:T(8,128)S(1)} %get-tuple-element.44), channel_id=1, source_target_pairs={{257,0},{256,1},{259,2},{258,3},{261,4},{260,5},{263,6},{262,7},{2... | collective-permute-start | bytes 1572872 | tf_op jit(solution)/shard_map/ppermute | solution.py:56
  51.2 22.3 %collective-permute-start.3 = (f32[8,72,256]{2,1,0:T(8,128)S(1)}, f32[8,72,256]{2,1,0:T(8,128)S(1)}, u32[]{:S(2)}, u32[]{:S(2)}) collective-permute-start(f32[8,72,256]{2,1,0:T(8,128)S(1)} %collective-permute-done.2.pack), channel_id=1, source_target_pairs={{257,0},{256,1},{259,2},{258,3},{261,4},{260,5},{263,6},{262,7},{2... | collective-permute-start | bytes 1769480 | tf_op jit(solution)/shard_map/ppermute | solution.py:56
  53.2 8.2 %copy-start.2 = (f32[512,512]{1,0:T(8,128)S(1)}, f32[512,512]{1,0:T(8,128)}, u32[]{:S(2)}) copy-start(f32[512,512]{1,0:T(8,128)} %get-tuple-element.39.count) | copy-start | bytes 3145732
  56.2 17.3 %collective-permute-start.6 = (f32[8,64,256]{2,1,0:T(8,128)S(1)}, f32[8,64,256]{2,1,0:T(8,128)S(1)}, u32[]{:S(2)}, u32[]{:S(2)}) collective-permute-start(f32[8,64,256]{2,1,0:T(8,128)S(1)} %get-tuple-element.46), channel_id=1, source_target_pairs={{257,0},{256,1},{259,2},{258,3},{261,4},{260,5},{263,6},{262,7},{2... | collective-permute-start | bytes 1572872 | tf_op jit(solution)/shard_map/ppermute | solution.py:56
  61.4 12.1 %copy-start.1 = (f32[512,512]{1,0:T(8,128)S(1)}, f32[512,512]{1,0:T(8,128)}, u32[]{:S(2)}) copy-start(f32[512,512]{1,0:T(8,128)} %get-tuple-element.30.count) | copy-start | bytes 3145732
  64.5 12.1 %collective-permute-start.8 = (f32[8,64,256]{2,1,0:T(8,128)S(1)}, f32[8,64,256]{2,1,0:T(8,128)S(1)}, u32[]{:S(2)}, u32[]{:S(2)}) collective-permute-start(f32[8,64,256]{2,1,0:T(8,128)S(1)} %get-tuple-element.49), channel_id=1, source_target_pairs={{256,0},{257,1},{258,2},{259,3},{260,4},{261,5},{262,6},{263,7},{2... | collective-permute-start | bytes 1572872 | tf_op jit(solution)/shard_map/ppermute | solution.py:56
  104.6 7.0 %collective-permute-start.9 = (f32[8,256]{1,0:T(8,128)S(1)}, f32[8,256]{1,0:T(8,128)S(1)}, u32[]{:S(2)}, u32[]{:S(2)}) collective-permute-start(f32[8,256]{1,0:T(8,128)S(1)} %broadcast_multiply_fusion), channel_id=1, source_target_pairs={{1,0},{0,1},{3,2},{2,3},{5,4},{4,5},{7,6},{6,7},{9,8},{8,9},{11,10... | collective-permute-start | bytes 24584 | tf_op jit(solution)/shard_map/ppermute | solution.py:56
  112.4 16.8 %all-to-all-start.2 = ((f32[32,8,256]{2,1,0:T(8,128)}), f32[32,8,256]{2,1,0:T(8,128)S(1)}, u32[]{:S(2)}, u32[]{:S(2)}) async-start(f32[32,8,256]{2,1,0:T(8,128)} %broadcast_in_dim.5), calls=%async_computation.2 | async-start | bytes 524288 | tf_op jit(solution)/shard_map/all_to_all | solution.py:261
  117.7 3.4 %collective-permute-start.7 = (f32[256,256]{1,0:T(8,128)S(1)}, f32[256,256]{1,0:T(8,128)S(1)}, u32[]{:S(2)}, u32[]{:S(2)}) collective-permute-start(f32[256,256]{1,0:T(8,128)S(1)} %slice.7), channel_id=1, source_target_pairs={{16,0},{17,1},{18,2},{19,3},{20,4},{21,5},{22,6},{23,7},{24,8},{25... | collective-permute-start | bytes 786440 | tf_op jit(solution)/shard_map/ppermute | solution.py:56

commit v6 on v5

--- a/solution.py
+++ b/solution.py
@@ -28,10 +28,6 @@
     return pairs
 
 
-def x_far(at):
-    return {"xhi": 1 - at["xhi"]}
-
-
 def core_swap(at):
     return {"core": 1 - at["core"]}
 
@@ -42,6 +38,10 @@
 
 def x_next(at):
     return {"xlo": 1 - at["xlo"], "xhi": 1 - at["xhi"]}
+
+
+def x_next_core(at):
+    return {**x_next(at), **core_swap(at)}
 
 
 def side_a(at):
@@ -251,15 +251,19 @@
     from_a = fetch(g_a, side_b)
     r, g_b = cells(2, table, prepared, s_b, r, sent)
     from_b = fetch(g_b, side_a)
-    r, g = cells(3, table, prepared, s_far, r, from_a)
-    g = g + from_b
+    r, g = cells(3, table, prepared, s_far, r)
+    g = lax.optimization_barrier(g + from_a) + from_b
 
     g = lax.all_to_all(g.reshape(64, 8, DIM), ("z", "y"), 0, 0)
     row_grad = (r[:ROWS] + fetch(r[ROWS:], core_swap)) * (1.0 / 64.0)
     g = jnp.sum(g, axis=0) * (1.0 / math.sqrt(131072.0))
-    g = fetch(g, x_far)
-    g = lax.all_to_all(jnp.broadcast_to(g[None], (32, 8, DIM)), ("core", "xlo", "y"), 0, 0)
-    return row_grad, g.reshape(256, DIM)
+    g = lax.all_to_all(jnp.broadcast_to(g[None], (16, 8, DIM)), ("xlo", "y"), 0, 0)
+    g = g.reshape(2 * SLICE, DIM)
+    same, other = fetch(g, x_next), fetch(g, x_next_core)
+    col_grad = jnp.where(
+        core == 0, jnp.concatenate([same, other]), jnp.concatenate([other, same])
+    )
+    return row_grad, col_grad
 
 
 def solution(mesh):

time: 131 us -> 132 us (level)
  blocking collectives: 27.8 us -> 13.3 us
  waiting for transfers between devices: 27.6 us -> 36.3 us
  starting transfers between devices: 42.9 us -> 48.7 us
  other arithmetic: 2.55 us -> 4.15 us
  local copies, waits for them, and re-layouts: 3.46 us -> 2.03 us
    all_to_all x1, blocking collectives: 27.8 us -> 13.3 us  [body(): lax.all_to_all(jnp.broadcast_to(g[None], (16, 8, DIM)), ('xlo', 'y'), 0, 0)]
    all_to_all x1, waiting for transfers between devices: 7.3 us -> 17.4 us  [body(): g = lax.all_to_all(g.reshape(64, 8, DIM), ('z', 'y'), 0, 0)]
    all_to_all x1, starting transfers between devices: 5.28 us -> 8.74 us  [body(): g = lax.all_to_all(g.reshape(64, 8, DIM), ('z', 'y'), 0, 0)]
    ppermute x10 -> x11, starting transfers between devices: 27.4 us -> 29.6 us  [fetch(): return lax.ppermute(value, AXES, pairs_to(move))]
    ppermute x10 -> x11, waiting for transfers between devices: 15.6 us -> 14.2 us  [fetch(): return lax.ppermute(value, AXES, pairs_to(move))]
  transfers between devices with their start and end apart: 12 -> 13, of which waited for: 6 -> 7; matrix products, arithmetic and copies ran while one was open for 2% -> 3% of each run, Pallas kernels for 18% -> 18%
where the time goes in v6:
time: 132 us; the launch traced here: 130 us
  starting transfers between devices  48.7 us (37%)
  waiting for transfers between devices  36.3 us (27%)
  Pallas kernels  23.9 us (18%)
  blocking collectives  13.3 us (10%)
  other arithmetic  4.15 us (3%)
  local copies, waits for them, and re-layouts  2.03 us (2%)
  between operations  1.56 us (1%)
    ppermute x11, starting transfers between devices, fetch(): return lax.ppermute(value, AXES, pairs_to(move))  29.6 us
    all_to_all x1, waiting for transfers between devices, body(): g = lax.all_to_all(g.reshape(64, 8, DIM), ('z', 'y'), 0, 0)  17.4 us
    ppermute x11, waiting for transfers between devices, fetch(): return lax.ppermute(value, AXES, pairs_to(move))  14.2 us
    all_to_all x1, blocking collectives, body(): lax.all_to_all(jnp.broadcast_to(g[None], (16, 8, DIM)), ('xlo', 'y'), 0, 0)  13.3 us
    pallas_call x4, Pallas kernels, cells(): pl.pallas_call(functools.partial(cells_kernel, which, r_in is not None, g...  12.3 us
    all_to_all x1, starting transfers between devices, body(): s_own = lax.all_to_all(pack_slice(col_embed, col_marg), 'z', 0, 0)  10.3 us
    pallas_call x1, Pallas kernels, prepare_counts(): pl.pallas_call(counts_kernel, grid_spec=pltpu.PrefetchScalarGridSpec(num_...  9.59 us
    all_to_all x1, starting transfers between devices, body(): g = lax.all_to_all(g.reshape(64, 8, DIM), ('z', 'y'), 0, 0)  8.74 us
  transfers between devices with their start and end apart: 13, of which 7 were waited for; matrix products, arithmetic and copies ran while one was open for 3% of the time, Pallas kernels for 18%

profile of v6, /device:TPU:6, one launch (start us, length us, event | category | flops | bytes accessed | tf_op | source)
XLA Modules:
  0.0 130.0 jit_solution(7705488089691917745)
XLA Ops:
  0.6 1.9 %collective-permute-start.1 = (s32[256,4096]{1,0:T(8,128)}, s32[256,4096]{1,0:T(8,128)}, u32[]{:S(2)}, u32[]{:S(2)}) collective-permute-start(s32[256,4096]{1,0:T(8,128)} %c_own.1), channel_id=1, source_target_pairs={{16,0},{17,1},{18,2},{19,3},{20,4},{21,5},{22,6},{23,7},{24,8},{25... | collective-permute-start | bytes 12582920 | tf_op jit(solution)/shard_map/ppermute | solution.py:56
  2.6 1.9 %shard_map.77 = f32[8,72,256]{2,1,0:T(8,128)} custom-call(f32[256,256]{1,0:T(8,128)} %embed.1, s32[1,256]{1,0:T(1,128)} %bitcast.14), custom_call_target="tpu_custom_call" | custom-call | tf_op jit(solution)/shard_map/pallas_call | solution.py:88
  4.5 10.3 %all-to-all-start = ((f32[8,72,256]{2,1,0:T(8,128)}), f32[8,72,256]{2,1,0:T(8,128)S(1)}, u32[]{:S(2)}, u32[]{:S(2)}) async-start(f32[8,72,256]{2,1,0:T(8,128)} %shard_map.77), calls=%async_computation | async-start | bytes 1179648 | tf_op jit(solution)/shard_map/all_to_all | solution.py:237
  16.2 1.0 pad_maximum_fusion.rb_own
  17.2 2.1 %collective-permute-start = (f32[256,384]{1,0:T(8,128)S(1)}, f32[256,384]{1,0:T(8,128)S(1)}, u32[]{:S(2)}, u32[]{:S(2)}) collective-permute-start(f32[256,384]{1,0:T(8,128)S(1)} %pad_maximum_fusion.rb_own), channel_id=1, source_target_pairs={{16,0},{17,1},{18,2},{19,3},{20,4},{21,5},{22,6},{23,7},{24,8},{25... | collective-permute-start | bytes 1179656 | tf_op jit(solution)/shard_map/ppermute | solution.py:56
  20.0 9.6 %shard_map.78 = (f32[512,512]{1,0:T(8,128)}, f32[512,512]{1,0:T(8,128)}, f32[512,512]{1,0:T(8,128)}, f32[512,512]{1,0:T(8,128)}) custom-call(s32[12]{0:T(128)} %stack.36.table, s32[256,4096]{1,0:T(8,128)} %c_own.1, s32[256,4096]{1,0:T(8,128)} %collective-permute-done.1.c_oth), custom_call_target="tpu_custom_call" | custom-call | flops 4194304 | bytes 2097152 | tf_op jit(solution)/shard_map/pallas_call | solution.py:148
  29.6 4.8 %all-to-all-done.pack = f32[8,72,256]{2,1,0:T(8,128)S(1)} async-done(((f32[8,72,256]{2,1,0:T(8,128)}), f32[8,72,256]{2,1,0:T(8,128)S(1)}, u32[]{:S(2)}, u32[]{:S(2)}) %all-to-all-start) | async-done | bytes 589856 | tf_op jit(solution)/shard_map/all_to_all | solution.py:237
  34.4 2.7 %collective-permute-start.2 = (f32[8,72,256]{2,1,0:T(8,128)S(1)}, f32[8,72,256]{2,1,0:T(8,128)S(1)}, u32[]{:S(2)}, u32[]{:S(2)}) collective-permute-start(f32[8,72,256]{2,1,0:T(8,128)S(1)} %all-to-all-done.pack), channel_id=1, source_target_pairs={{256,0},{257,1},{258,2},{259,3},{260,4},{261,5},{262,6},{263,7},{2... | collective-permute-start | bytes 1769480 | tf_op jit(solution)/shard_map/ppermute | solution.py:56
  37.1 3.0 %collective-permute-start.4 = (f32[8,72,256]{2,1,0:T(8,128)S(1)}, f32[8,72,256]{2,1,0:T(8,128)S(1)}, u32[]{:S(2)}, u32[]{:S(2)}) collective-permute-start(f32[8,72,256]{2,1,0:T(8,128)S(1)} %all-to-all-done.pack), channel_id=1, source_target_pairs={{257,0},{256,1},{259,2},{258,3},{261,4},{260,5},{263,6},{262,7},{2... | collective-permute-start | bytes 1769480 | tf_op jit(solution)/shard_map/ppermute | solution.py:56
  40.4 1.2 copy-done.4
  41.6 3.1 %shard_map.80 = (f32[512,256]{1,0:T(8,128)S(1)}, f32[8,64,256]{2,1,0:T(8,128)S(1)}) custom-call(s32[12]{0:T(128)S(1)} %copy-done, f32[512,512]{1,0:T(8,128)S(1)} %copy-done.4, bf16[512,256]{1,0:T(8,128)(2,1)S(1)} %get-tuple-element.33.rh, bf16[512,256]{1,0:T(8,128)(2,1)S(1)} %get-tuple-element.34.rl, bf16[256,512]{1,0:T(8,128)(2,1)S(1)} %get-tuple-element.35.th, ...), custom_call_target="tpu_custom_call" | custom-call | flops 4000000000 | bytes 4194304 | tf_op jit(solution)/shard_map/pallas_call | solution.py:213
  44.7 4.0 %collective-permute-start.5 = (f32[8,64,256]{2,1,0:T(8,128)S(1)}, f32[8,64,256]{2,1,0:T(8,128)S(1)}, u32[]{:S(2)}, u32[]{:S(2)}) collective-permute-start(f32[8,64,256]{2,1,0:T(8,128)S(1)} %get-tuple-element.44), channel_id=1, source_target_pairs={{257,0},{256,1},{259,2},{258,3},{261,4},{260,5},{263,6},{262,7},{2... | collective-permute-start | bytes 1572872 | tf_op jit(solution)/shard_map/ppermute | solution.py:56
  48.7 2.6 %collective-permute-done.2.pack = f32[8,72,256]{2,1,0:T(8,128)S(1)} collective-permute-done((f32[8,72,256]{2,1,0:T(8,128)S(1)}, f32[8,72,256]{2,1,0:T(8,128)S(1)}, u32[]{:S(2)}, u32[]{:S(2)}) %collective-permute-start.2) | collective-permute-done | bytes 589856 | tf_op jit(solution)/shard_map/ppermute | solution.py:56
  51.2 1.9 %collective-permute-start.3 = (f32[8,72,256]{2,1,0:T(8,128)S(1)}, f32[8,72,256]{2,1,0:T(8,128)S(1)}, u32[]{:S(2)}, u32[]{:S(2)}) collective-permute-start(f32[8,72,256]{2,1,0:T(8,128)S(1)} %collective-permute-done.2.pack), channel_id=1, source_target_pairs={{257,0},{256,1},{259,2},{258,3},{261,4},{260,5},{263,6},{262,7},{2... | collective-permute-start | bytes 1769480 | tf_op jit(solution)/shard_map/ppermute | solution.py:56
  53.2 3.1 %shard_map.81 = (f32[512,256]{1,0:T(8,128)S(1)}, f32[8,64,256]{2,1,0:T(8,128)S(1)}) custom-call(s32[12]{0:T(128)S(1)} %copy-done, f32[512,512]{1,0:T(8,128)S(1)} %copy-done.3, bf16[512,256]{1,0:T(8,128)(2,1)S(1)} %get-tuple-element.33.rh, bf16[512,256]{1,0:T(8,128)(2,1)S(1)} %get-tuple-element.34.rl, bf16[256,512]{1,0:T(8,128)(2,1)S(1)} %get-tuple-element.35.th, ...), custom_call_target="tpu_custom_call" | custom-call | flops 4000000000 | bytes 4194304 | tf_op jit(solution)/shard_map/pallas_call | solution.py:213
  56.3 5.1 %collective-permute-start.7 = (f32[8,64,256]{2,1,0:T(8,128)S(1)}, f32[8,64,256]{2,1,0:T(8,128)S(1)}, u32[]{:S(2)}, u32[]{:S(2)}) collective-permute-start(f32[8,64,256]{2,1,0:T(8,128)S(1)} %get-tuple-element.48), channel_id=1, source_target_pairs={{257,0},{256,1},{259,2},{258,3},{261,4},{260,5},{263,6},{262,7},{2... | collective-permute-start | bytes 1572872 | tf_op jit(solution)/shard_map/ppermute | solution.py:56
  61.4 3.1 %shard_map.82 = (f32[512,256]{1,0:T(8,128)S(1)}, f32[8,64,256]{2,1,0:T(8,128)S(1)}) custom-call(s32[12]{0:T(128)S(1)} %copy-done, f32[512,512]{1,0:T(8,128)S(1)} %copy-done.2, bf16[512,256]{1,0:T(8,128)(2,1)S(1)} %get-tuple-element.33.rh, bf16[512,256]{1,0:T(8,128)(2,1)S(1)} %get-tuple-element.34.rl, bf16[256,512]{1,0:T(8,128)(2,1)S(1)} %get-tuple-element.35.th, ...), custom_call_target="tpu_custom_call" | custom-call | flops 4000000000 | bytes 4194304 | tf_op jit(solution)/shard_map/pallas_call | solution.py:213
  64.5 1.9 %collective-permute-start.8 = (f32[8,64,256]{2,1,0:T(8,128)S(1)}, f32[8,64,256]{2,1,0:T(8,128)S(1)}, u32[]{:S(2)}, u32[]{:S(2)}) collective-permute-start(f32[8,64,256]{2,1,0:T(8,128)S(1)} %get-tuple-element.49), channel_id=1, source_target_pairs={{256,0},{257,1},{258,2},{259,3},{260,4},{261,5},{262,6},{263,7},{2... | collective-permute-start | bytes 1572872 | tf_op jit(solution)/shard_map/ppermute | solution.py:56
  66.5 3.1 %shard_map.83 = (f32[512,256]{1,0:T(8,128)S(1)}, f32[8,64,256]{2,1,0:T(8,128)S(1)}) custom-call(s32[12]{0:T(128)S(1)} %copy-done, f32[512,512]{1,0:T(8,128)S(1)} %copy-done.1, bf16[512,256]{1,0:T(8,128)(2,1)S(1)} %get-tuple-element.33.rh, bf16[512,256]{1,0:T(8,128)(2,1)S(1)} %get-tuple-element.34.rl, bf16[256,512]{1,0:T(8,128)(2,1)S(1)} %get-tuple-element.35.th, ...), custom_call_target="tpu_custom_call" | custom-call | flops 4000000000 | bytes 4194304 | tf_op jit(solution)/shard_map/pallas_call | solution.py:213
  69.5 4.0 %collective-permute-done.7 = f32[8,64,256]{2,1,0:T(8,128)S(1)} collective-permute-done((f32[8,64,256]{2,1,0:T(8,128)S(1)}, f32[8,64,256]{2,1,0:T(8,128)S(1)}, u32[]{:S(2)}, u32[]{:S(2)}) %collective-permute-start.7) | collective-permute-done | bytes 524320 | tf_op jit(solution)/shard_map/ppermute | solution.py:56
  73.6 2.0 %collective-permute-done.8 = f32[8,64,256]{2,1,0:T(8,128)S(1)} collective-permute-done((f32[8,64,256]{2,1,0:T(8,128)S(1)}, f32[8,64,256]{2,1,0:T(8,128)S(1)}, u32[]{:S(2)}, u32[]{:S(2)}) %collective-permute-start.8) | collective-permute-done | bytes 524320 | tf_op jit(solution)/shard_map/ppermute | solution.py:56
  75.6 0.9 add.11
  76.5 8.7 %all-to-all-start.1 = ((f32[64,8,256]{2,1,0:T(8,128)}), f32[64,8,256]{2,1,0:T(8,128)S(1)}, u32[]{:S(2)}, u32[]{:S(2)}) async-start(f32[64,8,256]{2,1,0:T(8,128)} %bitcast.9), calls=%async_computation.1 | async-start | bytes 1048576 | tf_op jit(solution)/shard_map/all_to_all | solution.py:257
  85.3 2.0 %collective-permute-start.6 = (f32[256,256]{1,0:T(8,128)S(1)}, f32[256,256]{1,0:T(8,128)S(1)}, u32[]{:S(2)}, u32[]{:S(2)}) collective-permute-start(f32[256,256]{1,0:T(8,128)S(1)} %slice.7), channel_id=1, source_target_pairs={{16,0},{17,1},{18,2},{19,3},{20,4},{21,5},{22,6},{23,7},{24,8},{25... | collective-permute-start | bytes 786440 | tf_op jit(solution)/shard_map/ppermute | solution.py:56
  87.3 17.4 %all-to-all-done.1 = f32[64,8,256]{2,1,0:T(8,128)S(1)} async-done(((f32[64,8,256]{2,1,0:T(8,128)}), f32[64,8,256]{2,1,0:T(8,128)S(1)}, u32[]{:S(2)}, u32[]{:S(2)}) %all-to-all-start.1) | async-done | bytes 524320 | tf_op jit(solution)/shard_map/all_to_all | solution.py:257
  104.8 13.3 %all_to_all.15 = f32[16,8,256]{2,1,0:T(8,128)S(1)} all-to-all(f32[16,8,256]{2,1,0:T(8,128)S(1)} %broadcast_in_dim.5), channel_id=1, replica_groups=mesh['xlo'=2,'y'=8,'core'=2,'z'=8,'xhi'=2] {'xlo','y'}, dimensions={0} | all-to-all | bytes 262144 | tf_op jit(solution)/shard_map/all_to_all | solution.py:260
  118.1 1.9 %collective-permute-start.10 = (f32[128,256]{1,0:T(8,128)S(1)}, f32[128,256]{1,0:T(8,128)S(1)}, u32[]{:S(2)}, u32[]{:S(2)}) collective-permute-start(f32[128,256]{1,0:T(8,128)S(1)} %bitcast.12), channel_id=1, source_target_pairs={{273,0},{272,1},{275,2},{274,3},{277,4},{276,5},{279,6},{278,7},{2... | collective-permute-start | bytes 393224 | tf_op jit(solution)/shard_map/ppermute | solution.py:56
  120.0 3.0 %collective-permute-start.9 = (f32[128,256]{1,0:T(8,128)S(1)}, f32[128,256]{1,0:T(8,128)S(1)}, u32[]{:S(2)}, u32[]{:S(2)}) collective-permute-start(f32[128,256]{1,0:T(8,128)S(1)} %bitcast.13), channel_id=1, source_target_pairs={{257,0},{256,1},{259,2},{258,3},{261,4},{260,5},{263,6},{262,7},{2... | collective-permute-start | bytes 393224 | tf_op jit(solution)/shard_map/ppermute | solution.py:56
  123.0 0.7 add_multiply_fusion
  123.7 1.8 %collective-permute-done.10 = f32[128,256]{1,0:T(8,128)S(1)} collective-permute-done((f32[128,256]{1,0:T(8,128)S(1)}, f32[128,256]{1,0:T(8,128)S(1)}, u32[]{:S(2)}, u32[]{:S(2)}) %collective-permute-start.10) | collective-permute-done | bytes 131104 | tf_op jit(solution)/shard_map/ppermute | solution.py:56
  125.5 3.7 %collective-permute-done.9 = f32[128,256]{1,0:T(8,128)S(1)} collective-permute-done((f32[128,256]{1,0:T(8,128)S(1)}, f32[128,256]{1,0:T(8,128)S(1)}, u32[]{:S(2)}, u32[]{:S(2)}) %collective-permute-start.9) | collective-permute-done | bytes 131104 | tf_op jit(solution)/shard_map/ppermute | solution.py:56
  129.2 0.7 maximum_select_fusion
  (24 shorter events, 1.9 us)
Async XLA Ops:
  0.6 19.4 %collective-permute-start.1 = (s32[256,4096]{1,0:T(8,128)}, s32[256,4096]{1,0:T(8,128)}, u32[]{:S(2)}, u32[]{:S(2)}) collective-permute-start(s32[256,4096]{1,0:T(8,128)} %c_own.1), channel_id=1, source_target_pairs={{16,0},{17,1},{18,2},{19,3},{20,4},{21,5},{22,6},{23,7},{24,8},{25... | collective-permute-start | bytes 12582920 | tf_op jit(solution)/shard_map/ppermute | solution.py:56
  4.5 29.9 %all-to-all-start = ((f32[8,72,256]{2,1,0:T(8,128)}), f32[8,72,256]{2,1,0:T(8,128)S(1)}, u32[]{:S(2)}, u32[]{:S(2)}) async-start(f32[8,72,256]{2,1,0:T(8,128)} %shard_map.77), calls=%async_computation | async-start | bytes 1179648 | tf_op jit(solution)/shard_map/all_to_all | solution.py:237
  17.2 12.4 %collective-permute-start = (f32[256,384]{1,0:T(8,128)S(1)}, f32[256,384]{1,0:T(8,128)S(1)}, u32[]{:S(2)}, u32[]{:S(2)}) collective-permute-start(f32[256,384]{1,0:T(8,128)S(1)} %pad_maximum_fusion.rb_own), channel_id=1, source_target_pairs={{16,0},{17,1},{18,2},{19,3},{20,4},{21,5},{22,6},{23,7},{24,8},{25... | collective-permute-start | bytes 1179656 | tf_op jit(solution)/shard_map/ppermute | solution.py:56
  20.0 20.4 %copy-start = (s32[12]{0:T(128)S(1)}, s32[12]{0:T(128)}, u32[]{:S(2)}) copy-start(s32[12]{0:T(128)} %stack.36.table) | copy-start | bytes 148
  34.4 16.9 %collective-permute-start.2 = (f32[8,72,256]{2,1,0:T(8,128)S(1)}, f32[8,72,256]{2,1,0:T(8,128)S(1)}, u32[]{:S(2)}, u32[]{:S(2)}) collective-permute-start(f32[8,72,256]{2,1,0:T(8,128)S(1)} %all-to-all-done.pack), channel_id=1, source_target_pairs={{256,0},{257,1},{258,2},{259,3},{260,4},{261,5},{262,6},{263,7},{2... | collective-permute-start | bytes 1769480 | tf_op jit(solution)/shard_map/ppermute | solution.py:56
  37.1 24.3 %collective-permute-start.4 = (f32[8,72,256]{2,1,0:T(8,128)S(1)}, f32[8,72,256]{2,1,0:T(8,128)S(1)}, u32[]{:S(2)}, u32[]{:S(2)}) collective-permute-start(f32[8,72,256]{2,1,0:T(8,128)S(1)} %all-to-all-done.pack), channel_id=1, source_target_pairs={{257,0},{256,1},{259,2},{258,3},{261,4},{260,5},{263,6},{262,7},{2... | collective-permute-start | bytes 1769480 | tf_op jit(solution)/shard_map/ppermute | solution.py:56
  40.4 1.2 copy-start.4
  41.6 11.6 %copy-start.3 = (f32[512,512]{1,0:T(8,128)S(1)}, f32[512,512]{1,0:T(8,128)}, u32[]{:S(2)}) copy-start(f32[512,512]{1,0:T(8,128)} %get-tuple-element.40.count) | copy-start | bytes 3145732
  44.7 16.7 %collective-permute-start.5 = (f32[8,64,256]{2,1,0:T(8,128)S(1)}, f32[8,64,256]{2,1,0:T(8,128)S(1)}, u32[]{:S(2)}, u32[]{:S(2)}) collective-permute-start(f32[8,64,256]{2,1,0:T(8,128)S(1)} %get-tuple-element.44), channel_id=1, source_target_pairs={{257,0},{256,1},{259,2},{258,3},{261,4},{260,5},{263,6},{262,7},{2... | collective-permute-start | bytes 1572872 | tf_op jit(solution)/shard_map/ppermute | solution.py:56
  51.2 15.2 %collective-permute-start.3 = (f32[8,72,256]{2,1,0:T(8,128)S(1)}, f32[8,72,256]{2,1,0:T(8,128)S(1)}, u32[]{:S(2)}, u32[]{:S(2)}) collective-permute-start(f32[8,72,256]{2,1,0:T(8,128)S(1)} %collective-permute-done.2.pack), channel_id=1, source_target_pairs={{257,0},{256,1},{259,2},{258,3},{261,4},{260,5},{263,6},{262,7},{2... | collective-permute-start | bytes 1769480 | tf_op jit(solution)/shard_map/ppermute | solution.py:56
  53.2 8.2 %copy-start.2 = (f32[512,512]{1,0:T(8,128)S(1)}, f32[512,512]{1,0:T(8,128)}, u32[]{:S(2)}) copy-start(f32[512,512]{1,0:T(8,128)} %get-tuple-element.39.count) | copy-start | bytes 3145732
  56.3 17.3 %collective-permute-start.7 = (f32[8,64,256]{2,1,0:T(8,128)S(1)}, f32[8,64,256]{2,1,0:T(8,128)S(1)}, u32[]{:S(2)}, u32[]{:S(2)}) collective-permute-start(f32[8,64,256]{2,1,0:T(8,128)S(1)} %get-tuple-element.48), channel_id=1, source_target_pairs={{257,0},{256,1},{259,2},{258,3},{261,4},{260,5},{263,6},{262,7},{2... | collective-permute-start | bytes 1572872 | tf_op jit(solution)/shard_map/ppermute | solution.py:56
  61.4 5.0 %copy-start.1 = (f32[512,512]{1,0:T(8,128)S(1)}, f32[512,512]{1,0:T(8,128)}, u32[]{:S(2)}) copy-start(f32[512,512]{1,0:T(8,128)} %get-tuple-element.30.count) | copy-start | bytes 3145732
  64.5 11.1 %collective-permute-start.8 = (f32[8,64,256]{2,1,0:T(8,128)S(1)}, f32[8,64,256]{2,1,0:T(8,128)S(1)}, u32[]{:S(2)}, u32[]{:S(2)}) collective-permute-start(f32[8,64,256]{2,1,0:T(8,128)S(1)} %get-tuple-element.49), channel_id=1, source_target_pairs={{256,0},{257,1},{258,2},{259,3},{260,4},{261,5},{262,6},{263,7},{2... | collective-permute-start | bytes 1572872 | tf_op jit(solution)/shard_map/ppermute | solution.py:56
  76.5 28.2 %all-to-all-start.1 = ((f32[64,8,256]{2,1,0:T(8,128)}), f32[64,8,256]{2,1,0:T(8,128)S(1)}, u32[]{:S(2)}, u32[]{:S(2)}) async-start(f32[64,8,256]{2,1,0:T(8,128)} %bitcast.9), calls=%async_computation.1 | async-start | bytes 1048576 | tf_op jit(solution)/shard_map/all_to_all | solution.py:257
  85.3 37.7 %collective-permute-start.6 = (f32[256,256]{1,0:T(8,128)S(1)}, f32[256,256]{1,0:T(8,128)S(1)}, u32[]{:S(2)}, u32[]{:S(2)}) collective-permute-start(f32[256,256]{1,0:T(8,128)S(1)} %slice.7), channel_id=1, source_target_pairs={{16,0},{17,1},{18,2},{19,3},{20,4},{21,5},{22,6},{23,7},{24,8},{25... | collective-permute-start | bytes 786440 | tf_op jit(solution)/shard_map/ppermute | solution.py:56
  118.1 7.5 %collective-permute-start.10 = (f32[128,256]{1,0:T(8,128)S(1)}, f32[128,256]{1,0:T(8,128)S(1)}, u32[]{:S(2)}, u32[]{:S(2)}) collective-permute-start(f32[128,256]{1,0:T(8,128)S(1)} %bitcast.12), channel_id=1, source_target_pairs={{273,0},{272,1},{275,2},{274,3},{277,4},{276,5},{279,6},{278,7},{2... | collective-permute-start | bytes 393224 | tf_op jit(solution)/shard_map/ppermute | solution.py:56
  120.0 9.3 %collective-permute-start.9 = (f32[128,256]{1,0:T(8,128)S(1)}, f32[128,256]{1,0:T(8,128)S(1)}, u32[]{:S(2)}, u32[]{:S(2)}) collective-permute-start(f32[128,256]{1,0:T(8,128)S(1)} %bitcast.13), channel_id=1, source_target_pairs={{257,0},{256,1},{259,2},{258,3},{261,4},{260,5},{263,6},{262,7},{2... | collective-permute-start | bytes 393224 | tf_op jit(solution)/shard_map/ppermute | solution.py:56

commit v7 on v5

--- a/solution.py
+++ b/solution.py
@@ -243,16 +243,18 @@
     )
     prepared = (by_slice, prepare_rows(rb, rb_oth))
 
-    s_a, s_b = fetch(s_own, side_a), fetch(s_own, side_b)
+    s_a = fetch(s_own, side_a)
     r, g_own = cells(0, table, prepared, s_own)
+    s_own, g_own = lax.optimization_barrier((s_own, g_own))
+    s_b = fetch(s_own, side_b)
     sent = fetch(g_own, side_b)
     s_far = fetch(s_a, side_b)
     r, g_a = cells(1, table, prepared, s_a, r)
     from_a = fetch(g_a, side_b)
     r, g_b = cells(2, table, prepared, s_b, r, sent)
     from_b = fetch(g_b, side_a)
-    r, g = cells(3, table, prepared, s_far, r, from_a)
-    g = g + from_b
+    r, g = cells(3, table, prepared, s_far, r)
+    g = lax.optimization_barrier(g + from_a) + from_b
 
     g = lax.all_to_all(g.reshape(64, 8, DIM), ("z", "y"), 0, 0)
     row_grad = (r[:ROWS] + fetch(r[ROWS:], core_swap)) * (1.0 / 64.0)

time: 131 us -> 132 us (level)
  transfers between devices with their start and end apart: 12 -> 12, of which waited for: 6 -> 7; matrix products, arithmetic and copies ran while one was open for 2% -> 3% of each run, Pallas kernels for 18% -> 18%
where the time goes in v7:
time: 132 us; the launch traced here: 131 us
  starting transfers between devices  43.7 us (33%)
  waiting for transfers between devices  28 us (21%)
  blocking collectives  28 us (21%)
  Pallas kernels  23.9 us (18%)
  local copies, waits for them, and re-layouts  3.46 us (3%)
  other arithmetic  2.62 us (2%)
  between operations  1.51 us (1%)
    all_to_all x1, blocking collectives, body(): g = lax.all_to_all(g.reshape(64, 8, DIM), ('z', 'y'), 0, 0)  28 us
    ppermute x10, starting transfers between devices, fetch(): return lax.ppermute(value, AXES, pairs_to(move))  27.7 us
    ppermute x10, waiting for transfers between devices, fetch(): return lax.ppermute(value, AXES, pairs_to(move))  16 us
    pallas_call x4, Pallas kernels, cells(): pl.pallas_call(functools.partial(cells_kernel, which, r_in is not None, g...  12.2 us
    all_to_all x1, starting transfers between devices, body(): s_own = lax.all_to_all(pack_slice(col_embed, col_marg), 'z', 0, 0)  10.3 us
    pallas_call x1, Pallas kernels, prepare_counts(): pl.pallas_call(counts_kernel, grid_spec=pltpu.PrefetchScalarGridSpec(num_...  9.61 us
    all_to_all x1, waiting for transfers between devices, body(): lax.all_to_all(jnp.broadcast_to(g[None], (32, 8, DIM)), ('core', 'xlo', '...  7.3 us
    all_to_all x1, starting transfers between devices, body(): lax.all_to_all(jnp.broadcast_to(g[None], (32, 8, DIM)), ('core', 'xlo', '...  5.74 us
  transfers between devices with their start and end apart: 12, of which 7 were waited for; matrix products, arithmetic and copies ran while one was open for 3% of the time, Pallas kernels for 18%

profile of v7, /device:TPU:6, one launch (start us, length us, event | category | flops | bytes accessed | tf_op | source)
XLA Modules:
  0.0 131.2 jit_solution(1563968745647169362)
XLA Ops:
  0.6 1.9 %collective-permute-start.1 = (s32[256,4096]{1,0:T(8,128)}, s32[256,4096]{1,0:T(8,128)}, u32[]{:S(2)}, u32[]{:S(2)}) collective-permute-start(s32[256,4096]{1,0:T(8,128)} %c_own.1), channel_id=1, source_target_pairs={{16,0},{17,1},{18,2},{19,3},{20,4},{21,5},{22,6},{23,7},{24,8},{25... | collective-permute-start | bytes 12582920 | tf_op jit(solution)/shard_map/ppermute | solution.py:56
  2.6 1.9 %shard_map.77 = f32[8,72,256]{2,1,0:T(8,128)} custom-call(f32[256,256]{1,0:T(8,128)} %embed.1, s32[1,256]{1,0:T(1,128)} %bitcast.14), custom_call_target="tpu_custom_call" | custom-call | tf_op jit(solution)/shard_map/pallas_call | solution.py:88
  4.4 10.3 %all-to-all-start = ((f32[8,72,256]{2,1,0:T(8,128)}), f32[8,72,256]{2,1,0:T(8,128)S(1)}, u32[]{:S(2)}, u32[]{:S(2)}) async-start(f32[8,72,256]{2,1,0:T(8,128)} %shard_map.77), calls=%async_computation | async-start | bytes 1179648 | tf_op jit(solution)/shard_map/all_to_all | solution.py:237
  16.2 1.0 pad_maximum_fusion.rb_own
  17.2 2.1 %collective-permute-start = (f32[256,384]{1,0:T(8,128)S(1)}, f32[256,384]{1,0:T(8,128)S(1)}, u32[]{:S(2)}, u32[]{:S(2)}) collective-permute-start(f32[256,384]{1,0:T(8,128)S(1)} %pad_maximum_fusion.rb_own), channel_id=1, source_target_pairs={{16,0},{17,1},{18,2},{19,3},{20,4},{21,5},{22,6},{23,7},{24,8},{25... | collective-permute-start | bytes 1179656 | tf_op jit(solution)/shard_map/ppermute | solution.py:56
  19.3 0.7 stack.36.table
  20.0 9.6 %shard_map.78 = (f32[512,512]{1,0:T(8,128)}, f32[512,512]{1,0:T(8,128)}, f32[512,512]{1,0:T(8,128)}, f32[512,512]{1,0:T(8,128)}) custom-call(s32[12]{0:T(128)} %stack.36.table, s32[256,4096]{1,0:T(8,128)} %c_own.1, s32[256,4096]{1,0:T(8,128)} %collective-permute-done.1.c_oth), custom_call_target="tpu_custom_call" | custom-call | flops 4194304 | bytes 2097152 | tf_op jit(solution)/shard_map/pallas_call | solution.py:148
  29.6 4.7 %all-to-all-done.pack = f32[8,72,256]{2,1,0:T(8,128)S(1)} async-done(((f32[8,72,256]{2,1,0:T(8,128)}), f32[8,72,256]{2,1,0:T(8,128)S(1)}, u32[]{:S(2)}, u32[]{:S(2)}) %all-to-all-start) | async-done | bytes 589856 | tf_op jit(solution)/shard_map/all_to_all | solution.py:237
  34.4 2.7 %collective-permute-start.2 = (f32[8,72,256]{2,1,0:T(8,128)S(1)}, f32[8,72,256]{2,1,0:T(8,128)S(1)}, u32[]{:S(2)}, u32[]{:S(2)}) collective-permute-start(f32[8,72,256]{2,1,0:T(8,128)S(1)} %all-to-all-done.pack), channel_id=1, source_target_pairs={{256,0},{257,1},{258,2},{259,3},{260,4},{261,5},{262,6},{263,7},{2... | collective-permute-start | bytes 1769480 | tf_op jit(solution)/shard_map/ppermute | solution.py:56
  37.3 1.2 copy-done.4
  38.5 3.1 %shard_map.80 = (f32[512,256]{1,0:T(8,128)S(1)}, f32[8,64,256]{2,1,0:T(8,128)S(1)}) custom-call(s32[12]{0:T(128)S(1)} %copy-done, f32[512,512]{1,0:T(8,128)S(1)} %copy-done.4, bf16[512,256]{1,0:T(8,128)(2,1)S(1)} %get-tuple-element.35.rh, bf16[512,256]{1,0:T(8,128)(2,1)S(1)} %get-tuple-element.36.rl, bf16[256,512]{1,0:T(8,128)(2,1)S(1)} %get-tuple-element.37.th, ...), custom_call_target="tpu_custom_call" | custom-call | flops 4000000000 | bytes 4194304 | tf_op jit(solution)/shard_map/pallas_call | solution.py:213
  41.6 3.0 %collective-permute-start.4 = (f32[8,72,256]{2,1,0:T(8,128)S(1)}, f32[8,72,256]{2,1,0:T(8,128)S(1)}, u32[]{:S(2)}, u32[]{:S(2)}) collective-permute-start(f32[8,72,256]{2,1,0:T(8,128)S(1)} %all-to-all-done.pack), channel_id=1, source_target_pairs={{257,0},{256,1},{259,2},{258,3},{261,4},{260,5},{263,6},{262,7},{2... | collective-permute-start | bytes 1769480 | tf_op jit(solution)/shard_map/ppermute | solution.py:56
  44.7 4.0 %collective-permute-start.5 = (f32[8,64,256]{2,1,0:T(8,128)S(1)}, f32[8,64,256]{2,1,0:T(8,128)S(1)}, u32[]{:S(2)}, u32[]{:S(2)}) collective-permute-start(f32[8,64,256]{2,1,0:T(8,128)S(1)} %get-tuple-element.48), channel_id=1, source_target_pairs={{257,0},{256,1},{259,2},{258,3},{261,4},{260,5},{263,6},{262,7},{2... | collective-permute-start | bytes 1572872 | tf_op jit(solution)/shard_map/ppermute | solution.py:56
  48.7 3.0 %collective-permute-start.3 = (f32[8,72,256]{2,1,0:T(8,128)S(1)}, f32[8,72,256]{2,1,0:T(8,128)S(1)}, u32[]{:S(2)}, u32[]{:S(2)}) collective-permute-start(f32[8,72,256]{2,1,0:T(8,128)S(1)} %collective-permute-done.2.pack), channel_id=1, source_target_pairs={{257,0},{256,1},{259,2},{258,3},{261,4},{260,5},{263,6},{262,7},{2... | collective-permute-start | bytes 1769480 | tf_op jit(solution)/shard_map/ppermute | solution.py:56
  51.8 3.1 %shard_map.81 = (f32[512,256]{1,0:T(8,128)S(1)}, f32[8,64,256]{2,1,0:T(8,128)S(1)}) custom-call(s32[12]{0:T(128)S(1)} %copy-done, f32[512,512]{1,0:T(8,128)S(1)} %copy-done.3, bf16[512,256]{1,0:T(8,128)(2,1)S(1)} %get-tuple-element.35.rh, bf16[512,256]{1,0:T(8,128)(2,1)S(1)} %get-tuple-element.36.rl, bf16[256,512]{1,0:T(8,128)(2,1)S(1)} %get-tuple-element.37.th, ...), custom_call_target="tpu_custom_call" | custom-call | flops 4000000000 | bytes 4194304 | tf_op jit(solution)/shard_map/pallas_call | solution.py:213
  54.8 4.0 %collective-permute-start.7 = (f32[8,64,256]{2,1,0:T(8,128)S(1)}, f32[8,64,256]{2,1,0:T(8,128)S(1)}, u32[]{:S(2)}, u32[]{:S(2)}) collective-permute-start(f32[8,64,256]{2,1,0:T(8,128)S(1)} %get-tuple-element.52), channel_id=1, source_target_pairs={{257,0},{256,1},{259,2},{258,3},{261,4},{260,5},{263,6},{262,7},{2... | collective-permute-start | bytes 1572872 | tf_op jit(solution)/shard_map/ppermute | solution.py:56
  58.8 1.4 %collective-permute-done.5.rest_1_ = f32[8,64,256]{2,1,0:T(8,128)S(1)} collective-permute-done((f32[8,64,256]{2,1,0:T(8,128)S(1)}, f32[8,64,256]{2,1,0:T(8,128)S(1)}, u32[]{:S(2)}, u32[]{:S(2)}) %collective-permute-start.5) | collective-permute-done | bytes 524320 | tf_op jit(solution)/shard_map/ppermute | solution.py:56
  60.2 3.1 %shard_map.82 = (f32[512,256]{1,0:T(8,128)S(1)}, f32[8,64,256]{2,1,0:T(8,128)S(1)}) custom-call(s32[12]{0:T(128)S(1)} %copy-done, f32[512,512]{1,0:T(8,128)S(1)} %copy-done.2, bf16[512,256]{1,0:T(8,128)(2,1)S(1)} %get-tuple-element.35.rh, bf16[512,256]{1,0:T(8,128)(2,1)S(1)} %get-tuple-element.36.rl, bf16[256,512]{1,0:T(8,128)(2,1)S(1)} %get-tuple-element.37.th, ...), custom_call_target="tpu_custom_call" | custom-call | flops 4000000000 | bytes 4194304 | tf_op jit(solution)/shard_map/pallas_call | solution.py:213
  63.3 1.9 %collective-permute-start.8 = (f32[8,64,256]{2,1,0:T(8,128)S(1)}, f32[8,64,256]{2,1,0:T(8,128)S(1)}, u32[]{:S(2)}, u32[]{:S(2)}) collective-permute-start(f32[8,64,256]{2,1,0:T(8,128)S(1)} %get-tuple-element.53), channel_id=1, source_target_pairs={{256,0},{257,1},{258,2},{259,3},{260,4},{261,5},{262,6},{263,7},{2... | collective-permute-start | bytes 1572872 | tf_op jit(solution)/shard_map/ppermute | solution.py:56
  65.2 1.3 collective-permute-done.3.pack
  66.5 3.1 %shard_map.83 = (f32[512,256]{1,0:T(8,128)S(1)}, f32[8,64,256]{2,1,0:T(8,128)S(1)}) custom-call(s32[12]{0:T(128)S(1)} %copy-done, f32[512,512]{1,0:T(8,128)S(1)} %copy-done.1, bf16[512,256]{1,0:T(8,128)(2,1)S(1)} %get-tuple-element.35.rh, bf16[512,256]{1,0:T(8,128)(2,1)S(1)} %get-tuple-element.36.rl, bf16[256,512]{1,0:T(8,128)(2,1)S(1)} %get-tuple-element.37.th, ...), custom_call_target="tpu_custom_call" | custom-call | flops 4000000000 | bytes 4194304 | tf_op jit(solution)/shard_map/pallas_call | solution.py:213
  69.6 7.7 %collective-permute-done.7 = f32[8,64,256]{2,1,0:T(8,128)S(1)} collective-permute-done((f32[8,64,256]{2,1,0:T(8,128)S(1)}, f32[8,64,256]{2,1,0:T(8,128)S(1)}, u32[]{:S(2)}, u32[]{:S(2)}) %collective-permute-start.7) | collective-permute-done | bytes 524320 | tf_op jit(solution)/shard_map/ppermute | solution.py:56
  77.4 28.0 %all_to_all.15 = f32[64,8,256]{2,1,0:T(8,128)S(1)} all-to-all(f32[64,8,256]{2,1,0:T(8,128)S(1)} %bitcast.12), channel_id=1, replica_groups=mesh['xlo'=2,'y'=8,'core'=2,'z'=8,'xhi'=2] {'z','y'}, dimensions={0} | all-to-all | bytes 1048576 | tf_op jit(solution)/shard_map/all_to_all | solution.py:259
  105.5 2.8 %collective-permute-start.9 = (f32[8,256]{1,0:T(8,128)S(1)}, f32[8,256]{1,0:T(8,128)S(1)}, u32[]{:S(2)}, u32[]{:S(2)}) collective-permute-start(f32[8,256]{1,0:T(8,128)S(1)} %broadcast_multiply_fusion), channel_id=1, source_target_pairs={{1,0},{0,1},{3,2},{2,3},{5,4},{4,5},{7,6},{6,7},{9,8},{8,9},{11,10... | collective-permute-start | bytes 24584 | tf_op jit(solution)/shard_map/ppermute | solution.py:56
  108.3 4.2 %collective-permute-done.9 = f32[8,256]{1,0:T(8,128)S(1)} collective-permute-done((f32[8,256]{1,0:T(8,128)S(1)}, f32[8,256]{1,0:T(8,128)S(1)}, u32[]{:S(2)}, u32[]{:S(2)}) %collective-permute-start.9) | collective-permute-done | bytes 8224 | tf_op jit(solution)/shard_map/ppermute | solution.py:56
  112.5 0.7 broadcast_in_dim.5
  113.2 5.7 %all-to-all-start.2 = ((f32[32,8,256]{2,1,0:T(8,128)}), f32[32,8,256]{2,1,0:T(8,128)S(1)}, u32[]{:S(2)}, u32[]{:S(2)}) async-start(f32[32,8,256]{2,1,0:T(8,128)} %broadcast_in_dim.5), calls=%async_computation.2 | async-start | bytes 524288 | tf_op jit(solution)/shard_map/all_to_all | solution.py:263
  119.0 2.1 %collective-permute-start.6 = (f32[256,256]{1,0:T(8,128)S(1)}, f32[256,256]{1,0:T(8,128)S(1)}, u32[]{:S(2)}, u32[]{:S(2)}) collective-permute-start(f32[256,256]{1,0:T(8,128)S(1)} %slice.7), channel_id=1, source_target_pairs={{16,0},{17,1},{18,2},{19,3},{20,4},{21,5},{22,6},{23,7},{24,8},{25... | collective-permute-start | bytes 786440 | tf_op jit(solution)/shard_map/ppermute | solution.py:56
  121.1 1.4 %collective-permute-done.6 = f32[256,256]{1,0:T(8,128)S(1)} collective-permute-done((f32[256,256]{1,0:T(8,128)S(1)}, f32[256,256]{1,0:T(8,128)S(1)}, u32[]{:S(2)}, u32[]{:S(2)}) %collective-permute-start.6) | collective-permute-done | bytes 262176 | tf_op jit(solution)/shard_map/ppermute | solution.py:56
  122.5 0.7 add_multiply_fusion
  123.2 7.3 %all-to-all-done.2 = f32[32,8,256]{2,1,0:T(8,128)S(1)} async-done(((f32[32,8,256]{2,1,0:T(8,128)}), f32[32,8,256]{2,1,0:T(8,128)S(1)}, u32[]{:S(2)}, u32[]{:S(2)}) %all-to-all-start.2) | async-done | bytes 262176 | tf_op jit(solution)/shard_map/all_to_all | solution.py:263
  130.5 0.7 copy.10
  (22 shorter events, 1.3 us)
Async XLA Ops:
  0.6 19.4 %collective-permute-start.1 = (s32[256,4096]{1,0:T(8,128)}, s32[256,4096]{1,0:T(8,128)}, u32[]{:S(2)}, u32[]{:S(2)}) collective-permute-start(s32[256,4096]{1,0:T(8,128)} %c_own.1), channel_id=1, source_target_pairs={{16,0},{17,1},{18,2},{19,3},{20,4},{21,5},{22,6},{23,7},{24,8},{25... | collective-permute-start | bytes 12582920 | tf_op jit(solution)/shard_map/ppermute | solution.py:56
  4.4 29.9 %all-to-all-start = ((f32[8,72,256]{2,1,0:T(8,128)}), f32[8,72,256]{2,1,0:T(8,128)S(1)}, u32[]{:S(2)}, u32[]{:S(2)}) async-start(f32[8,72,256]{2,1,0:T(8,128)} %shard_map.77), calls=%async_computation | async-start | bytes 1179648 | tf_op jit(solution)/shard_map/all_to_all | solution.py:237
  17.2 12.5 %collective-permute-start = (f32[256,384]{1,0:T(8,128)S(1)}, f32[256,384]{1,0:T(8,128)S(1)}, u32[]{:S(2)}, u32[]{:S(2)}) collective-permute-start(f32[256,384]{1,0:T(8,128)S(1)} %pad_maximum_fusion.rb_own), channel_id=1, source_target_pairs={{16,0},{17,1},{18,2},{19,3},{20,4},{21,5},{22,6},{23,7},{24,8},{25... | collective-permute-start | bytes 1179656 | tf_op jit(solution)/shard_map/ppermute | solution.py:56
  20.0 17.3 %copy-start = (s32[12]{0:T(128)S(1)}, s32[12]{0:T(128)}, u32[]{:S(2)}) copy-start(s32[12]{0:T(128)} %stack.36.table) | copy-start | bytes 148
  34.4 14.3 %collective-permute-start.2 = (f32[8,72,256]{2,1,0:T(8,128)S(1)}, f32[8,72,256]{2,1,0:T(8,128)S(1)}, u32[]{:S(2)}, u32[]{:S(2)}) collective-permute-start(f32[8,72,256]{2,1,0:T(8,128)S(1)} %all-to-all-done.pack), channel_id=1, source_target_pairs={{256,0},{257,1},{258,2},{259,3},{260,4},{261,5},{262,6},{263,7},{2... | collective-permute-start | bytes 1769480 | tf_op jit(solution)/shard_map/ppermute | solution.py:56
  37.3 1.2 copy-start.4
  38.5 13.2 %copy-start.3 = (f32[512,512]{1,0:T(8,128)S(1)}, f32[512,512]{1,0:T(8,128)}, u32[]{:S(2)}) copy-start(f32[512,512]{1,0:T(8,128)} %get-tuple-element.45.count) | copy-start | bytes 3145732
  41.6 18.6 %collective-permute-start.4 = (f32[8,72,256]{2,1,0:T(8,128)S(1)}, f32[8,72,256]{2,1,0:T(8,128)S(1)}, u32[]{:S(2)}, u32[]{:S(2)}) collective-permute-start(f32[8,72,256]{2,1,0:T(8,128)S(1)} %all-to-all-done.pack), channel_id=1, source_target_pairs={{257,0},{256,1},{259,2},{258,3},{261,4},{260,5},{263,6},{262,7},{2... | collective-permute-start | bytes 1769480 | tf_op jit(solution)/shard_map/ppermute | solution.py:56
  44.7 15.5 %collective-permute-start.5 = (f32[8,64,256]{2,1,0:T(8,128)S(1)}, f32[8,64,256]{2,1,0:T(8,128)S(1)}, u32[]{:S(2)}, u32[]{:S(2)}) collective-permute-start(f32[8,64,256]{2,1,0:T(8,128)S(1)} %get-tuple-element.48), channel_id=1, source_target_pairs={{257,0},{256,1},{259,2},{258,3},{261,4},{260,5},{263,6},{262,7},{2... | collective-permute-start | bytes 1572872 | tf_op jit(solution)/shard_map/ppermute | solution.py:56
  48.7 17.8 %collective-permute-start.3 = (f32[8,72,256]{2,1,0:T(8,128)S(1)}, f32[8,72,256]{2,1,0:T(8,128)S(1)}, u32[]{:S(2)}, u32[]{:S(2)}) collective-permute-start(f32[8,72,256]{2,1,0:T(8,128)S(1)} %collective-permute-done.2.pack), channel_id=1, source_target_pairs={{257,0},{256,1},{259,2},{258,3},{261,4},{260,5},{263,6},{262,7},{2... | collective-permute-start | bytes 1769480 | tf_op jit(solution)/shard_map/ppermute | solution.py:56
  51.8 8.5 %copy-start.2 = (f32[512,512]{1,0:T(8,128)S(1)}, f32[512,512]{1,0:T(8,128)}, u32[]{:S(2)}) copy-start(f32[512,512]{1,0:T(8,128)} %get-tuple-element.41.count) | copy-start | bytes 3145732
  54.8 22.4 %collective-permute-start.7 = (f32[8,64,256]{2,1,0:T(8,128)S(1)}, f32[8,64,256]{2,1,0:T(8,128)S(1)}, u32[]{:S(2)}, u32[]{:S(2)}) collective-permute-start(f32[8,64,256]{2,1,0:T(8,128)S(1)} %get-tuple-element.52), channel_id=1, source_target_pairs={{257,0},{256,1},{259,2},{258,3},{261,4},{260,5},{263,6},{262,7},{2... | collective-permute-start | bytes 1572872 | tf_op jit(solution)/shard_map/ppermute | solution.py:56
  60.2 6.3 %copy-start.1 = (f32[512,512]{1,0:T(8,128)S(1)}, f32[512,512]{1,0:T(8,128)}, u32[]{:S(2)}) copy-start(f32[512,512]{1,0:T(8,128)} %get-tuple-element.32.count) | copy-start | bytes 3145732
  63.3 14.1 %collective-permute-start.8 = (f32[8,64,256]{2,1,0:T(8,128)S(1)}, f32[8,64,256]{2,1,0:T(8,128)S(1)}, u32[]{:S(2)}, u32[]{:S(2)}) collective-permute-start(f32[8,64,256]{2,1,0:T(8,128)S(1)} %get-tuple-element.53), channel_id=1, source_target_pairs={{256,0},{257,1},{258,2},{259,3},{260,4},{261,5},{262,6},{263,7},{2... | collective-permute-start | bytes 1572872 | tf_op jit(solution)/shard_map/ppermute | solution.py:56
  105.5 7.0 %collective-permute-start.9 = (f32[8,256]{1,0:T(8,128)S(1)}, f32[8,256]{1,0:T(8,128)S(1)}, u32[]{:S(2)}, u32[]{:S(2)}) collective-permute-start(f32[8,256]{1,0:T(8,128)S(1)} %broadcast_multiply_fusion), channel_id=1, source_target_pairs={{1,0},{0,1},{3,2},{2,3},{5,4},{4,5},{7,6},{6,7},{9,8},{8,9},{11,10... | collective-permute-start | bytes 24584 | tf_op jit(solution)/shard_map/ppermute | solution.py:56
  113.2 17.3 %all-to-all-start.2 = ((f32[32,8,256]{2,1,0:T(8,128)}), f32[32,8,256]{2,1,0:T(8,128)S(1)}, u32[]{:S(2)}, u32[]{:S(2)}) async-start(f32[32,8,256]{2,1,0:T(8,128)} %broadcast_in_dim.5), calls=%async_computation.2 | async-start | bytes 524288 | tf_op jit(solution)/shard_map/all_to_all | solution.py:263
  119.0 3.4 %collective-permute-start.6 = (f32[256,256]{1,0:T(8,128)S(1)}, f32[256,256]{1,0:T(8,128)S(1)}, u32[]{:S(2)}, u32[]{:S(2)}) collective-permute-start(f32[256,256]{1,0:T(8,128)S(1)} %slice.7), channel_id=1, source_target_pairs={{16,0},{17,1},{18,2},{19,3},{20,4},{21,5},{22,6},{23,7},{24,8},{25... | collective-permute-start | bytes 786440 | tf_op jit(solution)/shard_map/ppermute | solution.py:56

commit v8 on v5

--- a/solution.py
+++ b/solution.py
@@ -16,6 +16,7 @@
 SLICE = 64
 PACK = 72
 STRIP = 64
+PARITY = 12
 GROUP = 4
 
 
@@ -50,6 +51,10 @@
 
 def side_b(at):
     return x_pair(at) if at["core"] else x_next(at)
+
+
+def y_pair(at):
+    return {"y": at["y"] ^ 1}
 
 
 def fetch(value, move):
@@ -162,8 +167,25 @@
     )(table, *counts)
 
 
-def cells_kernel(which, adds_r, adds_g, table, count, rh, rl, th, tl, base, pack, *rest):
+def half_kernel(table, pack, out):
+    out[...] = jnp.where(table[PARITY] == 0, pack[:GROUP], pack[GROUP:])
+
+
+def half_of(table, pack):
+    vmem = pl.BlockSpec(memory_space=pltpu.VMEM)
+    return pl.pallas_call(
+        half_kernel,
+        in_specs=[pl.BlockSpec(memory_space=pltpu.SMEM), vmem],
+        out_specs=vmem,
+        out_shape=jax.ShapeDtypeStruct((GROUP, PACK, DIM), jnp.float32),
+        compiler_params=pltpu.CompilerParams(vmem_limit_bytes=8 * 2**20),
+    )(table, pack)
+
+
+def cells_kernel(which, halves, adds_r, adds_g, table, count, rh, rl, th, tl, base, *rest):
     rest = list(rest)
+    pack = rest.pop(0)
+    pack_more = rest.pop(0) if halves else None
     r_in = rest.pop(0) if adds_r else None
     g_in = rest.pop(0) if adds_g else None
     r_out, g_out = rest
@@ -174,7 +196,10 @@
     r_sum = None
     for j in range(8 // GROUP):
         part = slice(j * DIM, (j + 1) * DIM)
-        here = pack[j * GROUP : (j + 1) * GROUP]
+        if halves:
+            here = jnp.where(table[PARITY] == j, pack[...], pack_more[...])
+        else:
+            here = pack[j * GROUP : (j + 1) * GROUP]
         e = split(here[:, :SLICE, :].reshape(DIM, DIM))
         logs = [here[i, SLICE : SLICE + 8, :] for i in range(GROUP)]
         log_col = jnp.concatenate(
@@ -209,9 +234,9 @@
 def cells(which, table, prepared, pack, r_in=None, g_in=None):
     vmem = pl.BlockSpec(memory_space=pltpu.VMEM)
     counts, rows = prepared
-    args = [counts[which], *rows, pack] + [a for a in (r_in, g_in) if a is not None]
-    return pl.pallas_call(
-        functools.partial(cells_kernel, which, r_in is not None, g_in is not None),
+    args = [counts[which], *rows, *pack] + [a for a in (r_in, g_in) if a is not None]
+    return pl.pallas_call(
+        functools.partial(cells_kernel, which, len(pack) == 2, r_in is not None, g_in is not None),
         in_specs=[pl.BlockSpec(memory_space=pltpu.SMEM)] + [vmem] * len(args),
         out_specs=[vmem] * 2,
         out_shape=[
@@ -227,11 +252,12 @@
 
 def body(counts, row_marg, col_marg, log_total, row_embed, col_embed):
     core, xlo, xhi = (lax.axis_index(a) for a in ("core", "xlo", "xhi"))
+    parity = lax.axis_index("y") % 2
     table = jnp.stack(
         [core, xhi, xlo]
         + [core, jnp.where(core == 0, xhi, 1 - xhi), 1 - xlo]
         + [core, jnp.where(core == 0, 1 - xhi, xhi), 1 - xlo]
-        + [core, 1 - xhi, xlo]
+        + [core, 1 - xhi, xlo, parity]
     ).astype(jnp.int32)
 
     s_own = lax.all_to_all(pack_slice(col_embed, col_marg), "z", 0, 0)
@@ -244,14 +270,15 @@
     prepared = (by_slice, prepare_rows(rb, rb_oth))
 
     s_a, s_b = fetch(s_own, side_a), fetch(s_own, side_b)
-    r, g_own = cells(0, table, prepared, s_own)
+    r, g_own = cells(0, table, prepared, [s_own])
     sent = fetch(g_own, side_b)
-    s_far = fetch(s_a, side_b)
-    r, g_a = cells(1, table, prepared, s_a, r)
+    s_far = fetch(half_of(table, s_a), side_b)
+    s_more = fetch(s_far, y_pair)
+    r, g_a = cells(1, table, prepared, [s_a], r)
     from_a = fetch(g_a, side_b)
-    r, g_b = cells(2, table, prepared, s_b, r, sent)
+    r, g_b = cells(2, table, prepared, [s_b], r, sent)
     from_b = fetch(g_b, side_a)
-    r, g = cells(3, table, prepared, s_far, r, from_a)
+    r, g = cells(3, table, prepared, [s_far, s_more], r, from_a)
     g = g + from_b
 
     g = lax.all_to_all(g.reshape(64, 8, DIM), ("z", "y"), 0, 0)

time: 131 us -> 132 us (level)
  starting transfers between devices: 42.9 us -> 45.9 us
  blocking collectives: 27.8 us -> 26.4 us
    ppermute x10 -> x11, starting transfers between devices: 27.4 us -> 30.3 us  [fetch(): return lax.ppermute(value, AXES, pairs_to(move))]
    all_to_all x1, blocking collectives: 27.8 us -> 26.4 us  [body(): g = lax.all_to_all(g.reshape(64, 8, DIM), ('z', 'y'), 0, 0)]
    pallas_call x4 -> x5, Pallas kernels: 12.2 us -> 12.8 us  [the longest x4 12.3 us: cells(): pl.pallas_call(functools.partial(cells_kernel, which, len(pack) == 2, r_i...]
    ppermute x10 -> x11, waiting for transfers between devices: 15.6 us -> 15 us  [fetch(): return lax.ppermute(value, AXES, pairs_to(move))]
  transfers between devices with their start and end apart: 12 -> 13, of which waited for: 6 -> 7; matrix products, arithmetic and copies ran while one was open for 2% -> 2% of each run, Pallas kernels for 18% -> 19%
where the time goes in v8:
time: 132 us
  starting transfers between devices  45.9 us (35%)
  waiting for transfers between devices  27.1 us (21%)
  blocking collectives  26.4 us (20%)
  Pallas kernels  24.5 us (19%)
  local copies, waits for them, and re-layouts  3.45 us (3%)
  other arithmetic  2.55 us (2%)
  between operations  1.56 us (1%)
    ppermute x11, starting transfers between devices, fetch(): return lax.ppermute(value, AXES, pairs_to(move))  30.3 us
    all_to_all x1, blocking collectives, body(): g = lax.all_to_all(g.reshape(64, 8, DIM), ('z', 'y'), 0, 0)  26.4 us
    ppermute x11, waiting for transfers between devices, fetch(): return lax.ppermute(value, AXES, pairs_to(move))  15 us
    pallas_call x4, Pallas kernels, cells(): pl.pallas_call(functools.partial(cells_kernel, which, len(pack) == 2, r_i...  12.3 us
    all_to_all x1, starting transfers between devices, body(): s_own = lax.all_to_all(pack_slice(col_embed, col_marg), 'z', 0, 0)  10.3 us
    pallas_call x1, Pallas kernels, prepare_counts(): pl.pallas_call(counts_kernel, grid_spec=pltpu.PrefetchScalarGridSpec(num_...  9.59 us
    all_to_all x1, waiting for transfers between devices, body(): lax.all_to_all(jnp.broadcast_to(g[None], (32, 8, DIM)), ('core', 'xlo', '...  7.3 us
    all_to_all x1, starting transfers between devices, body(): lax.all_to_all(jnp.broadcast_to(g[None], (32, 8, DIM)), ('core', 'xlo', '...  5.27 us
  transfers between devices with their start and end apart: 13, of which 7 were waited for; matrix products, arithmetic and copies ran while one was open for 2% of the time, Pallas kernels for 19%

profile of v8, /device:TPU:6, one launch (start us, length us, event | category | flops | bytes accessed | tf_op | source)
XLA Modules:
  0.0 131.5 jit_solution(5466424578102593905)
XLA Ops:
  0.6 1.9 %collective-permute-start.1 = (s32[256,4096]{1,0:T(8,128)}, s32[256,4096]{1,0:T(8,128)}, u32[]{:S(2)}, u32[]{:S(2)}) collective-permute-start(s32[256,4096]{1,0:T(8,128)} %c_own.1), channel_id=1, source_target_pairs={{16,0},{17,1},{18,2},{19,3},{20,4},{21,5},{22,6},{23,7},{24,8},{25... | collective-permute-start | bytes 12582920 | tf_op jit(solution)/shard_map/ppermute | solution.py:61
  2.6 1.9 %shard_map.77 = f32[8,72,256]{2,1,0:T(8,128)} custom-call(f32[256,256]{1,0:T(8,128)} %embed.1, s32[1,256]{1,0:T(1,128)} %bitcast.15), custom_call_target="tpu_custom_call" | custom-call | tf_op jit(solution)/shard_map/pallas_call | solution.py:93
  4.5 10.3 %all-to-all-start = ((f32[8,72,256]{2,1,0:T(8,128)}), f32[8,72,256]{2,1,0:T(8,128)S(1)}, u32[]{:S(2)}, u32[]{:S(2)}) async-start(f32[8,72,256]{2,1,0:T(8,128)} %shard_map.77), calls=%async_computation | async-start | bytes 1179648 | tf_op jit(solution)/shard_map/all_to_all | solution.py:263
  16.2 1.0 pad_maximum_fusion.rb_own
  17.2 2.1 %collective-permute-start = (f32[256,384]{1,0:T(8,128)S(1)}, f32[256,384]{1,0:T(8,128)S(1)}, u32[]{:S(2)}, u32[]{:S(2)}) collective-permute-start(f32[256,384]{1,0:T(8,128)S(1)} %pad_maximum_fusion.rb_own), channel_id=1, source_target_pairs={{16,0},{17,1},{18,2},{19,3},{20,4},{21,5},{22,6},{23,7},{24,8},{25... | collective-permute-start | bytes 1179656 | tf_op jit(solution)/shard_map/ppermute | solution.py:61
  20.0 9.6 %shard_map.78 = (f32[512,512]{1,0:T(8,128)}, f32[512,512]{1,0:T(8,128)}, f32[512,512]{1,0:T(8,128)}, f32[512,512]{1,0:T(8,128)}) custom-call(s32[13]{0:T(128)} %stack.40.table, s32[256,4096]{1,0:T(8,128)} %c_own.1, s32[256,4096]{1,0:T(8,128)} %collective-permute-done.1.c_oth), custom_call_target="tpu_custom_call" | custom-call | flops 4194304 | bytes 2097152 | tf_op jit(solution)/shard_map/pallas_call | solution.py:153
  29.6 4.7 %all-to-all-done.rest_0_ = f32[8,72,256]{2,1,0:T(8,128)S(1)} async-done(((f32[8,72,256]{2,1,0:T(8,128)}), f32[8,72,256]{2,1,0:T(8,128)S(1)}, u32[]{:S(2)}, u32[]{:S(2)}) %all-to-all-start) | async-done | bytes 589856 | tf_op jit(solution)/shard_map/all_to_all | solution.py:263
  34.4 2.7 %collective-permute-start.2 = (f32[8,72,256]{2,1,0:T(8,128)S(1)}, f32[8,72,256]{2,1,0:T(8,128)S(1)}, u32[]{:S(2)}, u32[]{:S(2)}) collective-permute-start(f32[8,72,256]{2,1,0:T(8,128)S(1)} %all-to-all-done.rest_0_), channel_id=1, source_target_pairs={{256,0},{257,1},{258,2},{259,3},{260,4},{261,5},{262,6},{263,7},{2... | collective-permute-start | bytes 1769480 | tf_op jit(solution)/shard_map/ppermute | solution.py:61
  37.1 3.0 %collective-permute-start.5 = (f32[8,72,256]{2,1,0:T(8,128)S(1)}, f32[8,72,256]{2,1,0:T(8,128)S(1)}, u32[]{:S(2)}, u32[]{:S(2)}) collective-permute-start(f32[8,72,256]{2,1,0:T(8,128)S(1)} %all-to-all-done.rest_0_), channel_id=1, source_target_pairs={{257,0},{256,1},{259,2},{258,3},{261,4},{260,5},{263,6},{262,7},{2... | collective-permute-start | bytes 1769480 | tf_op jit(solution)/shard_map/ppermute | solution.py:61
  40.4 1.2 copy-done.4
  41.6 3.1 %shard_map.81 = (f32[512,256]{1,0:T(8,128)S(1)}, f32[8,64,256]{2,1,0:T(8,128)S(1)}) custom-call(s32[13]{0:T(128)S(1)} %copy-done, f32[512,512]{1,0:T(8,128)S(1)} %copy-done.4, bf16[512,256]{1,0:T(8,128)(2,1)S(1)} %get-tuple-element.33.rh, bf16[512,256]{1,0:T(8,128)(2,1)S(1)} %get-tuple-element.34.rl, bf16[256,512]{1,0:T(8,128)(2,1)S(1)} %get-tuple-element.35.th, ...), custom_call_target="tpu_custom_call" | custom-call | flops 4000000000 | bytes 4194304 | tf_op jit(solution)/shard_map/pallas_call | solution.py:238
  44.7 4.0 %collective-permute-start.6 = (f32[8,64,256]{2,1,0:T(8,128)S(1)}, f32[8,64,256]{2,1,0:T(8,128)S(1)}, u32[]{:S(2)}, u32[]{:S(2)}) collective-permute-start(f32[8,64,256]{2,1,0:T(8,128)S(1)} %get-tuple-element.44), channel_id=1, source_target_pairs={{257,0},{256,1},{259,2},{258,3},{261,4},{260,5},{263,6},{262,7},{2... | collective-permute-start | bytes 1572872 | tf_op jit(solution)/shard_map/ppermute | solution.py:61
  48.7 2.6 %collective-permute-done.2.pack.rest_0_ = f32[8,72,256]{2,1,0:T(8,128)S(1)} collective-permute-done((f32[8,72,256]{2,1,0:T(8,128)S(1)}, f32[8,72,256]{2,1,0:T(8,128)S(1)}, u32[]{:S(2)}, u32[]{:S(2)}) %collective-permute-start.2) | collective-permute-done | bytes 589856 | tf_op jit(solution)/shard_map/ppermute | solution.py:61
  51.8 1.9 %collective-permute-start.3 = (f32[4,72,256]{2,1,0:T(8,128)S(1)}, f32[4,72,256]{2,1,0:T(8,128)S(1)}, u32[]{:S(2)}, u32[]{:S(2)}) collective-permute-start(f32[4,72,256]{2,1,0:T(8,128)S(1)} %shard_map.80), channel_id=1, source_target_pairs={{257,0},{256,1},{259,2},{258,3},{261,4},{260,5},{263,6},{262,7},{2... | collective-permute-start | bytes 884744 | tf_op jit(solution)/shard_map/ppermute | solution.py:61
  53.8 3.1 %shard_map.82 = (f32[512,256]{1,0:T(8,128)S(1)}, f32[8,64,256]{2,1,0:T(8,128)S(1)}) custom-call(s32[13]{0:T(128)S(1)} %copy-done, f32[512,512]{1,0:T(8,128)S(1)} %copy-done.3, bf16[512,256]{1,0:T(8,128)(2,1)S(1)} %get-tuple-element.33.rh, bf16[512,256]{1,0:T(8,128)(2,1)S(1)} %get-tuple-element.34.rl, bf16[256,512]{1,0:T(8,128)(2,1)S(1)} %get-tuple-element.35.th, ...), custom_call_target="tpu_custom_call" | custom-call | flops 4000000000 | bytes 4194304 | tf_op jit(solution)/shard_map/pallas_call | solution.py:238
  56.8 5.1 %collective-permute-start.7 = (f32[8,64,256]{2,1,0:T(8,128)S(1)}, f32[8,64,256]{2,1,0:T(8,128)S(1)}, u32[]{:S(2)}, u32[]{:S(2)}) collective-permute-start(f32[8,64,256]{2,1,0:T(8,128)S(1)} %get-tuple-element.46), channel_id=1, source_target_pairs={{257,0},{256,1},{259,2},{258,3},{261,4},{260,5},{263,6},{262,7},{2... | collective-permute-start | bytes 1572872 | tf_op jit(solution)/shard_map/ppermute | solution.py:61
  62.0 3.5 %collective-permute-start.4 = (f32[4,72,256]{2,1,0:T(8,128)S(1)}, f32[4,72,256]{2,1,0:T(8,128)S(1)}, u32[]{:S(2)}, u32[]{:S(2)}) collective-permute-start(f32[4,72,256]{2,1,0:T(8,128)S(1)} %collective-permute-done.3.rest_0_), channel_id=1, source_target_pairs={{32,0},{33,1},{34,2},{35,3},{36,4},{37,5},{38,6},{39,7},{40,8},{41... | collective-permute-start | bytes 884744 | tf_op jit(solution)/shard_map/ppermute | solution.py:61
  65.5 3.1 %shard_map.83 = (f32[512,256]{1,0:T(8,128)S(1)}, f32[8,64,256]{2,1,0:T(8,128)S(1)}) custom-call(s32[13]{0:T(128)S(1)} %copy-done, f32[512,512]{1,0:T(8,128)S(1)} %copy-done.2, bf16[512,256]{1,0:T(8,128)(2,1)S(1)} %get-tuple-element.33.rh, bf16[512,256]{1,0:T(8,128)(2,1)S(1)} %get-tuple-element.34.rl, bf16[256,512]{1,0:T(8,128)(2,1)S(1)} %get-tuple-element.35.th, ...), custom_call_target="tpu_custom_call" | custom-call | flops 4000000000 | bytes 4194304 | tf_op jit(solution)/shard_map/pallas_call | solution.py:238
  68.6 1.9 %collective-permute-start.9 = (f32[8,64,256]{2,1,0:T(8,128)S(1)}, f32[8,64,256]{2,1,0:T(8,128)S(1)}, u32[]{:S(2)}, u32[]{:S(2)}) collective-permute-start(f32[8,64,256]{2,1,0:T(8,128)S(1)} %get-tuple-element.49), channel_id=1, source_target_pairs={{256,0},{257,1},{258,2},{259,3},{260,4},{261,5},{262,6},{263,7},{2... | collective-permute-start | bytes 1572872 | tf_op jit(solution)/shard_map/ppermute | solution.py:61
  70.5 1.6 %collective-permute-done.4.rest_1_ = f32[4,72,256]{2,1,0:T(8,128)S(1)} collective-permute-done((f32[4,72,256]{2,1,0:T(8,128)S(1)}, f32[4,72,256]{2,1,0:T(8,128)S(1)}, u32[]{:S(2)}, u32[]{:S(2)}) %collective-permute-start.4) | collective-permute-done | bytes 294944 | tf_op jit(solution)/shard_map/ppermute | solution.py:61
  72.2 3.1 %shard_map.84 = (f32[512,256]{1,0:T(8,128)S(1)}, f32[8,64,256]{2,1,0:T(8,128)S(1)}) custom-call(s32[13]{0:T(128)S(1)} %copy-done, f32[512,512]{1,0:T(8,128)S(1)} %copy-done.1, bf16[512,256]{1,0:T(8,128)(2,1)S(1)} %get-tuple-element.33.rh, bf16[512,256]{1,0:T(8,128)(2,1)S(1)} %get-tuple-element.34.rl, bf16[256,512]{1,0:T(8,128)(2,1)S(1)} %get-tuple-element.35.th, ...), custom_call_target="tpu_custom_call" | custom-call | flops 4000000000 | bytes 4194304 | tf_op jit(solution)/shard_map/pallas_call | solution.py:238
  75.2 4.5 %collective-permute-done.9 = f32[8,64,256]{2,1,0:T(8,128)S(1)} collective-permute-done((f32[8,64,256]{2,1,0:T(8,128)S(1)}, f32[8,64,256]{2,1,0:T(8,128)S(1)}, u32[]{:S(2)}, u32[]{:S(2)}) %collective-permute-start.9) | collective-permute-done | bytes 524320 | tf_op jit(solution)/shard_map/ppermute | solution.py:61
  79.8 26.4 %all_to_all.15 = f32[64,8,256]{2,1,0:T(8,128)S(1)} all-to-all(f32[64,8,256]{2,1,0:T(8,128)S(1)} %bitcast.13), channel_id=1, replica_groups=mesh['xlo'=2,'y'=8,'core'=2,'z'=8,'xhi'=2] {'z','y'}, dimensions={0} | all-to-all | bytes 1048576 | tf_op jit(solution)/shard_map/all_to_all | solution.py:284
  106.3 2.0 %collective-permute-start.10 = (f32[8,256]{1,0:T(8,128)S(1)}, f32[8,256]{1,0:T(8,128)S(1)}, u32[]{:S(2)}, u32[]{:S(2)}) collective-permute-start(f32[8,256]{1,0:T(8,128)S(1)} %broadcast_multiply_fusion), channel_id=1, source_target_pairs={{1,0},{0,1},{3,2},{2,3},{5,4},{4,5},{7,6},{6,7},{9,8},{8,9},{11,10... | collective-permute-start | bytes 24584 | tf_op jit(solution)/shard_map/ppermute | solution.py:61
  108.3 5.0 %collective-permute-done.10 = f32[8,256]{1,0:T(8,128)S(1)} collective-permute-done((f32[8,256]{1,0:T(8,128)S(1)}, f32[8,256]{1,0:T(8,128)S(1)}, u32[]{:S(2)}, u32[]{:S(2)}) %collective-permute-start.10) | collective-permute-done | bytes 8224 | tf_op jit(solution)/shard_map/ppermute | solution.py:61
  113.3 0.7 broadcast_in_dim.5
  114.1 5.3 %all-to-all-start.2 = ((f32[32,8,256]{2,1,0:T(8,128)}), f32[32,8,256]{2,1,0:T(8,128)S(1)}, u32[]{:S(2)}, u32[]{:S(2)}) async-start(f32[32,8,256]{2,1,0:T(8,128)} %broadcast_in_dim.5), calls=%async_computation.2 | async-start | bytes 524288 | tf_op jit(solution)/shard_map/all_to_all | solution.py:288
  119.4 2.1 %collective-permute-start.8 = (f32[256,256]{1,0:T(8,128)S(1)}, f32[256,256]{1,0:T(8,128)S(1)}, u32[]{:S(2)}, u32[]{:S(2)}) collective-permute-start(f32[256,256]{1,0:T(8,128)S(1)} %slice.7), channel_id=1, source_target_pairs={{16,0},{17,1},{18,2},{19,3},{20,4},{21,5},{22,6},{23,7},{24,8},{25... | collective-permute-start | bytes 786440 | tf_op jit(solution)/shard_map/ppermute | solution.py:61
  121.4 1.4 %collective-permute-done.8 = f32[256,256]{1,0:T(8,128)S(1)} collective-permute-done((f32[256,256]{1,0:T(8,128)S(1)}, f32[256,256]{1,0:T(8,128)S(1)}, u32[]{:S(2)}, u32[]{:S(2)}) %collective-permute-start.8) | collective-permute-done | bytes 262176 | tf_op jit(solution)/shard_map/ppermute | solution.py:61
  122.8 0.7 add_multiply_fusion
  123.5 7.3 %all-to-all-done.2 = f32[32,8,256]{2,1,0:T(8,128)S(1)} async-done(((f32[32,8,256]{2,1,0:T(8,128)}), f32[32,8,256]{2,1,0:T(8,128)S(1)}, u32[]{:S(2)}, u32[]{:S(2)}) %all-to-all-start.2) | async-done | bytes 262176 | tf_op jit(solution)/shard_map/all_to_all | solution.py:288
  130.8 0.7 copy.10
  (24 shorter events, 2.4 us)
Async XLA Ops:
  0.6 19.4 %collective-permute-start.1 = (s32[256,4096]{1,0:T(8,128)}, s32[256,4096]{1,0:T(8,128)}, u32[]{:S(2)}, u32[]{:S(2)}) collective-permute-start(s32[256,4096]{1,0:T(8,128)} %c_own.1), channel_id=1, source_target_pairs={{16,0},{17,1},{18,2},{19,3},{20,4},{21,5},{22,6},{23,7},{24,8},{25... | collective-permute-start | bytes 12582920 | tf_op jit(solution)/shard_map/ppermute | solution.py:61
  4.5 29.9 %all-to-all-start = ((f32[8,72,256]{2,1,0:T(8,128)}), f32[8,72,256]{2,1,0:T(8,128)S(1)}, u32[]{:S(2)}, u32[]{:S(2)}) async-start(f32[8,72,256]{2,1,0:T(8,128)} %shard_map.77), calls=%async_computation | async-start | bytes 1179648 | tf_op jit(solution)/shard_map/all_to_all | solution.py:263
  17.2 12.4 %collective-permute-start = (f32[256,384]{1,0:T(8,128)S(1)}, f32[256,384]{1,0:T(8,128)S(1)}, u32[]{:S(2)}, u32[]{:S(2)}) collective-permute-start(f32[256,384]{1,0:T(8,128)S(1)} %pad_maximum_fusion.rb_own), channel_id=1, source_target_pairs={{16,0},{17,1},{18,2},{19,3},{20,4},{21,5},{22,6},{23,7},{24,8},{25... | collective-permute-start | bytes 1179656 | tf_op jit(solution)/shard_map/ppermute | solution.py:61
  20.0 20.4 %copy-start = (s32[13]{0:T(128)S(1)}, s32[13]{0:T(128)}, u32[]{:S(2)}) copy-start(s32[13]{0:T(128)} %stack.40.table) | copy-start | bytes 160
  34.4 16.9 %collective-permute-start.2 = (f32[8,72,256]{2,1,0:T(8,128)S(1)}, f32[8,72,256]{2,1,0:T(8,128)S(1)}, u32[]{:S(2)}, u32[]{:S(2)}) collective-permute-start(f32[8,72,256]{2,1,0:T(8,128)S(1)} %all-to-all-done.rest_0_), channel_id=1, source_target_pairs={{256,0},{257,1},{258,2},{259,3},{260,4},{261,5},{262,6},{263,7},{2... | collective-permute-start | bytes 1769480 | tf_op jit(solution)/shard_map/ppermute | solution.py:61
  37.1 28.4 %collective-permute-start.5 = (f32[8,72,256]{2,1,0:T(8,128)S(1)}, f32[8,72,256]{2,1,0:T(8,128)S(1)}, u32[]{:S(2)}, u32[]{:S(2)}) collective-permute-start(f32[8,72,256]{2,1,0:T(8,128)S(1)} %all-to-all-done.rest_0_), channel_id=1, source_target_pairs={{257,0},{256,1},{259,2},{258,3},{261,4},{260,5},{263,6},{262,7},{2... | collective-permute-start | bytes 1769480 | tf_op jit(solution)/shard_map/ppermute | solution.py:61
  40.4 1.2 copy-start.4
  41.6 12.1 %copy-start.3 = (f32[512,512]{1,0:T(8,128)S(1)}, f32[512,512]{1,0:T(8,128)}, u32[]{:S(2)}) copy-start(f32[512,512]{1,0:T(8,128)} %get-tuple-element.40.count) | copy-start | bytes 3145732
  44.7 20.8 %collective-permute-start.6 = (f32[8,64,256]{2,1,0:T(8,128)S(1)}, f32[8,64,256]{2,1,0:T(8,128)S(1)}, u32[]{:S(2)}, u32[]{:S(2)}) collective-permute-start(f32[8,64,256]{2,1,0:T(8,128)S(1)} %get-tuple-element.44), channel_id=1, source_target_pairs={{257,0},{256,1},{259,2},{258,3},{261,4},{260,5},{263,6},{262,7},{2... | collective-permute-start | bytes 1572872 | tf_op jit(solution)/shard_map/ppermute | solution.py:61
  51.8 10.2 %collective-permute-start.3 = (f32[4,72,256]{2,1,0:T(8,128)S(1)}, f32[4,72,256]{2,1,0:T(8,128)S(1)}, u32[]{:S(2)}, u32[]{:S(2)}) collective-permute-start(f32[4,72,256]{2,1,0:T(8,128)S(1)} %shard_map.80), channel_id=1, source_target_pairs={{257,0},{256,1},{259,2},{258,3},{261,4},{260,5},{263,6},{262,7},{2... | collective-permute-start | bytes 884744 | tf_op jit(solution)/shard_map/ppermute | solution.py:61
  53.8 11.7 %copy-start.2 = (f32[512,512]{1,0:T(8,128)S(1)}, f32[512,512]{1,0:T(8,128)}, u32[]{:S(2)}) copy-start(f32[512,512]{1,0:T(8,128)} %get-tuple-element.39.count) | copy-start | bytes 3145732
  56.8 13.7 %collective-permute-start.7 = (f32[8,64,256]{2,1,0:T(8,128)S(1)}, f32[8,64,256]{2,1,0:T(8,128)S(1)}, u32[]{:S(2)}, u32[]{:S(2)}) collective-permute-start(f32[8,64,256]{2,1,0:T(8,128)S(1)} %get-tuple-element.46), channel_id=1, source_target_pairs={{257,0},{256,1},{259,2},{258,3},{261,4},{260,5},{263,6},{262,7},{2... | collective-permute-start | bytes 1572872 | tf_op jit(solution)/shard_map/ppermute | solution.py:61
  62.0 10.2 %collective-permute-start.4 = (f32[4,72,256]{2,1,0:T(8,128)S(1)}, f32[4,72,256]{2,1,0:T(8,128)S(1)}, u32[]{:S(2)}, u32[]{:S(2)}) collective-permute-start(f32[4,72,256]{2,1,0:T(8,128)S(1)} %collective-permute-done.3.rest_0_), channel_id=1, source_target_pairs={{32,0},{33,1},{34,2},{35,3},{36,4},{37,5},{38,6},{39,7},{40,8},{41... | collective-permute-start | bytes 884744 | tf_op jit(solution)/shard_map/ppermute | solution.py:61
  65.5 6.6 %copy-start.1 = (f32[512,512]{1,0:T(8,128)S(1)}, f32[512,512]{1,0:T(8,128)}, u32[]{:S(2)}) copy-start(f32[512,512]{1,0:T(8,128)} %get-tuple-element.30.count) | copy-start | bytes 3145732
  68.6 11.1 %collective-permute-start.9 = (f32[8,64,256]{2,1,0:T(8,128)S(1)}, f32[8,64,256]{2,1,0:T(8,128)S(1)}, u32[]{:S(2)}, u32[]{:S(2)}) collective-permute-start(f32[8,64,256]{2,1,0:T(8,128)S(1)} %get-tuple-element.49), channel_id=1, source_target_pairs={{256,0},{257,1},{258,2},{259,3},{260,4},{261,5},{262,6},{263,7},{2... | collective-permute-start | bytes 1572872 | tf_op jit(solution)/shard_map/ppermute | solution.py:61
  106.3 7.0 %collective-permute-start.10 = (f32[8,256]{1,0:T(8,128)S(1)}, f32[8,256]{1,0:T(8,128)S(1)}, u32[]{:S(2)}, u32[]{:S(2)}) collective-permute-start(f32[8,256]{1,0:T(8,128)S(1)} %broadcast_multiply_fusion), channel_id=1, source_target_pairs={{1,0},{0,1},{3,2},{2,3},{5,4},{4,5},{7,6},{6,7},{9,8},{8,9},{11,10... | collective-permute-start | bytes 24584 | tf_op jit(solution)/shard_map/ppermute | solution.py:61
  114.1 16.8 %all-to-all-start.2 = ((f32[32,8,256]{2,1,0:T(8,128)}), f32[32,8,256]{2,1,0:T(8,128)S(1)}, u32[]{:S(2)}, u32[]{:S(2)}) async-start(f32[32,8,256]{2,1,0:T(8,128)} %broadcast_in_dim.5), calls=%async_computation.2 | async-start | bytes 524288 | tf_op jit(solution)/shard_map/all_to_all | solution.py:288
  119.4 3.4 %collective-permute-start.8 = (f32[256,256]{1,0:T(8,128)S(1)}, f32[256,256]{1,0:T(8,128)S(1)}, u32[]{:S(2)}, u32[]{:S(2)}) collective-permute-start(f32[256,256]{1,0:T(8,128)S(1)} %slice.7), channel_id=1, source_target_pairs={{16,0},{17,1},{18,2},{19,3},{20,4},{21,5},{22,6},{23,7},{24,8},{25... | collective-permute-start | bytes 786440 | tf_op jit(solution)/shard_map/ppermute | solution.py:61

commit v9 on v7

--- a/solution.py
+++ b/solution.py
@@ -243,10 +243,8 @@
     )
     prepared = (by_slice, prepare_rows(rb, rb_oth))
 
-    s_a = fetch(s_own, side_a)
+    s_a, s_b = fetch(s_own, side_a), fetch(s_own, side_b)
     r, g_own = cells(0, table, prepared, s_own)
-    s_own, g_own = lax.optimization_barrier((s_own, g_own))
-    s_b = fetch(s_own, side_b)
     sent = fetch(g_own, side_b)
     s_far = fetch(s_a, side_b)
     r, g_a = cells(1, table, prepared, s_a, r)

time: 132 us -> 131 us (level)
  waiting for transfers between devices: 28 us -> 25.8 us
    ppermute x10, waiting for transfers between devices: 16 us -> 13.8 us  [fetch(): return lax.ppermute(value, AXES, pairs_to(move))]
where the time goes in v9:
time: 131 us; the launch traced here: 130 us
  starting transfers between devices  44.6 us (34%)
  blocking collectives  27.8 us (21%)
  waiting for transfers between devices  25.8 us (20%)
  Pallas kernels  23.9 us (18%)
  local copies, waits for them, and re-layouts  3.46 us (3%)
  other arithmetic  2.63 us (2%)
  between operations  1.54 us (1%)
    ppermute x10, starting transfers between devices, fetch(): return lax.ppermute(value, AXES, pairs_to(move))  28.1 us
    all_to_all x1, blocking collectives, body(): g = lax.all_to_all(g.reshape(64, 8, DIM), ('z', 'y'), 0, 0)  27.8 us
    ppermute x10, waiting for transfers between devices, fetch(): return lax.ppermute(value, AXES, pairs_to(move))  13.8 us
    pallas_call x4, Pallas kernels, cells(): pl.pallas_call(functools.partial(cells_kernel, which, r_in is not None, g...  12.2 us
    all_to_all x1, starting transfers between devices, body(): s_own = lax.all_to_all(pack_slice(col_embed, col_marg), 'z', 0, 0)  10.3 us
    pallas_call x1, Pallas kernels, prepare_counts(): pl.pallas_call(counts_kernel, grid_spec=pltpu.PrefetchScalarGridSpec(num_...  9.61 us
    all_to_all x1, waiting for transfers between devices, body(): lax.all_to_all(jnp.broadcast_to(g[None], (32, 8, DIM)), ('core', 'xlo', '...  7.3 us
    all_to_all x1, starting transfers between devices, body(): lax.all_to_all(jnp.broadcast_to(g[None], (32, 8, DIM)), ('core', 'xlo', '...  6.24 us
  transfers between devices with their start and end apart: 12, of which 7 were waited for; matrix products, arithmetic and copies ran while one was open for 3% of the time, Pallas kernels for 18%

profile of v9, /device:TPU:6, one launch (start us, length us, event | category | flops | bytes accessed | tf_op | source)
XLA Modules:
  0.0 129.8 jit_solution(12762498158991536268)
XLA Ops:
  0.6 1.9 %collective-permute-start.1 = (s32[256,4096]{1,0:T(8,128)}, s32[256,4096]{1,0:T(8,128)}, u32[]{:S(2)}, u32[]{:S(2)}) collective-permute-start(s32[256,4096]{1,0:T(8,128)} %c_own.1), channel_id=1, source_target_pairs={{16,0},{17,1},{18,2},{19,3},{20,4},{21,5},{22,6},{23,7},{24,8},{25... | collective-permute-start | bytes 12582920 | tf_op jit(solution)/shard_map/ppermute | solution.py:56
  2.6 1.9 %shard_map.77 = f32[8,72,256]{2,1,0:T(8,128)} custom-call(f32[256,256]{1,0:T(8,128)} %embed.1, s32[1,256]{1,0:T(1,128)} %bitcast.14), custom_call_target="tpu_custom_call" | custom-call | tf_op jit(solution)/shard_map/pallas_call | solution.py:88
  4.4 10.3 %all-to-all-start = ((f32[8,72,256]{2,1,0:T(8,128)}), f32[8,72,256]{2,1,0:T(8,128)S(1)}, u32[]{:S(2)}, u32[]{:S(2)}) async-start(f32[8,72,256]{2,1,0:T(8,128)} %shard_map.77), calls=%async_computation | async-start | bytes 1179648 | tf_op jit(solution)/shard_map/all_to_all | solution.py:237
  16.2 1.0 pad_maximum_fusion.rb_own
  17.2 2.1 %collective-permute-start = (f32[256,384]{1,0:T(8,128)S(1)}, f32[256,384]{1,0:T(8,128)S(1)}, u32[]{:S(2)}, u32[]{:S(2)}) collective-permute-start(f32[256,384]{1,0:T(8,128)S(1)} %pad_maximum_fusion.rb_own), channel_id=1, source_target_pairs={{16,0},{17,1},{18,2},{19,3},{20,4},{21,5},{22,6},{23,7},{24,8},{25... | collective-permute-start | bytes 1179656 | tf_op jit(solution)/shard_map/ppermute | solution.py:56
  19.3 0.7 stack.36.table
  20.0 9.6 %shard_map.78 = (f32[512,512]{1,0:T(8,128)}, f32[512,512]{1,0:T(8,128)}, f32[512,512]{1,0:T(8,128)}, f32[512,512]{1,0:T(8,128)}) custom-call(s32[12]{0:T(128)} %stack.36.table, s32[256,4096]{1,0:T(8,128)} %c_own.1, s32[256,4096]{1,0:T(8,128)} %collective-permute-done.1.c_oth), custom_call_target="tpu_custom_call" | custom-call | flops 4194304 | bytes 2097152 | tf_op jit(solution)/shard_map/pallas_call | solution.py:148
  29.6 4.7 %all-to-all-done.pack = f32[8,72,256]{2,1,0:T(8,128)S(1)} async-done(((f32[8,72,256]{2,1,0:T(8,128)}), f32[8,72,256]{2,1,0:T(8,128)S(1)}, u32[]{:S(2)}, u32[]{:S(2)}) %all-to-all-start) | async-done | bytes 589856 | tf_op jit(solution)/shard_map/all_to_all | solution.py:237
  34.4 2.7 %collective-permute-start.2 = (f32[8,72,256]{2,1,0:T(8,128)S(1)}, f32[8,72,256]{2,1,0:T(8,128)S(1)}, u32[]{:S(2)}, u32[]{:S(2)}) collective-permute-start(f32[8,72,256]{2,1,0:T(8,128)S(1)} %all-to-all-done.pack), channel_id=1, source_target_pairs={{256,0},{257,1},{258,2},{259,3},{260,4},{261,5},{262,6},{263,7},{2... | collective-permute-start | bytes 1769480 | tf_op jit(solution)/shard_map/ppermute | solution.py:56
  37.1 3.0 %collective-permute-start.4 = (f32[8,72,256]{2,1,0:T(8,128)S(1)}, f32[8,72,256]{2,1,0:T(8,128)S(1)}, u32[]{:S(2)}, u32[]{:S(2)}) collective-permute-start(f32[8,72,256]{2,1,0:T(8,128)S(1)} %all-to-all-done.pack), channel_id=1, source_target_pairs={{257,0},{256,1},{259,2},{258,3},{261,4},{260,5},{263,6},{262,7},{2... | collective-permute-start | bytes 1769480 | tf_op jit(solution)/shard_map/ppermute | solution.py:56
  40.4 1.2 copy-done.4
  41.6 3.1 %shard_map.80 = (f32[512,256]{1,0:T(8,128)S(1)}, f32[8,64,256]{2,1,0:T(8,128)S(1)}) custom-call(s32[12]{0:T(128)S(1)} %copy-done, f32[512,512]{1,0:T(8,128)S(1)} %copy-done.4, bf16[512,256]{1,0:T(8,128)(2,1)S(1)} %get-tuple-element.33.rh, bf16[512,256]{1,0:T(8,128)(2,1)S(1)} %get-tuple-element.34.rl, bf16[256,512]{1,0:T(8,128)(2,1)S(1)} %get-tuple-element.35.th, ...), custom_call_target="tpu_custom_call" | custom-call | flops 4000000000 | bytes 4194304 | tf_op jit(solution)/shard_map/pallas_call | solution.py:213
  44.7 4.0 %collective-permute-start.5 = (f32[8,64,256]{2,1,0:T(8,128)S(1)}, f32[8,64,256]{2,1,0:T(8,128)S(1)}, u32[]{:S(2)}, u32[]{:S(2)}) collective-permute-start(f32[8,64,256]{2,1,0:T(8,128)S(1)} %get-tuple-element.44), channel_id=1, source_target_pairs={{257,0},{256,1},{259,2},{258,3},{261,4},{260,5},{263,6},{262,7},{2... | collective-permute-start | bytes 1572872 | tf_op jit(solution)/shard_map/ppermute | solution.py:56
  48.7 2.6 %collective-permute-done.2.pack = f32[8,72,256]{2,1,0:T(8,128)S(1)} collective-permute-done((f32[8,72,256]{2,1,0:T(8,128)S(1)}, f32[8,72,256]{2,1,0:T(8,128)S(1)}, u32[]{:S(2)}, u32[]{:S(2)}) %collective-permute-start.2) | collective-permute-done | bytes 589856 | tf_op jit(solution)/shard_map/ppermute | solution.py:56
  51.2 1.9 %collective-permute-start.3 = (f32[8,72,256]{2,1,0:T(8,128)S(1)}, f32[8,72,256]{2,1,0:T(8,128)S(1)}, u32[]{:S(2)}, u32[]{:S(2)}) collective-permute-start(f32[8,72,256]{2,1,0:T(8,128)S(1)} %collective-permute-done.2.pack), channel_id=1, source_target_pairs={{257,0},{256,1},{259,2},{258,3},{261,4},{260,5},{263,6},{262,7},{2... | collective-permute-start | bytes 1769480 | tf_op jit(solution)/shard_map/ppermute | solution.py:56
  53.2 3.1 %shard_map.81 = (f32[512,256]{1,0:T(8,128)S(1)}, f32[8,64,256]{2,1,0:T(8,128)S(1)}) custom-call(s32[12]{0:T(128)S(1)} %copy-done, f32[512,512]{1,0:T(8,128)S(1)} %copy-done.3, bf16[512,256]{1,0:T(8,128)(2,1)S(1)} %get-tuple-element.33.rh, bf16[512,256]{1,0:T(8,128)(2,1)S(1)} %get-tuple-element.34.rl, bf16[256,512]{1,0:T(8,128)(2,1)S(1)} %get-tuple-element.35.th, ...), custom_call_target="tpu_custom_call" | custom-call | flops 4000000000 | bytes 4194304 | tf_op jit(solution)/shard_map/pallas_call | solution.py:213
  56.2 5.1 %collective-permute-start.7 = (f32[8,64,256]{2,1,0:T(8,128)S(1)}, f32[8,64,256]{2,1,0:T(8,128)S(1)}, u32[]{:S(2)}, u32[]{:S(2)}) collective-permute-start(f32[8,64,256]{2,1,0:T(8,128)S(1)} %get-tuple-element.48), channel_id=1, source_target_pairs={{257,0},{256,1},{259,2},{258,3},{261,4},{260,5},{263,6},{262,7},{2... | collective-permute-start | bytes 1572872 | tf_op jit(solution)/shard_map/ppermute | solution.py:56
  61.4 3.1 %shard_map.82 = (f32[512,256]{1,0:T(8,128)S(1)}, f32[8,64,256]{2,1,0:T(8,128)S(1)}) custom-call(s32[12]{0:T(128)S(1)} %copy-done, f32[512,512]{1,0:T(8,128)S(1)} %copy-done.2, bf16[512,256]{1,0:T(8,128)(2,1)S(1)} %get-tuple-element.33.rh, bf16[512,256]{1,0:T(8,128)(2,1)S(1)} %get-tuple-element.34.rl, bf16[256,512]{1,0:T(8,128)(2,1)S(1)} %get-tuple-element.35.th, ...), custom_call_target="tpu_custom_call" | custom-call | flops 4000000000 | bytes 4194304 | tf_op jit(solution)/shard_map/pallas_call | solution.py:213
  64.5 1.9 %collective-permute-start.8 = (f32[8,64,256]{2,1,0:T(8,128)S(1)}, f32[8,64,256]{2,1,0:T(8,128)S(1)}, u32[]{:S(2)}, u32[]{:S(2)}) collective-permute-start(f32[8,64,256]{2,1,0:T(8,128)S(1)} %get-tuple-element.49), channel_id=1, source_target_pairs={{256,0},{257,1},{258,2},{259,3},{260,4},{261,5},{262,6},{263,7},{2... | collective-permute-start | bytes 1572872 | tf_op jit(solution)/shard_map/ppermute | solution.py:56
  66.4 3.1 %shard_map.83 = (f32[512,256]{1,0:T(8,128)S(1)}, f32[8,64,256]{2,1,0:T(8,128)S(1)}) custom-call(s32[12]{0:T(128)S(1)} %copy-done, f32[512,512]{1,0:T(8,128)S(1)} %copy-done.1, bf16[512,256]{1,0:T(8,128)(2,1)S(1)} %get-tuple-element.33.rh, bf16[512,256]{1,0:T(8,128)(2,1)S(1)} %get-tuple-element.34.rl, bf16[256,512]{1,0:T(8,128)(2,1)S(1)} %get-tuple-element.35.th, ...), custom_call_target="tpu_custom_call" | custom-call | flops 4000000000 | bytes 4194304 | tf_op jit(solution)/shard_map/pallas_call | solution.py:213
  69.5 4.0 %collective-permute-done.7 = f32[8,64,256]{2,1,0:T(8,128)S(1)} collective-permute-done((f32[8,64,256]{2,1,0:T(8,128)S(1)}, f32[8,64,256]{2,1,0:T(8,128)S(1)}, u32[]{:S(2)}, u32[]{:S(2)}) %collective-permute-start.7) | collective-permute-done | bytes 524320 | tf_op jit(solution)/shard_map/ppermute | solution.py:56
  73.6 2.0 %collective-permute-done.8 = f32[8,64,256]{2,1,0:T(8,128)S(1)} collective-permute-done((f32[8,64,256]{2,1,0:T(8,128)S(1)}, f32[8,64,256]{2,1,0:T(8,128)S(1)}, u32[]{:S(2)}, u32[]{:S(2)}) %collective-permute-start.8) | collective-permute-done | bytes 524320 | tf_op jit(solution)/shard_map/ppermute | solution.py:56
  75.7 27.8 %all_to_all.15 = f32[64,8,256]{2,1,0:T(8,128)S(1)} all-to-all(f32[64,8,256]{2,1,0:T(8,128)S(1)} %bitcast.12), channel_id=1, replica_groups=mesh['xlo'=2,'y'=8,'core'=2,'z'=8,'xhi'=2] {'z','y'}, dimensions={0} | all-to-all | bytes 1048576 | tf_op jit(solution)/shard_map/all_to_all | solution.py:257
  103.6 3.2 %collective-permute-start.9 = (f32[8,256]{1,0:T(8,128)S(1)}, f32[8,256]{1,0:T(8,128)S(1)}, u32[]{:S(2)}, u32[]{:S(2)}) collective-permute-start(f32[8,256]{1,0:T(8,128)S(1)} %broadcast_multiply_fusion), channel_id=1, source_target_pairs={{1,0},{0,1},{3,2},{2,3},{5,4},{4,5},{7,6},{6,7},{9,8},{8,9},{11,10... | collective-permute-start | bytes 24584 | tf_op jit(solution)/shard_map/ppermute | solution.py:56
  106.8 3.8 %collective-permute-done.9 = f32[8,256]{1,0:T(8,128)S(1)} collective-permute-done((f32[8,256]{1,0:T(8,128)S(1)}, f32[8,256]{1,0:T(8,128)S(1)}, u32[]{:S(2)}, u32[]{:S(2)}) %collective-permute-start.9) | collective-permute-done | bytes 8224 | tf_op jit(solution)/shard_map/ppermute | solution.py:56
  110.6 0.7 broadcast_in_dim.5
  111.4 6.2 %all-to-all-start.2 = ((f32[32,8,256]{2,1,0:T(8,128)}), f32[32,8,256]{2,1,0:T(8,128)S(1)}, u32[]{:S(2)}, u32[]{:S(2)}) async-start(f32[32,8,256]{2,1,0:T(8,128)} %broadcast_in_dim.5), calls=%async_computation.2 | async-start | bytes 524288 | tf_op jit(solution)/shard_map/all_to_all | solution.py:261
  117.6 2.1 %collective-permute-start.6 = (f32[256,256]{1,0:T(8,128)S(1)}, f32[256,256]{1,0:T(8,128)S(1)}, u32[]{:S(2)}, u32[]{:S(2)}) collective-permute-start(f32[256,256]{1,0:T(8,128)S(1)} %slice.7), channel_id=1, source_target_pairs={{16,0},{17,1},{18,2},{19,3},{20,4},{21,5},{22,6},{23,7},{24,8},{25... | collective-permute-start | bytes 786440 | tf_op jit(solution)/shard_map/ppermute | solution.py:56
  119.7 1.4 %collective-permute-done.6 = f32[256,256]{1,0:T(8,128)S(1)} collective-permute-done((f32[256,256]{1,0:T(8,128)S(1)}, f32[256,256]{1,0:T(8,128)S(1)}, u32[]{:S(2)}, u32[]{:S(2)}) %collective-permute-start.6) | collective-permute-done | bytes 262176 | tf_op jit(solution)/shard_map/ppermute | solution.py:56
  121.1 0.7 add_multiply_fusion
  121.8 7.3 %all-to-all-done.2 = f32[32,8,256]{2,1,0:T(8,128)S(1)} async-done(((f32[32,8,256]{2,1,0:T(8,128)}), f32[32,8,256]{2,1,0:T(8,128)S(1)}, u32[]{:S(2)}, u32[]{:S(2)}) %all-to-all-start.2) | async-done | bytes 262176 | tf_op jit(solution)/shard_map/all_to_all | solution.py:261
  129.1 0.7 copy.10
  (22 shorter events, 1.3 us)
Async XLA Ops:
  0.6 19.4 %collective-permute-start.1 = (s32[256,4096]{1,0:T(8,128)}, s32[256,4096]{1,0:T(8,128)}, u32[]{:S(2)}, u32[]{:S(2)}) collective-permute-start(s32[256,4096]{1,0:T(8,128)} %c_own.1), channel_id=1, source_target_pairs={{16,0},{17,1},{18,2},{19,3},{20,4},{21,5},{22,6},{23,7},{24,8},{25... | collective-permute-start | bytes 12582920 | tf_op jit(solution)/shard_map/ppermute | solution.py:56
  4.4 29.9 %all-to-all-start = ((f32[8,72,256]{2,1,0:T(8,128)}), f32[8,72,256]{2,1,0:T(8,128)S(1)}, u32[]{:S(2)}, u32[]{:S(2)}) async-start(f32[8,72,256]{2,1,0:T(8,128)} %shard_map.77), calls=%async_computation | async-start | bytes 1179648 | tf_op jit(solution)/shard_map/all_to_all | solution.py:237
  17.2 12.5 %collective-permute-start = (f32[256,384]{1,0:T(8,128)S(1)}, f32[256,384]{1,0:T(8,128)S(1)}, u32[]{:S(2)}, u32[]{:S(2)}) collective-permute-start(f32[256,384]{1,0:T(8,128)S(1)} %pad_maximum_fusion.rb_own), channel_id=1, source_target_pairs={{16,0},{17,1},{18,2},{19,3},{20,4},{21,5},{22,6},{23,7},{24,8},{25... | collective-permute-start | bytes 1179656 | tf_op jit(solution)/shard_map/ppermute | solution.py:56
  20.0 20.4 %copy-start = (s32[12]{0:T(128)S(1)}, s32[12]{0:T(128)}, u32[]{:S(2)}) copy-start(s32[12]{0:T(128)} %stack.36.table) | copy-start | bytes 148
  34.4 16.9 %collective-permute-start.2 = (f32[8,72,256]{2,1,0:T(8,128)S(1)}, f32[8,72,256]{2,1,0:T(8,128)S(1)}, u32[]{:S(2)}, u32[]{:S(2)}) collective-permute-start(f32[8,72,256]{2,1,0:T(8,128)S(1)} %all-to-all-done.pack), channel_id=1, source_target_pairs={{256,0},{257,1},{258,2},{259,3},{260,4},{261,5},{262,6},{263,7},{2... | collective-permute-start | bytes 1769480 | tf_op jit(solution)/shard_map/ppermute | solution.py:56
  37.1 24.3 %collective-permute-start.4 = (f32[8,72,256]{2,1,0:T(8,128)S(1)}, f32[8,72,256]{2,1,0:T(8,128)S(1)}, u32[]{:S(2)}, u32[]{:S(2)}) collective-permute-start(f32[8,72,256]{2,1,0:T(8,128)S(1)} %all-to-all-done.pack), channel_id=1, source_target_pairs={{257,0},{256,1},{259,2},{258,3},{261,4},{260,5},{263,6},{262,7},{2... | collective-permute-start | bytes 1769480 | tf_op jit(solution)/shard_map/ppermute | solution.py:56
  40.4 1.2 copy-start.4
  41.6 11.6 %copy-start.3 = (f32[512,512]{1,0:T(8,128)S(1)}, f32[512,512]{1,0:T(8,128)}, u32[]{:S(2)}) copy-start(f32[512,512]{1,0:T(8,128)} %get-tuple-element.40.count) | copy-start | bytes 3145732
  44.7 16.7 %collective-permute-start.5 = (f32[8,64,256]{2,1,0:T(8,128)S(1)}, f32[8,64,256]{2,1,0:T(8,128)S(1)}, u32[]{:S(2)}, u32[]{:S(2)}) collective-permute-start(f32[8,64,256]{2,1,0:T(8,128)S(1)} %get-tuple-element.44), channel_id=1, source_target_pairs={{257,0},{256,1},{259,2},{258,3},{261,4},{260,5},{263,6},{262,7},{2... | collective-permute-start | bytes 1572872 | tf_op jit(solution)/shard_map/ppermute | solution.py:56
  51.2 15.2 %collective-permute-start.3 = (f32[8,72,256]{2,1,0:T(8,128)S(1)}, f32[8,72,256]{2,1,0:T(8,128)S(1)}, u32[]{:S(2)}, u32[]{:S(2)}) collective-permute-start(f32[8,72,256]{2,1,0:T(8,128)S(1)} %collective-permute-done.2.pack), channel_id=1, source_target_pairs={{257,0},{256,1},{259,2},{258,3},{261,4},{260,5},{263,6},{262,7},{2... | collective-permute-start | bytes 1769480 | tf_op jit(solution)/shard_map/ppermute | solution.py:56
  53.2 8.2 %copy-start.2 = (f32[512,512]{1,0:T(8,128)S(1)}, f32[512,512]{1,0:T(8,128)}, u32[]{:S(2)}) copy-start(f32[512,512]{1,0:T(8,128)} %get-tuple-element.39.count) | copy-start | bytes 3145732
  56.2 17.3 %collective-permute-start.7 = (f32[8,64,256]{2,1,0:T(8,128)S(1)}, f32[8,64,256]{2,1,0:T(8,128)S(1)}, u32[]{:S(2)}, u32[]{:S(2)}) collective-permute-start(f32[8,64,256]{2,1,0:T(8,128)S(1)} %get-tuple-element.48), channel_id=1, source_target_pairs={{257,0},{256,1},{259,2},{258,3},{261,4},{260,5},{263,6},{262,7},{2... | collective-permute-start | bytes 1572872 | tf_op jit(solution)/shard_map/ppermute | solution.py:56
  61.4 5.0 %copy-start.1 = (f32[512,512]{1,0:T(8,128)S(1)}, f32[512,512]{1,0:T(8,128)}, u32[]{:S(2)}) copy-start(f32[512,512]{1,0:T(8,128)} %get-tuple-element.30.count) | copy-start | bytes 3145732
  64.5 11.1 %collective-permute-start.8 = (f32[8,64,256]{2,1,0:T(8,128)S(1)}, f32[8,64,256]{2,1,0:T(8,128)S(1)}, u32[]{:S(2)}, u32[]{:S(2)}) collective-permute-start(f32[8,64,256]{2,1,0:T(8,128)S(1)} %get-tuple-element.49), channel_id=1, source_target_pairs={{256,0},{257,1},{258,2},{259,3},{260,4},{261,5},{262,6},{263,7},{2... | collective-permute-start | bytes 1572872 | tf_op jit(solution)/shard_map/ppermute | solution.py:56
  103.6 7.0 %collective-permute-start.9 = (f32[8,256]{1,0:T(8,128)S(1)}, f32[8,256]{1,0:T(8,128)S(1)}, u32[]{:S(2)}, u32[]{:S(2)}) collective-permute-start(f32[8,256]{1,0:T(8,128)S(1)} %broadcast_multiply_fusion), channel_id=1, source_target_pairs={{1,0},{0,1},{3,2},{2,3},{5,4},{4,5},{7,6},{6,7},{9,8},{8,9},{11,10... | collective-permute-start | bytes 24584 | tf_op jit(solution)/shard_map/ppermute | solution.py:56
  111.4 17.8 %all-to-all-start.2 = ((f32[32,8,256]{2,1,0:T(8,128)}), f32[32,8,256]{2,1,0:T(8,128)S(1)}, u32[]{:S(2)}, u32[]{:S(2)}) async-start(f32[32,8,256]{2,1,0:T(8,128)} %broadcast_in_dim.5), calls=%async_computation.2 | async-start | bytes 524288 | tf_op jit(solution)/shard_map/all_to_all | solution.py:261
  117.6 3.4 %collective-permute-start.6 = (f32[256,256]{1,0:T(8,128)S(1)}, f32[256,256]{1,0:T(8,128)S(1)}, u32[]{:S(2)}, u32[]{:S(2)}) collective-permute-start(f32[256,256]{1,0:T(8,128)S(1)} %slice.7), channel_id=1, source_target_pairs={{16,0},{17,1},{18,2},{19,3},{20,4},{21,5},{22,6},{23,7},{24,8},{25... | collective-permute-start | bytes 786440 | tf_op jit(solution)/shard_map/ppermute | solution.py:56

commit v10 on v9

--- a/solution.py
+++ b/solution.py
@@ -26,10 +26,6 @@
         at.update(move(at))
         pairs.append((int(np.ravel_multi_index([at[a] for a in AXES], SIZES)), target))
     return pairs
-
-
-def x_far(at):
-    return {"xhi": 1 - at["xhi"]}
 
 
 def core_swap(at):
@@ -257,9 +253,11 @@
     g = lax.all_to_all(g.reshape(64, 8, DIM), ("z", "y"), 0, 0)
     row_grad = (r[:ROWS] + fetch(r[ROWS:], core_swap)) * (1.0 / 64.0)
     g = jnp.sum(g, axis=0) * (1.0 / math.sqrt(131072.0))
-    g = fetch(g, x_far)
+    g = fetch(g, x_next)
     g = lax.all_to_all(jnp.broadcast_to(g[None], (32, 8, DIM)), ("core", "xlo", "y"), 0, 0)
-    return row_grad, g.reshape(256, DIM)
+    g = g.reshape(2, 2, SLICE, DIM)
+    col_grad = jnp.stack([g[:, 1], g[:, 0]], axis=1)
+    return row_grad, col_grad.reshape(256, DIM)
 
 
 def solution(mesh):

time: 131 us -> 130 us (level)
  no operation moved by 1% of the time
where the time goes in v10:
time: 130 us
  starting transfers between devices  44.7 us (34%)
  blocking collectives  28 us (22%)
  waiting for transfers between devices  25.3 us (19%)
  Pallas kernels  23.9 us (18%)
  other arithmetic  3.35 us (3%)
  local copies, waits for them, and re-layouts  2.76 us (2%)
  between operations  1.54 us (1%)
    ppermute x10, starting transfers between devices, fetch(): return lax.ppermute(value, AXES, pairs_to(move))  28.3 us
    all_to_all x1, blocking collectives, body(): g = lax.all_to_all(g.reshape(64, 8, DIM), ('z', 'y'), 0, 0)  28 us
    ppermute x10, waiting for transfers between devices, fetch(): return lax.ppermute(value, AXES, pairs_to(move))  13.2 us
    pallas_call x4, Pallas kernels, cells(): pl.pallas_call(functools.partial(cells_kernel, which, r_in is not None, g...  12.3 us
    all_to_all x1, starting transfers between devices, body(): s_own = lax.all_to_all(pack_slice(col_embed, col_marg), 'z', 0, 0)  10.3 us
    pallas_call x1, Pallas kernels, prepare_counts(): pl.pallas_call(counts_kernel, grid_spec=pltpu.PrefetchScalarGridSpec(num_...  9.59 us
    all_to_all x1, waiting for transfers between devices, body(): lax.all_to_all(jnp.broadcast_to(g[None], (32, 8, DIM)), ('core', 'xlo', '...  7.3 us
    all_to_all x1, starting transfers between devices, body(): lax.all_to_all(jnp.broadcast_to(g[None], (32, 8, DIM)), ('core', 'xlo', '...  6.09 us
  transfers between devices with their start and end apart: 12, of which 7 were waited for; matrix products, arithmetic and copies ran while one was open for 3% of the time, Pallas kernels for 18%

profile of v10, /device:TPU:6, one launch (start us, length us, event | category | flops | bytes accessed | tf_op | source)
XLA Modules:
  0.0 129.6 jit_solution(2515553153402044784)
XLA Ops:
  0.6 1.9 %collective-permute-start.1 = (s32[256,4096]{1,0:T(8,128)}, s32[256,4096]{1,0:T(8,128)}, u32[]{:S(2)}, u32[]{:S(2)}) collective-permute-start(s32[256,4096]{1,0:T(8,128)} %c_own.1), channel_id=1, source_target_pairs={{16,0},{17,1},{18,2},{19,3},{20,4},{21,5},{22,6},{23,7},{24,8},{25... | collective-permute-start | bytes 12582920 | tf_op jit(solution)/shard_map/ppermute | solution.py:52
  2.6 1.9 %shard_map.77 = f32[8,72,256]{2,1,0:T(8,128)} custom-call(f32[256,256]{1,0:T(8,128)} %embed.1, s32[1,256]{1,0:T(1,128)} %bitcast.16), custom_call_target="tpu_custom_call" | custom-call | tf_op jit(solution)/shard_map/pallas_call | solution.py:84
  4.5 10.3 %all-to-all-start = ((f32[8,72,256]{2,1,0:T(8,128)}), f32[8,72,256]{2,1,0:T(8,128)S(1)}, u32[]{:S(2)}, u32[]{:S(2)}) async-start(f32[8,72,256]{2,1,0:T(8,128)} %shard_map.77), calls=%async_computation | async-start | bytes 1179648 | tf_op jit(solution)/shard_map/all_to_all | solution.py:233
  15.4 0.7 log_subtract_fusion
  16.2 1.0 pad_maximum_fusion.rb_own
  17.2 2.1 %collective-permute-start = (f32[256,384]{1,0:T(8,128)S(1)}, f32[256,384]{1,0:T(8,128)S(1)}, u32[]{:S(2)}, u32[]{:S(2)}) collective-permute-start(f32[256,384]{1,0:T(8,128)S(1)} %pad_maximum_fusion.rb_own), channel_id=1, source_target_pairs={{16,0},{17,1},{18,2},{19,3},{20,4},{21,5},{22,6},{23,7},{24,8},{25... | collective-permute-start | bytes 1179656 | tf_op jit(solution)/shard_map/ppermute | solution.py:52
  20.0 9.6 %shard_map.78 = (f32[512,512]{1,0:T(8,128)}, f32[512,512]{1,0:T(8,128)}, f32[512,512]{1,0:T(8,128)}, f32[512,512]{1,0:T(8,128)}) custom-call(s32[12]{0:T(128)} %stack.39.table, s32[256,4096]{1,0:T(8,128)} %c_own.1, s32[256,4096]{1,0:T(8,128)} %collective-permute-done.1.c_oth), custom_call_target="tpu_custom_call" | custom-call | flops 4194304 | bytes 2097152 | tf_op jit(solution)/shard_map/pallas_call | solution.py:144
  29.6 4.8 %all-to-all-done.pack = f32[8,72,256]{2,1,0:T(8,128)S(1)} async-done(((f32[8,72,256]{2,1,0:T(8,128)}), f32[8,72,256]{2,1,0:T(8,128)S(1)}, u32[]{:S(2)}, u32[]{:S(2)}) %all-to-all-start) | async-done | bytes 589856 | tf_op jit(solution)/shard_map/all_to_all | solution.py:233
  34.4 2.7 %collective-permute-start.2 = (f32[8,72,256]{2,1,0:T(8,128)S(1)}, f32[8,72,256]{2,1,0:T(8,128)S(1)}, u32[]{:S(2)}, u32[]{:S(2)}) collective-permute-start(f32[8,72,256]{2,1,0:T(8,128)S(1)} %all-to-all-done.pack), channel_id=1, source_target_pairs={{256,0},{257,1},{258,2},{259,3},{260,4},{261,5},{262,6},{263,7},{2... | collective-permute-start | bytes 1769480 | tf_op jit(solution)/shard_map/ppermute | solution.py:52
  37.1 3.0 %collective-permute-start.4 = (f32[8,72,256]{2,1,0:T(8,128)S(1)}, f32[8,72,256]{2,1,0:T(8,128)S(1)}, u32[]{:S(2)}, u32[]{:S(2)}) collective-permute-start(f32[8,72,256]{2,1,0:T(8,128)S(1)} %all-to-all-done.pack), channel_id=1, source_target_pairs={{257,0},{256,1},{259,2},{258,3},{261,4},{260,5},{263,6},{262,7},{2... | collective-permute-start | bytes 1769480 | tf_op jit(solution)/shard_map/ppermute | solution.py:52
  40.4 1.2 copy-done.4
  41.6 3.1 %shard_map.80 = (f32[512,256]{1,0:T(8,128)S(1)}, f32[8,64,256]{2,1,0:T(8,128)S(1)}) custom-call(s32[12]{0:T(128)S(1)} %copy-done, f32[512,512]{1,0:T(8,128)S(1)} %copy-done.4, bf16[512,256]{1,0:T(8,128)(2,1)S(1)} %get-tuple-element.33.rh, bf16[512,256]{1,0:T(8,128)(2,1)S(1)} %get-tuple-element.34.rl, bf16[256,512]{1,0:T(8,128)(2,1)S(1)} %get-tuple-element.35.th, ...), custom_call_target="tpu_custom_call" | custom-call | flops 4000000000 | bytes 4194304 | tf_op jit(solution)/shard_map/pallas_call | solution.py:209
  44.7 4.0 %collective-permute-start.5 = (f32[8,64,256]{2,1,0:T(8,128)S(1)}, f32[8,64,256]{2,1,0:T(8,128)S(1)}, u32[]{:S(2)}, u32[]{:S(2)}) collective-permute-start(f32[8,64,256]{2,1,0:T(8,128)S(1)} %get-tuple-element.44), channel_id=1, source_target_pairs={{257,0},{256,1},{259,2},{258,3},{261,4},{260,5},{263,6},{262,7},{2... | collective-permute-start | bytes 1572872 | tf_op jit(solution)/shard_map/ppermute | solution.py:52
  48.7 2.6 %collective-permute-done.2.pack = f32[8,72,256]{2,1,0:T(8,128)S(1)} collective-permute-done((f32[8,72,256]{2,1,0:T(8,128)S(1)}, f32[8,72,256]{2,1,0:T(8,128)S(1)}, u32[]{:S(2)}, u32[]{:S(2)}) %collective-permute-start.2) | collective-permute-done | bytes 589856 | tf_op jit(solution)/shard_map/ppermute | solution.py:52
  51.2 1.9 %collective-permute-start.3 = (f32[8,72,256]{2,1,0:T(8,128)S(1)}, f32[8,72,256]{2,1,0:T(8,128)S(1)}, u32[]{:S(2)}, u32[]{:S(2)}) collective-permute-start(f32[8,72,256]{2,1,0:T(8,128)S(1)} %collective-permute-done.2.pack), channel_id=1, source_target_pairs={{257,0},{256,1},{259,2},{258,3},{261,4},{260,5},{263,6},{262,7},{2... | collective-permute-start | bytes 1769480 | tf_op jit(solution)/shard_map/ppermute | solution.py:52
  53.2 3.1 %shard_map.81 = (f32[512,256]{1,0:T(8,128)S(1)}, f32[8,64,256]{2,1,0:T(8,128)S(1)}) custom-call(s32[12]{0:T(128)S(1)} %copy-done, f32[512,512]{1,0:T(8,128)S(1)} %copy-done.3, bf16[512,256]{1,0:T(8,128)(2,1)S(1)} %get-tuple-element.33.rh, bf16[512,256]{1,0:T(8,128)(2,1)S(1)} %get-tuple-element.34.rl, bf16[256,512]{1,0:T(8,128)(2,1)S(1)} %get-tuple-element.35.th, ...), custom_call_target="tpu_custom_call" | custom-call | flops 4000000000 | bytes 4194304 | tf_op jit(solution)/shard_map/pallas_call | solution.py:209
  56.3 5.1 %collective-permute-start.7 = (f32[8,64,256]{2,1,0:T(8,128)S(1)}, f32[8,64,256]{2,1,0:T(8,128)S(1)}, u32[]{:S(2)}, u32[]{:S(2)}) collective-permute-start(f32[8,64,256]{2,1,0:T(8,128)S(1)} %get-tuple-element.48), channel_id=1, source_target_pairs={{257,0},{256,1},{259,2},{258,3},{261,4},{260,5},{263,6},{262,7},{2... | collective-permute-start | bytes 1572872 | tf_op jit(solution)/shard_map/ppermute | solution.py:52
  61.4 3.1 %shard_map.82 = (f32[512,256]{1,0:T(8,128)S(1)}, f32[8,64,256]{2,1,0:T(8,128)S(1)}) custom-call(s32[12]{0:T(128)S(1)} %copy-done, f32[512,512]{1,0:T(8,128)S(1)} %copy-done.2, bf16[512,256]{1,0:T(8,128)(2,1)S(1)} %get-tuple-element.33.rh, bf16[512,256]{1,0:T(8,128)(2,1)S(1)} %get-tuple-element.34.rl, bf16[256,512]{1,0:T(8,128)(2,1)S(1)} %get-tuple-element.35.th, ...), custom_call_target="tpu_custom_call" | custom-call | flops 4000000000 | bytes 4194304 | tf_op jit(solution)/shard_map/pallas_call | solution.py:209
  64.5 1.9 %collective-permute-start.8 = (f32[8,64,256]{2,1,0:T(8,128)S(1)}, f32[8,64,256]{2,1,0:T(8,128)S(1)}, u32[]{:S(2)}, u32[]{:S(2)}) collective-permute-start(f32[8,64,256]{2,1,0:T(8,128)S(1)} %get-tuple-element.49), channel_id=1, source_target_pairs={{256,0},{257,1},{258,2},{259,3},{260,4},{261,5},{262,6},{263,7},{2... | collective-permute-start | bytes 1572872 | tf_op jit(solution)/shard_map/ppermute | solution.py:52
  66.5 3.1 %shard_map.83 = (f32[512,256]{1,0:T(8,128)S(1)}, f32[8,64,256]{2,1,0:T(8,128)S(1)}) custom-call(s32[12]{0:T(128)S(1)} %copy-done, f32[512,512]{1,0:T(8,128)S(1)} %copy-done.1, bf16[512,256]{1,0:T(8,128)(2,1)S(1)} %get-tuple-element.33.rh, bf16[512,256]{1,0:T(8,128)(2,1)S(1)} %get-tuple-element.34.rl, bf16[256,512]{1,0:T(8,128)(2,1)S(1)} %get-tuple-element.35.th, ...), custom_call_target="tpu_custom_call" | custom-call | flops 4000000000 | bytes 4194304 | tf_op jit(solution)/shard_map/pallas_call | solution.py:209
  69.5 4.0 %collective-permute-done.7 = f32[8,64,256]{2,1,0:T(8,128)S(1)} collective-permute-done((f32[8,64,256]{2,1,0:T(8,128)S(1)}, f32[8,64,256]{2,1,0:T(8,128)S(1)}, u32[]{:S(2)}, u32[]{:S(2)}) %collective-permute-start.7) | collective-permute-done | bytes 524320 | tf_op jit(solution)/shard_map/ppermute | solution.py:52
  73.6 2.0 %collective-permute-done.8 = f32[8,64,256]{2,1,0:T(8,128)S(1)} collective-permute-done((f32[8,64,256]{2,1,0:T(8,128)S(1)}, f32[8,64,256]{2,1,0:T(8,128)S(1)}, u32[]{:S(2)}, u32[]{:S(2)}) %collective-permute-start.8) | collective-permute-done | bytes 524320 | tf_op jit(solution)/shard_map/ppermute | solution.py:52
  75.7 28.0 %all_to_all.15 = f32[64,8,256]{2,1,0:T(8,128)S(1)} all-to-all(f32[64,8,256]{2,1,0:T(8,128)S(1)} %bitcast.13), channel_id=1, replica_groups=mesh['xlo'=2,'y'=8,'core'=2,'z'=8,'xhi'=2] {'z','y'}, dimensions={0} | all-to-all | bytes 1048576 | tf_op jit(solution)/shard_map/all_to_all | solution.py:253
  103.7 3.5 %collective-permute-start.9 = (f32[8,256]{1,0:T(8,128)S(1)}, f32[8,256]{1,0:T(8,128)S(1)}, u32[]{:S(2)}, u32[]{:S(2)}) collective-permute-start(f32[8,256]{1,0:T(8,128)S(1)} %broadcast_multiply_fusion), channel_id=1, source_target_pairs={{257,0},{256,1},{259,2},{258,3},{261,4},{260,5},{263,6},{262,7},{2... | collective-permute-start | bytes 24584 | tf_op jit(solution)/shard_map/ppermute | solution.py:52
  107.2 3.3 %collective-permute-done.9 = f32[8,256]{1,0:T(8,128)S(1)} collective-permute-done((f32[8,256]{1,0:T(8,128)S(1)}, f32[8,256]{1,0:T(8,128)S(1)}, u32[]{:S(2)}, u32[]{:S(2)}) %collective-permute-start.9) | collective-permute-done | bytes 8224 | tf_op jit(solution)/shard_map/ppermute | solution.py:52
  110.5 0.7 broadcast_in_dim.5
  111.2 6.1 %all-to-all-start.2 = ((f32[32,8,256]{2,1,0:T(8,128)}), f32[32,8,256]{2,1,0:T(8,128)S(1)}, u32[]{:S(2)}, u32[]{:S(2)}) async-start(f32[32,8,256]{2,1,0:T(8,128)} %broadcast_in_dim.5), calls=%async_computation.2 | async-start | bytes 524288 | tf_op jit(solution)/shard_map/all_to_all | solution.py:257
  117.3 2.1 %collective-permute-start.6 = (f32[256,256]{1,0:T(8,128)S(1)}, f32[256,256]{1,0:T(8,128)S(1)}, u32[]{:S(2)}, u32[]{:S(2)}) collective-permute-start(f32[256,256]{1,0:T(8,128)S(1)} %slice.13), channel_id=1, source_target_pairs={{16,0},{17,1},{18,2},{19,3},{20,4},{21,5},{22,6},{23,7},{24,8},{25... | collective-permute-start | bytes 786440 | tf_op jit(solution)/shard_map/ppermute | solution.py:52
  119.4 1.4 %collective-permute-done.6 = f32[256,256]{1,0:T(8,128)S(1)} collective-permute-done((f32[256,256]{1,0:T(8,128)S(1)}, f32[256,256]{1,0:T(8,128)S(1)}, u32[]{:S(2)}, u32[]{:S(2)}) %collective-permute-start.6) | collective-permute-done | bytes 262176 | tf_op jit(solution)/shard_map/ppermute | solution.py:52
  120.8 0.7 add_multiply_fusion
  121.5 7.3 %all-to-all-done.2 = f32[32,8,256]{2,1,0:T(8,128)S(1)} async-done(((f32[32,8,256]{2,1,0:T(8,128)}), f32[32,8,256]{2,1,0:T(8,128)S(1)}, u32[]{:S(2)}, u32[]{:S(2)}) %all-to-all-start.2) | async-done | bytes 262176 | tf_op jit(solution)/shard_map/all_to_all | solution.py:257
  128.8 0.7 pad_maximum_fusion.1
  (23 shorter events, 1.3 us)
Async XLA Ops:
  0.6 19.4 %collective-permute-start.1 = (s32[256,4096]{1,0:T(8,128)}, s32[256,4096]{1,0:T(8,128)}, u32[]{:S(2)}, u32[]{:S(2)}) collective-permute-start(s32[256,4096]{1,0:T(8,128)} %c_own.1), channel_id=1, source_target_pairs={{16,0},{17,1},{18,2},{19,3},{20,4},{21,5},{22,6},{23,7},{24,8},{25... | collective-permute-start | bytes 12582920 | tf_op jit(solution)/shard_map/ppermute | solution.py:52
  4.5 29.9 %all-to-all-start = ((f32[8,72,256]{2,1,0:T(8,128)}), f32[8,72,256]{2,1,0:T(8,128)S(1)}, u32[]{:S(2)}, u32[]{:S(2)}) async-start(f32[8,72,256]{2,1,0:T(8,128)} %shard_map.77), calls=%async_computation | async-start | bytes 1179648 | tf_op jit(solution)/shard_map/all_to_all | solution.py:233
  17.2 12.4 %collective-permute-start = (f32[256,384]{1,0:T(8,128)S(1)}, f32[256,384]{1,0:T(8,128)S(1)}, u32[]{:S(2)}, u32[]{:S(2)}) collective-permute-start(f32[256,384]{1,0:T(8,128)S(1)} %pad_maximum_fusion.rb_own), channel_id=1, source_target_pairs={{16,0},{17,1},{18,2},{19,3},{20,4},{21,5},{22,6},{23,7},{24,8},{25... | collective-permute-start | bytes 1179656 | tf_op jit(solution)/shard_map/ppermute | solution.py:52
  20.0 20.4 %copy-start = (s32[12]{0:T(128)S(1)}, s32[12]{0:T(128)}, u32[]{:S(2)}) copy-start(s32[12]{0:T(128)} %stack.39.table) | copy-start | bytes 148
  34.4 16.9 %collective-permute-start.2 = (f32[8,72,256]{2,1,0:T(8,128)S(1)}, f32[8,72,256]{2,1,0:T(8,128)S(1)}, u32[]{:S(2)}, u32[]{:S(2)}) collective-permute-start(f32[8,72,256]{2,1,0:T(8,128)S(1)} %all-to-all-done.pack), channel_id=1, source_target_pairs={{256,0},{257,1},{258,2},{259,3},{260,4},{261,5},{262,6},{263,7},{2... | collective-permute-start | bytes 1769480 | tf_op jit(solution)/shard_map/ppermute | solution.py:52
  37.1 24.3 %collective-permute-start.4 = (f32[8,72,256]{2,1,0:T(8,128)S(1)}, f32[8,72,256]{2,1,0:T(8,128)S(1)}, u32[]{:S(2)}, u32[]{:S(2)}) collective-permute-start(f32[8,72,256]{2,1,0:T(8,128)S(1)} %all-to-all-done.pack), channel_id=1, source_target_pairs={{257,0},{256,1},{259,2},{258,3},{261,4},{260,5},{263,6},{262,7},{2... | collective-permute-start | bytes 1769480 | tf_op jit(solution)/shard_map/ppermute | solution.py:52
  40.4 1.2 copy-start.4
  41.6 11.6 %copy-start.3 = (f32[512,512]{1,0:T(8,128)S(1)}, f32[512,512]{1,0:T(8,128)}, u32[]{:S(2)}) copy-start(f32[512,512]{1,0:T(8,128)} %get-tuple-element.40.count) | copy-start | bytes 3145732
  44.7 16.7 %collective-permute-start.5 = (f32[8,64,256]{2,1,0:T(8,128)S(1)}, f32[8,64,256]{2,1,0:T(8,128)S(1)}, u32[]{:S(2)}, u32[]{:S(2)}) collective-permute-start(f32[8,64,256]{2,1,0:T(8,128)S(1)} %get-tuple-element.44), channel_id=1, source_target_pairs={{257,0},{256,1},{259,2},{258,3},{261,4},{260,5},{263,6},{262,7},{2... | collective-permute-start | bytes 1572872 | tf_op jit(solution)/shard_map/ppermute | solution.py:52
  51.2 15.2 %collective-permute-start.3 = (f32[8,72,256]{2,1,0:T(8,128)S(1)}, f32[8,72,256]{2,1,0:T(8,128)S(1)}, u32[]{:S(2)}, u32[]{:S(2)}) collective-permute-start(f32[8,72,256]{2,1,0:T(8,128)S(1)} %collective-permute-done.2.pack), channel_id=1, source_target_pairs={{257,0},{256,1},{259,2},{258,3},{261,4},{260,5},{263,6},{262,7},{2... | collective-permute-start | bytes 1769480 | tf_op jit(solution)/shard_map/ppermute | solution.py:52
  53.2 8.2 %copy-start.2 = (f32[512,512]{1,0:T(8,128)S(1)}, f32[512,512]{1,0:T(8,128)}, u32[]{:S(2)}) copy-start(f32[512,512]{1,0:T(8,128)} %get-tuple-element.39.count) | copy-start | bytes 3145732
  56.3 17.3 %collective-permute-start.7 = (f32[8,64,256]{2,1,0:T(8,128)S(1)}, f32[8,64,256]{2,1,0:T(8,128)S(1)}, u32[]{:S(2)}, u32[]{:S(2)}) collective-permute-start(f32[8,64,256]{2,1,0:T(8,128)S(1)} %get-tuple-element.48), channel_id=1, source_target_pairs={{257,0},{256,1},{259,2},{258,3},{261,4},{260,5},{263,6},{262,7},{2... | collective-permute-start | bytes 1572872 | tf_op jit(solution)/shard_map/ppermute | solution.py:52
  61.4 5.0 %copy-start.1 = (f32[512,512]{1,0:T(8,128)S(1)}, f32[512,512]{1,0:T(8,128)}, u32[]{:S(2)}) copy-start(f32[512,512]{1,0:T(8,128)} %get-tuple-element.30.count) | copy-start | bytes 3145732
  64.5 11.1 %collective-permute-start.8 = (f32[8,64,256]{2,1,0:T(8,128)S(1)}, f32[8,64,256]{2,1,0:T(8,128)S(1)}, u32[]{:S(2)}, u32[]{:S(2)}) collective-permute-start(f32[8,64,256]{2,1,0:T(8,128)S(1)} %get-tuple-element.49), channel_id=1, source_target_pairs={{256,0},{257,1},{258,2},{259,3},{260,4},{261,5},{262,6},{263,7},{2... | collective-permute-start | bytes 1572872 | tf_op jit(solution)/shard_map/ppermute | solution.py:52
  103.7 6.8 %collective-permute-start.9 = (f32[8,256]{1,0:T(8,128)S(1)}, f32[8,256]{1,0:T(8,128)S(1)}, u32[]{:S(2)}, u32[]{:S(2)}) collective-permute-start(f32[8,256]{1,0:T(8,128)S(1)} %broadcast_multiply_fusion), channel_id=1, source_target_pairs={{257,0},{256,1},{259,2},{258,3},{261,4},{260,5},{263,6},{262,7},{2... | collective-permute-start | bytes 24584 | tf_op jit(solution)/shard_map/ppermute | solution.py:52
  111.2 17.6 %all-to-all-start.2 = ((f32[32,8,256]{2,1,0:T(8,128)}), f32[32,8,256]{2,1,0:T(8,128)S(1)}, u32[]{:S(2)}, u32[]{:S(2)}) async-start(f32[32,8,256]{2,1,0:T(8,128)} %broadcast_in_dim.5), calls=%async_computation.2 | async-start | bytes 524288 | tf_op jit(solution)/shard_map/all_to_all | solution.py:257
  117.3 3.4 %collective-permute-start.6 = (f32[256,256]{1,0:T(8,128)S(1)}, f32[256,256]{1,0:T(8,128)S(1)}, u32[]{:S(2)}, u32[]{:S(2)}) collective-permute-start(f32[256,256]{1,0:T(8,128)S(1)} %slice.13), channel_id=1, source_target_pairs={{16,0},{17,1},{18,2},{19,3},{20,4},{21,5},{22,6},{23,7},{24,8},{25... | collective-permute-start | bytes 786440 | tf_op jit(solution)/shard_map/ppermute | solution.py:52
